TPU v7x, 32 devices: a whole 2x2x4 slice. The times are simulated.
32 devices in a mesh: exp: 16 (over z, y, x), hid: 2 (over core).
Axes of the slice: x: 2, y: 2, z: 4, core: 2. Of those that a mesh axis runs over, the one named last changes fastest.
Arguments:
- tokens: bfloat16 [8192, 1280], P(('exp', 'hid')), may hold values from -6 to 6
- norm_one: float32 [1280], replicated, may hold values from 0.5 to 1.5
- w_query: bfloat16 [1280, 1280], P('hid'), may hold values from -0.15625 to 0.15625
- w_key: bfloat16 [1280, 1280], P('hid'), may hold values from -0.15625 to 0.15625
- w_value: bfloat16 [1280, 1280], P('hid'), may hold values from -0.15625 to 0.15625
- w_out: bfloat16 [1280, 1280], P('hid'), may hold values from -0.625 to 0.625
- norm_two: float32 [1280], replicated, may hold values from 0.5 to 1.5
- r_gate: bfloat16 [16, 1280, 896], P('exp', None, 'hid'), may hold values from -0.15625 to 0.15625
- r_up: bfloat16 [16, 1280, 896], P('exp', None, 'hid'), may hold values from -0.15625 to 0.15625
- r_down: bfloat16 [16, 896, 1280], P('exp', 'hid'), may hold values from -0.375 to 0.375
- s_gate: bfloat16 [1280, 896], P(None, 'hid'), may hold values from -0.15625 to 0.15625
- s_up: bfloat16 [1280, 896], P(None, 'hid'), may hold values from -0.15625 to 0.15625
- s_down: bfloat16 [896, 1280], P('hid'), may hold values from -0.375 to 0.375
- logits: float32 [8192, 7], P(('exp', 'hid')), may hold values from -3 to 3
- routes: int32 [8192, 7], P(('exp', 'hid')), may hold values from 0 to 14, all different within a row; in each aligned block of 256 rows (0 to 255, 256 to 511, ...) at most 216 rows name the same one
- lengths: int32 [32], P(('exp', 'hid')), may hold values from 64 to 256, as said below
- cotangent: bfloat16 [8192, 1280], P(('exp', 'hid')), may hold values from -6 to 6
Outputs:
- mixed_out: bfloat16 [8192, 1280], P(('exp', 'hid'))
- grad_tokens: bfloat16 [8192, 1280], P(('exp', 'hid'))
- grad_norm_one: float32 [1280], replicated
- grad_query: float32 [1280, 1280], P('hid')
- grad_key: float32 [1280, 1280], P('hid')
- grad_value: float32 [1280, 1280], P('hid')
- grad_wout: float32 [1280, 1280], P('hid')
- grad_norm_two: float32 [1280], replicated
- grad_rgate: float32 [16, 1280, 896], P('exp', None, 'hid')
- grad_rup: float32 [16, 1280, 896], P('exp', None, 'hid')
- grad_rdown: float32 [16, 896, 1280], P('exp', 'hid')
- grad_sgate: float32 [1280, 896], P(None, 'hid')
- grad_sup: float32 [1280, 896], P(None, 'hid')
- grad_sdown: float32 [896, 1280], P('hid')
- grad_logits: float32 [8192, 7], P(('exp', 'hid'))
- counts: int32 [16], replicated
Inputs may be any that keep to these rules, and one draw needn't show every extreme that they name: `routes`: each row names 7 different routed experts; among the rows of one device no expert is named more than 216 times. `lengths`: some sequence is used to its full length.
All inputs are finite; a program needn't handle non-finite values.
Results may differ from a plain program's by a relative error of at most 0.02.
Values may be sent and summed in bfloat16 or wider, within the bound.
A program may use at most 384 MiB of HBM per device.

v0:
```python
import jax
import jax.numpy as jnp
from jax import lax
from jax.sharding import PartitionSpec as P

HEADS = 10
HD = 128


norm_eps = 1e-06
rotary_base = 10000.0
block_rows = 512
contract_rows = (((0,), (0,)), ((), ()))
contract_cols = (((1,), (1,)), ((), ()))


def matmul(left_side, right_side):
    return jnp.dot(left_side, right_side, preferred_element_type=jnp.float32)


def outer_rows(left_side, right_side):
    return lax.dot_general(left_side, right_side, contract_rows, preferred_element_type=jnp.float32)


def inner_cols(left_side, right_side):
    return lax.dot_general(left_side, right_side, contract_cols, preferred_element_type=jnp.float32)


def rms_parts(values):
    inv_rms = lax.rsqrt(jnp.mean(values * values, axis=-1, keepdims=True) + norm_eps)
    return (values * inv_rms, inv_rms)


def rms_back(normed, inv_rms, norm_gain, upstream):
    gain_grad = jnp.sum(upstream * normed, axis=0)
    scaled_up = upstream * norm_gain
    return (
        inv_rms * (scaled_up - normed * jnp.mean(scaled_up * normed, axis=-1, keepdims=True)),
        gain_grad,
    )


def rotary_tables(seq_len, head_size):
    position = jnp.arange(seq_len).astype(jnp.float32)
    inverse_freq = rotary_base ** (
        -2.0 * jnp.arange(head_size // 2).astype(jnp.float32) / head_size
    )
    angle_grid = position[:, None] * inverse_freq[None, :]
    return (jnp.cos(angle_grid)[:, None, :], jnp.sin(angle_grid)[:, None, :])


def rotate(values, cosine_table, sine_table):
    half_width = values.shape[-1] // 2
    first_half = values[..., :half_width]
    second_half = values[..., half_width:]
    return jnp.concatenate(
        [
            first_half * cosine_table - second_half * sine_table,
            second_half * cosine_table + first_half * sine_table,
        ],
        axis=-1,
    )


def masked_scores(query_blk, keys_all, block_start, seq_length, score_scale):
    scores = (
        jnp.einsum("qhd,khd->hqk", query_blk, keys_all, preferred_element_type=jnp.float32)
        * score_scale
    )
    row_pos = block_start + jnp.arange(query_blk.shape[0])[:, None]
    col_pos = jnp.arange(keys_all.shape[0])[None, :]
    allowed = (col_pos <= row_pos) & (col_pos < seq_length)
    return jnp.where(allowed[None], scores, -1e30)


def attend_forward(queries, keys_all, values_all, seq_length):
    total_rows = queries.shape[0]
    step_rows = min(total_rows, block_rows)
    score_scale = queries.shape[-1] ** (-0.5)

    def one_block(block_start):
        scores = masked_scores(queries, keys_all, block_start, seq_length, score_scale)
        top_val = jnp.max(scores, axis=-1, keepdims=True)
        raised = jnp.exp(scores - top_val)
        totals = jnp.sum(raised, axis=-1, keepdims=True)
        attn_prob = (raised / totals).astype(jnp.bfloat16)
        attended = jnp.einsum(
            "hqk,khd->qhd", attn_prob, values_all, preferred_element_type=jnp.float32
        )
        return (attended, (top_val + jnp.log(totals))[..., 0])

    starts = jnp.arange(total_rows // step_rows) * step_rows
    attended, log_total = lax.map(one_block, starts)
    return (attended.reshape(queries.shape), log_total)


def attend_backward(queries, keys_all, values_all, seq_length, log_total, grad_out):
    total_rows = queries.shape[0]
    step_rows = min(total_rows, block_rows)
    score_scale = queries.shape[-1] ** (-0.5)

    def one_block(running, inputs):
        grad_keys, grad_values = running
        block_start, lse_block = inputs
        scores = masked_scores(queries, keys_all, block_start, seq_length, score_scale)
        attn_prob = jnp.exp(scores - lse_block[..., None])
        grad_values = grad_values + jnp.einsum(
            "hqk,qhd->khd",
            attn_prob.astype(jnp.bfloat16),
            grad_out,
            preferred_element_type=jnp.float32,
        )
        grad_prob = jnp.einsum(
            "qhd,khd->hqk", grad_out, values_all, preferred_element_type=jnp.float32
        )
        row_inner = jnp.sum(attn_prob * grad_prob, axis=-1, keepdims=True)
        grad_scores = (attn_prob * (grad_prob - row_inner)).astype(jnp.bfloat16)
        grad_query = (
            jnp.einsum("hqk,khd->qhd", grad_scores, keys_all, preferred_element_type=jnp.float32)
            * score_scale
        )
        grad_keys = (
            grad_keys
            + jnp.einsum("hqk,qhd->khd", grad_scores, queries, preferred_element_type=jnp.float32)
            * score_scale
        )
        return ((grad_keys, grad_values), grad_query)

    zero_grads = jnp.zeros(queries.shape, jnp.float32)
    starts = jnp.arange(total_rows // step_rows) * step_rows
    (grad_keys, grad_values), grad_query = lax.scan(
        one_block, (zero_grads, zero_grads), (starts, log_total)
    )
    return (grad_query.reshape(queries.shape), grad_keys, grad_values)


def swiglu_forward(expert_in, weights):
    gate_val = matmul(expert_in, weights[0])
    up_val = matmul(expert_in, weights[1])
    active = (jax.nn.silu(gate_val) * up_val).astype(jnp.bfloat16)
    return (matmul(active, weights[2]), (gate_val, up_val, active))


def swiglu_backward(expert_in, kept, upstream, weights):
    gate_val, up_val, active = kept
    grad_active = inner_cols(upstream, weights[2])
    sigmoid_val = jax.nn.sigmoid(gate_val)
    grad_gate = (
        grad_active * up_val * sigmoid_val * (1.0 + gate_val * (1.0 - sigmoid_val))
    ).astype(jnp.bfloat16)
    grad_up = (grad_active * gate_val * sigmoid_val).astype(jnp.bfloat16)
    grad_down = outer_rows(active, upstream)
    grad_wgate = outer_rows(expert_in, grad_gate)
    grad_wup = outer_rows(expert_in, grad_up)
    grad_input = inner_cols(grad_gate, weights[0]) + inner_cols(grad_up, weights[1])
    return (grad_input, grad_wgate, grad_wup, grad_down)


def on_device(
    tokens,
    norm_one,
    w_query,
    w_key,
    w_value,
    w_out,
    norm_two,
    r_gate,
    r_up,
    r_down,
    s_gate,
    s_up,
    s_down,
    logits,
    routes,
    lengths,
    cotangent,
):
    seq_len = tokens.shape[0]
    width = tokens.shape[1]
    top_count = routes.shape[1]
    slot_count = lax.axis_size("exp")
    routed_count = slot_count - 1
    capacity = min(seq_len, (seq_len * top_count * 9 // (5 * routed_count) + 7) // 8 * 8)
    seq_length = lengths[0]
    inputs_full = tokens.astype(jnp.float32)
    full_query, full_key, full_value, full_out = (
        lax.all_gather(w_query, "hid", axis=0, tiled=True),
        lax.all_gather(w_key, "hid", axis=0, tiled=True),
        lax.all_gather(w_value, "hid", axis=0, tiled=True),
        lax.all_gather(w_out, "hid", axis=0, tiled=True),
    )
    normed_one, scale_one = rms_parts(inputs_full)
    attn_in = (normed_one * norm_one).astype(jnp.bfloat16)
    cosine_table, sine_table = rotary_tables(seq_len, HD)
    heads_shape = (seq_len, HEADS, HD)
    queries = rotate(
        matmul(attn_in, full_query).reshape(heads_shape), cosine_table, sine_table
    ).astype(jnp.bfloat16)
    keys_all = rotate(
        matmul(attn_in, full_key).reshape(heads_shape), cosine_table, sine_table
    ).astype(jnp.bfloat16)
    values_all = matmul(attn_in, full_value).reshape(heads_shape).astype(jnp.bfloat16)
    attended, log_total = attend_forward(queries, keys_all, values_all, seq_length)
    attended_low = attended.reshape(seq_len, width).astype(jnp.bfloat16)
    mixed = inputs_full + matmul(attended_low, full_out)
    normed_two, scale_two = rms_parts(mixed)
    hidden_in = (normed_two * norm_two).astype(jnp.bfloat16)
    flat_routes = routes.reshape(-1)
    onehot = (flat_routes[:, None] == jnp.arange(slot_count)[None, :]).astype(jnp.int32)
    earlier = jnp.cumsum(onehot, axis=0) - onehot
    places = jnp.sum(earlier * onehot, axis=1)
    target = flat_routes * capacity + places
    assign_count = seq_len * top_count
    slot_assign = (
        jnp.full((slot_count * capacity,), assign_count, jnp.int32)
        .at[target]
        .set(jnp.arange(assign_count, dtype=jnp.int32))
    )
    slot_token = slot_assign // top_count
    token_valid = (jnp.arange(seq_len) < seq_length).astype(jnp.float32)
    soft_gates = jax.nn.softmax(logits, axis=-1)
    gate_share = soft_gates * token_valid[:, None]
    local_counts = jnp.sum(
        onehot.reshape(seq_len, top_count, slot_count).astype(jnp.float32)
        * token_valid[:, None, None],
        axis=(0, 1),
    )
    zero_row = jnp.zeros((1, width), jnp.bfloat16)
    send_rows = jnp.concatenate([hidden_in, zero_row], axis=0)[slot_token].reshape(
        slot_count, capacity, width
    )
    arrived = lax.all_to_all(send_rows, "exp", split_axis=0, concat_axis=0, tiled=True)
    gathered_rows, shared_rows = (
        lax.all_gather(arrived, "hid", axis=0, tiled=True),
        lax.all_gather(hidden_in, "hid", axis=0, tiled=True),
    )
    expert_in = gathered_rows.reshape(-1, width)
    routed_weights = (r_gate[0], r_up[0], r_down[0])
    shared_weights = (s_gate, s_up, s_down)
    routed_part, routed_kept = swiglu_forward(expert_in, routed_weights)
    shared_part, shared_kept = swiglu_forward(shared_rows, shared_weights)
    routed_own, shared_own = (
        lax.psum_scatter(
            routed_part.astype(jnp.bfloat16), "hid", scatter_dimension=0, tiled=True
        ).astype(jnp.float32),
        lax.psum_scatter(
            shared_part.astype(jnp.bfloat16), "hid", scatter_dimension=0, tiled=True
        ).astype(jnp.float32),
    )
    returned = lax.all_to_all(
        routed_own.astype(jnp.bfloat16).reshape(slot_count, capacity, width),
        "exp",
        split_axis=0,
        concat_axis=0,
        tiled=True,
    )
    picked = (
        returned.reshape(-1, width)[target].reshape(seq_len, top_count, width).astype(jnp.float32)
    )
    routed_sum = jnp.einsum("tk,tkd->td", gate_share, picked)
    output = mixed + shared_own + routed_sum
    upstream = cotangent.astype(jnp.float32)
    grad_share = jnp.sum(picked * upstream[:, None, :], axis=-1) * token_valid[:, None]
    grad_logits = soft_gates * (
        grad_share - jnp.sum(soft_gates * grad_share, axis=-1, keepdims=True)
    )
    grad_picked = (
        (gate_share[:, :, None] * upstream[:, None, :])
        .astype(jnp.bfloat16)
        .reshape(assign_count, width)
    )
    send_grads = jnp.concatenate([grad_picked, zero_row], axis=0)[slot_assign].reshape(
        slot_count, capacity, width
    )
    arrived_grads = lax.all_to_all(send_grads, "exp", split_axis=0, concat_axis=0, tiled=True)
    upstream_low = upstream.astype(jnp.bfloat16)
    gathered_grads, shared_upstream = (
        lax.all_gather(arrived_grads, "hid", axis=0, tiled=True),
        lax.all_gather(upstream_low, "hid", axis=0, tiled=True),
    )
    routed_upstream = gathered_grads.reshape(-1, width)
    routed_back = swiglu_backward(expert_in, routed_kept, routed_upstream, routed_weights)
    shared_back = swiglu_backward(shared_rows, shared_kept, shared_upstream, shared_weights)
    rows_grad, shared_in_grad = (
        lax.psum_scatter(
            routed_back[0].astype(jnp.bfloat16), "hid", scatter_dimension=0, tiled=True
        ).astype(jnp.float32),
        lax.psum_scatter(
            shared_back[0].astype(jnp.bfloat16), "hid", scatter_dimension=0, tiled=True
        ).astype(jnp.float32),
    )
    back_rows = lax.all_to_all(
        rows_grad.astype(jnp.bfloat16).reshape(slot_count, capacity, width),
        "exp",
        split_axis=0,
        concat_axis=0,
        tiled=True,
    )
    per_assign = (
        back_rows.reshape(-1, width)[target].reshape(seq_len, top_count, width).astype(jnp.float32)
    )
    grad_hidden = jnp.sum(per_assign, axis=1) + shared_in_grad
    grad_norm_in, grad_two = rms_back(normed_two, scale_two, norm_two, grad_hidden)
    grad_mixed = upstream + grad_norm_in
    grad_mixed_low = grad_mixed.astype(jnp.bfloat16)
    grad_wout = outer_rows(attended_low, grad_mixed_low)
    grad_attended = inner_cols(grad_mixed_low, full_out).astype(jnp.bfloat16).reshape(heads_shape)
    grad_query_rot, grad_key_rot, grad_value_all = attend_backward(
        queries, keys_all, values_all, seq_length, log_total, grad_attended
    )
    grad_query_pre = (
        rotate(grad_query_rot, cosine_table, -sine_table)
        .reshape(seq_len, width)
        .astype(jnp.bfloat16)
    )
    grad_key_pre = (
        rotate(grad_key_rot, cosine_table, -sine_table).reshape(seq_len, width).astype(jnp.bfloat16)
    )
    grad_value_pre = grad_value_all.reshape(seq_len, width).astype(jnp.bfloat16)
    grad_wquery = outer_rows(attn_in, grad_query_pre)
    grad_wkey = outer_rows(attn_in, grad_key_pre)
    grad_wvalue = outer_rows(attn_in, grad_value_pre)
    grad_attn_in = (
        inner_cols(grad_query_pre, full_query)
        + inner_cols(grad_key_pre, full_key)
        + inner_cols(grad_value_pre, full_value)
    )
    grad_in_one, grad_one = rms_back(normed_one, scale_one, norm_one, grad_attn_in)
    grad_tokens = (grad_mixed + grad_in_one).astype(jnp.bfloat16)
    attn_half = (
        lax.psum_scatter(
            grad_wquery.astype(jnp.bfloat16), "hid", scatter_dimension=0, tiled=True
        ).astype(jnp.float32),
        lax.psum_scatter(
            grad_wkey.astype(jnp.bfloat16), "hid", scatter_dimension=0, tiled=True
        ).astype(jnp.float32),
        lax.psum_scatter(
            grad_wvalue.astype(jnp.bfloat16), "hid", scatter_dimension=0, tiled=True
        ).astype(jnp.float32),
        lax.psum_scatter(
            grad_wout.astype(jnp.bfloat16), "hid", scatter_dimension=0, tiled=True
        ).astype(jnp.float32),
    )
    shared_grads = (shared_back[1], shared_back[2], shared_back[3])
    routed_grads = (routed_back[1][None], routed_back[2][None], routed_back[3][None])
    summed = lax.psum(
        (
            attn_half[0],
            attn_half[1],
            attn_half[2],
            attn_half[3],
            shared_grads[0],
            shared_grads[1],
            shared_grads[2],
        ),
        "exp",
    )
    small_sums = lax.psum((grad_one, grad_two, local_counts), ("exp", "hid"))
    counts = small_sums[2].astype(jnp.int32)
    return (
        output.astype(jnp.bfloat16),
        grad_tokens,
        small_sums[0],
        summed[0],
        summed[1],
        summed[2],
        summed[3],
        small_sums[1],
        routed_grads[0],
        routed_grads[1],
        routed_grads[2],
        summed[4],
        summed[5],
        summed[6],
        grad_logits,
        counts,
    )


def solution(mesh):
    in_specs = (
        P(("exp", "hid"), None),
        P(),
        P("hid", None),
        P("hid", None),
        P("hid", None),
        P("hid", None),
        P(),
        P("exp", None, "hid"),
        P("exp", None, "hid"),
        P("exp", "hid", None),
        P(None, "hid"),
        P(None, "hid"),
        P("hid", None),
        P(("exp", "hid"), None),
        P(("exp", "hid"), None),
        P(("exp", "hid")),
        P(("exp", "hid"), None),
    )
    out_specs = (
        P(("exp", "hid"), None),
        P(("exp", "hid"), None),
        P(),
        P("hid", None),
        P("hid", None),
        P("hid", None),
        P("hid", None),
        P(),
        P("exp", None, "hid"),
        P("exp", None, "hid"),
        P("exp", "hid", None),
        P(None, "hid"),
        P(None, "hid"),
        P("hid", None),
        P(("exp", "hid"), None),
        P(),
    )
    return jax.shard_map(
        on_device, mesh=mesh, in_specs=in_specs, out_specs=out_specs, check_vma=False
    )
```

profile of v0, /device:TPU:0, one launch (start us, length us, event | category | flops | bytes accessed | tf_op | source)
XLA Modules:
  0.0 1848.2 jit_solution(354958769540306111)
XLA Ops:
  18.0 7.3 scatter_custom_fusion
  30.7 9.1 all-gather.13.cloned.1.call-done
  48.3 6.5 all-gather.11.cloned.1.call-done
  76.2 12.4 gather_fusion
  88.6 7.0 all-to-all-start
  101.9 10.0 mul.524
  111.8 151.7 %all-to-all-done = bf16[16,216,1280]{2,1,0:T(8,128)(2,1)} async-done(((bf16[16,216,1280]{2,1,0:T(8,128)(2,1)}), bf16[16,216,1280]{2,1,0:T(8,128)(2,1)}, u32[]{:S(2)}, u32[]{:S(2)}) %all-to-all-start) | async-done | bytes 8847392 | tf_op jit(solution)/shard_map/all_to_all | solution.py:232
  270.5 21.9 %gather_fusion.2 = bf16[3456,1280]{1,0:T(8,128)(2,1)} fusion(bf16[1793,1280]{1,0:T(8,128)(2,1)} %concatenate.25, s32[4096]{0:T(1024)S(1)} %get-tuple-element.149), kind=kCustom, calls=%fused_computation.2 | custom fusion | bytes 17708544 | tf_op jit(solution)/shard_map/gather | solution.py:272
  292.5 233.7 %all_to_all.20 = bf16[16,216,1280]{2,1,0:T(8,128)(2,1)} all-to-all(bf16[16,216,1280]{2,1,0:T(8,128)(2,1)} %bitcast.132), channel_id=1, replica_groups=mesh['exp'=16,'hid'=2] {'exp'}, dimensions={0} | all-to-all | bytes 17694720 | tf_op jit(solution)/shard_map/all_to_all | solution.py:275
  527.5 17.8 fusion.24
  549.7 10.6 fusion.28
  560.3 33.5 %multiply_convert_fusion = (bf16[6912,448]{0,1:T(8,128)(2,1)}, bf16[6912,448]{0,1:T(8,128)(2,1)}, bf16[6912,448]{0,1:T(8,128)(2,1)}) fusion(f32[6912,448]{0,1:T(8,128)} %fusion.28, f32[6912,448]{0,1:T(8,128)} %fusion.24, bf16[6912,1280]{1,0:T(8,128)(2,1)} %bitcast.155, bf16[1,448,1280]{2,1,0:T(8,128)(2,1)S(1)} %copy-done), kind=kOutput, calls=%fused_computation.7 | convolution fusion | flops 7976779776 | bytes 62193664 | tf_op jit(solution)/shard_map/dot_general | solution.py:26
  593.9 15.4 convolution_convert_fusion
  609.5 24.4 %fusion.26 = f32[6912,1280]{1,0:T(8,128)} fusion(bf16[6912,448]{0,1:T(8,128)(2,1)} %get-tuple-element.114, bf16[1,1280,448]{1,2,0:T(8,128)(2,1)S(1)} %copy-done.71), kind=kOutput, calls=%fused_computation.79 | convolution fusion | flops 7927234560 | bytes 42729472 | tf_op jit(solution)/shard_map/dot_general | solution.py:26
  633.8 24.3 %add_convert_fusion = bf16[6912,1280]{1,0:T(8,128)(2,1)} fusion(f32[6912,1280]{1,0:T(8,128)} %fusion.26, bf16[6912,448]{0,1:T(8,128)(2,1)} %get-tuple-element.113, bf16[1,1280,448]{1,2,0:T(8,128)(2,1)S(1)} %copy-done.72), kind=kOutput, calls=%fused_computation.5 | convolution fusion | flops 7944929280 | bytes 60424192 | tf_op jit(solution)/shard_map/dot_general | solution.py:26
  663.0 21.3 %reduce-scatter.13.cloned.1.call-done = bf16[3456,1280]{1,0:T(8,128)(2,1)} async-done(((bf16[6912,1280]{1,0:T(8,128)(2,1)}), bf16[3456,1280]{1,0:T(8,128)(2,1)}) %reduce-scatter.13.cloned.1.call-update) | async-done | bytes 8847376 | tf_op jit(solution)/shard_map/reduce_scatter | solution.py:285
  684.3 146.6 %all-to-all-done.1 = bf16[16,216,1280]{2,1,0:T(8,128)(2,1)} async-done(((bf16[16,216,1280]{2,1,0:T(8,128)(2,1)}), bf16[16,216,1280]{2,1,0:T(8,128)(2,1)}, u32[]{:S(2)}, u32[]{:S(2)}) %all-to-all-start.1) | async-done | bytes 8847392 | tf_op jit(solution)/shard_map/all_to_all | solution.py:250
  830.9 39.6 %all-to-all-start.3 = ((bf16[16,216,1280]{2,1,0:T(8,128)(2,1)}), bf16[16,216,1280]{2,1,0:T(8,128)(2,1)}, u32[]{:S(2)}, u32[]{:S(2)}) async-start(bf16[16,216,1280]{2,1,0:T(8,128)(2,1)} %bitcast.133), calls=%async_computation.6 | async-start | bytes 17694720 | tf_op jit(solution)/shard_map/all_to_all | solution.py:292
  871.9 12.3 all-gather.17.cloned.1.call-done
  889.0 7.2 all-gather.23.cloned.1.call-done
  907.2 15.4 gather_fusion.1
  922.6 7.5 reshape.335
  930.1 104.0 %all-to-all-done.3 = bf16[16,216,1280]{2,1,0:T(8,128)(2,1)} async-done(((bf16[16,216,1280]{2,1,0:T(8,128)(2,1)}), bf16[16,216,1280]{2,1,0:T(8,128)(2,1)}, u32[]{:S(2)}, u32[]{:S(2)}) %all-to-all-start.3) | async-done | bytes 8847392 | tf_op jit(solution)/shard_map/all_to_all | solution.py:292
  1034.1 14.9 gather_fusion.3
  1049.0 8.0 reshape.341
  1057.1 7.1 reduce_sum.136
  1066.2 5.1 fusion.61
  1123.7 14.9 convolution_bitcast_fusion.2
  1138.7 14.9 convolution_bitcast_fusion
  1153.6 13.3 convolution_bitcast_fusion.1
  1176.5 77.8 %all-reduce.2 = (f32[1280]{0:T(1024)}, f32[1280]{0:T(1024)}, f32[16]{0:T(128)S(1)}) all-reduce(f32[1280]{0:T(1024)S(1)} %get-tuple-element.101, f32[1280]{0:T(1024)S(1)} %get-tuple-element.99, f32[16]{0:T(128)S(1)} %multiply_reduce_fusion.5), channel_id=1, replica_groups=mesh['exp'=16,'hid'=2] {'exp','hid'}, use_global_device_ids=true, to_apply=%region_19.20 | all-reduce | flops 2576 | bytes 20608 | tf_op jit(solution)/shard_map/psum | solution.py:358
  1258.1 576.2 %all-reduce.9 = (f32[640,1280]{1,0:T(8,128)}, f32[640,1280]{1,0:T(8,128)}, f32[640,1280]{1,0:T(8,128)}, f32[640,1280]{1,0:T(8,128)}) all-reduce(bf16[640,1280]{1,0:T(8,128)(2,1)} %reduce-scatter.17.cloned.1.call-done, bf16[640,1280]{1,0:T(8,128)(2,1)} %reduce-scatter.19.cloned.1.call-done, ...), channel_id=1, replica_groups=mesh['exp'=16,'hid'=2] {'exp'}, use_global_device_ids=true, to_apply=%region_21.22 | all-reduce | flops 3276800 | bytes 19660800 | tf_op jit(solution)/shard_map/psum | solution.py:346
  (302 shorter events, 160.6 us)
Async XLA Ops:
  7.2 553.1 %copy-start = (bf16[1,448,1280]{2,1,0:T(8,128)(2,1)S(1)}, bf16[1,448,1280]{2,1,0:T(8,128)(2,1)}, u32[]{:S(2)}) copy-start(bf16[1,448,1280]{2,1,0:T(8,128)(2,1)} %param.26) | copy-start | bytes 3440644
  7.2 19.3 %all-gather.9.cloned.1.call-start = ((), (), s32[]{:S(2)}) async-start(), calls=%async_computation.12 | async-start | bytes 4915200 | tf_op jit(solution)/shard_map/all_gather | solution.py:189
  7.9 31.8 %all-gather.13.cloned.1.call-start = ((), (), s32[]{:S(2)}) async-start(), calls=%async_computation.14 | async-start | bytes 4915200 | tf_op jit(solution)/shard_map/all_gather | solution.py:188
  8.7 46.1 %all-gather.11.cloned.1.call-start = ((), (), s32[]{:S(2)}) async-start(), calls=%async_computation.13 | async-start | bytes 4915200 | tf_op jit(solution)/shard_map/all_gather | solution.py:187
  9.4 62.1 %all-gather.15.cloned.1.call-start = ((), (), s32[]{:S(2)}) async-start(), calls=%async_computation.15 | async-start | bytes 4915200 | tf_op jit(solution)/shard_map/all_gather | solution.py:190
  10.4 16.1 copy-start.49
  11.5 43.3 %copy-start.61 = (f32[256]{0:T(256)}, f32[256]{0:T(256)S(1)}, u32[]{:S(2)}) copy-start(f32[256]{0:T(256)S(1)} %add_rsqrt_fusion.1) | copy-start | bytes 3076
  26.5 37.9 %copy-start.39 = (f32[256,64]{1,0:T(8,128)}, f32[256,64]{1,0:T(8,128)S(1)}, u32[]{:S(2)}) copy-start(f32[256,64]{1,0:T(8,128)S(1)} %get-tuple-element.141) | copy-start | bytes 196612
  88.6 174.9 %all-to-all-start = ((bf16[16,216,1280]{2,1,0:T(8,128)(2,1)}), bf16[16,216,1280]{2,1,0:T(8,128)(2,1)}, u32[]{:S(2)}, u32[]{:S(2)}) async-start(bf16[16,216,1280]{2,1,0:T(8,128)(2,1)} %bitcast.131), calls=%async_computation.1 | async-start | bytes 17694720 | tf_op jit(solution)/shard_map/all_to_all | solution.py:232
  95.5 430.7 %all-gather.19.cloned.1.call-start = ((), (), s32[]{:S(2)}) async-start(), calls=%async_computation.18 | async-start | bytes 26542080 | tf_op jit(solution)/shard_map/all_gather | solution.py:234
  263.5 296.8 %all-gather.21.cloned.1.call-start = ((), (), s32[]{:S(2)}) async-start(), calls=%async_computation.20 | async-start | bytes 26542080 | tf_op jit(solution)/shard_map/all_gather | solution.py:278
  526.2 132.0 %reduce-scatter.11.cloned.1.call-start = ((), (), s32[]{:S(2)}) async-start(), calls=%async_computation.19 | async-start | bytes 26542080 | tf_op jit(solution)/shard_map/reduce_scatter | solution.py:243
  527.5 21.6 %copy-start.69 = (bf16[32,216,1280]{2,1,0:T(8,128)(2,1)S(1)}, bf16[32,216,1280]{2,1,0:T(8,128)(2,1)}, u32[]{:S(2)}) copy-start(bf16[32,216,1280]{2,1,0:T(8,128)(2,1)} %all-gather.19.cloned.1.call-done) | copy-start | bytes 53084164
  527.5 22.2 %copy-start.71 = (bf16[1,1280,448]{1,2,0:T(8,128)(2,1)S(1)}, bf16[1,1280,448]{1,2,0:T(8,128)(2,1)}, u32[]{:S(2)}) copy-start(bf16[1,1280,448]{1,2,0:T(8,128)(2,1)} %param.24) | copy-start | bytes 3440644
  609.3 75.1 %reduce-scatter.13.cloned.1.call-start = ((), (), s32[]{:S(2)}) async-start(), calls=%async_computation.21 | async-start | bytes 26542080 | tf_op jit(solution)/shard_map/reduce_scatter | solution.py:285
  658.2 172.7 %all-to-all-start.1 = ((bf16[16,216,1280]{2,1,0:T(8,128)(2,1)}), bf16[16,216,1280]{2,1,0:T(8,128)(2,1)}, u32[]{:S(2)}, u32[]{:S(2)}) async-start(bf16[16,216,1280]{2,1,0:T(8,128)(2,1)} %bitcast.134), calls=%async_computation.3 | async-start | bytes 17694720 | tf_op jit(solution)/shard_map/all_to_all | solution.py:250
  830.9 53.2 %copy-start.42 = (bf16[1280,448]{0,1:T(8,128)(2,1)S(1)}, bf16[1280,448]{0,1:T(8,128)(2,1)}, u32[]{:S(2)}) copy-start(bf16[1280,448]{0,1:T(8,128)(2,1)} %param.28) | copy-start | bytes 3440644
  830.9 203.2 %all-to-all-start.3 = ((bf16[16,216,1280]{2,1,0:T(8,128)(2,1)}), bf16[16,216,1280]{2,1,0:T(8,128)(2,1)}, u32[]{:S(2)}, u32[]{:S(2)}) async-start(bf16[16,216,1280]{2,1,0:T(8,128)(2,1)} %bitcast.133), calls=%async_computation.6 | async-start | bytes 17694720 | tf_op jit(solution)/shard_map/all_to_all | solution.py:292
  870.5 13.7 all-gather.17.cloned.1.call-start
  871.3 24.9 %all-gather.23.cloned.1.call-start = ((), (), s32[]{:S(2)}) async-start(), calls=%async_computation.22 | async-start | bytes 1966080 | tf_op jit(solution)/shard_map/all_gather | solution.py:279
  871.8 15.5 copy-start.41
  871.9 192.4 %reduce-scatter.15.cloned.1.call-start = ((), (), s32[]{:S(2)}) async-start(), calls=%async_computation.23 | async-start | bytes 1966080 | tf_op jit(solution)/shard_map/reduce_scatter | solution.py:288
  903.1 168.3 %reduce-scatter.9.cloned.1.call-start = ((), (), s32[]{:S(2)}) async-start(), calls=%async_computation.17 | async-start | bytes 1966080 | tf_op jit(solution)/shard_map/reduce_scatter | solution.py:246
  906.3 351.7 %reduce-scatter.23.cloned.1.call-start = ((), (), s32[]{:S(2)}) async-start(), calls=%async_computation.27 | async-start | bytes 4915200 | tf_op jit(solution)/shard_map/reduce_scatter | solution.py:340
  1078.6 179.4 %reduce-scatter.21.cloned.1.call-start = ((), (), s32[]{:S(2)}) async-start(), calls=%async_computation.26 | async-start | bytes 4915200 | tf_op jit(solution)/shard_map/reduce_scatter | solution.py:337
  1090.3 167.7 %reduce-scatter.19.cloned.1.call-start = ((), (), s32[]{:S(2)}) async-start(), calls=%async_computation.25 | async-start | bytes 4915200 | tf_op jit(solution)/shard_map/reduce_scatter | solution.py:334
  1106.3 151.8 %reduce-scatter.17.cloned.1.call-start = ((), (), s32[]{:S(2)}) async-start(), calls=%async_computation.24 | async-start | bytes 4915200 | tf_op jit(solution)/shard_map/reduce_scatter | solution.py:331
  1115.0 719.2 %all-reduce.8.cloned.1.call-start = ((), (), s32[]{:S(2)}) async-start(), calls=%async_computation.28 | async-start | bytes 13762560 | tf_op jit(solution)/shard_map/psum | solution.py:346
  1123.7 29.9 %slice-start.2 = ((s8[6193152]{0:T(1024)(128)(4,1)}), s8[4194304]{0:T(1024)(128)(4,1)S(1)}, s32[]{:S(2)}) async-start(s8[6193152]{0:T(1024)(128)(4,1)} %bitcast.157), calls=%async_computation.31 | async-start | bytes 8388608
  1138.7 15.0 slice-start.3
  1138.7 28.3 %slice-start = ((s8[5242880]{0:T(1024)(128)(4,1)}), s8[4194304]{0:T(1024)(128)(4,1)S(1)}, s32[]{:S(2)}) async-start(s8[5242880]{0:T(1024)(128)(4,1)} %bitcast.129), calls=%async_computation.29 | async-start | bytes 8388608
  1153.6 13.4 slice-start.1
  (66 other events, 167.1 us)
Sparse Core Ops, SparseCore 0:
  9.6 15.0 all-gather.8
  26.2 13.5 all-gather.12
  41.3 13.4 all-gather.10
  56.2 13.4 all-gather.14
  263.6 66.5 all-gather.18
  526.3 31.2 all-gather.20
  609.4 25.4 reduce-scatter.10
  658.3 25.9 reduce-scatter.12
  873.5 10.6 all-gather.16
  885.6 10.5 all-gather.22
  903.2 9.9 reduce-scatter.14
  916.0 9.9 reduce-scatter.8
  1078.7 47.0 reduce-scatter.22
  1128.6 12.2 reduce-scatter.20
  1143.5 12.2 reduce-scatter.18
  1158.6 12.1 reduce-scatter.16
  1177.7 312.7 all-reduce.7
where the time goes:
time: 1850 us
  blocking collectives  888 us (48%)
  waiting for transfers between devices  463 us (25%)
  matrix products  239 us (13%)
  local copies, waits for them, and re-layouts  150 us (8%)
  starting transfers between devices  53.1 us (3%)
  other arithmetic  39.7 us (2%)
    psum x1, blocking collectives, on_device(): lax.psum((attn_half[0], attn_half[1], attn_half[2], attn_half[3], shared_...  576 us
    all_to_all x1, blocking collectives, on_device(): lax.all_to_all(send_grads, 'exp', split_axis=0, concat_axis=0, tiled=True)  234 us
    all_to_all x1, waiting for transfers between devices, on_device(): lax.all_to_all(send_rows, 'exp', split_axis=0, concat_axis=0, tiled=True)  152 us
    all_to_all x1, waiting for transfers between devices, on_device(): lax.all_to_all(routed_own.astype(jnp.bfloat16).reshape(slot_count, capaci...  147 us
    all_to_all x1, waiting for transfers between devices, on_device(): lax.all_to_all(rows_grad.astype(jnp.bfloat16).reshape(slot_count, capacit...  104 us
    dot_general x10, matrix products, inner_cols(): lax.dot_general(left_side, right_side, contract_cols, preferred_element_t...  98.1 us
    psum x1, blocking collectives, on_device(): small_sums = lax.psum((grad_one, grad_two, local_counts), ('exp', 'hid'))  77.8 us
    dot_general x10, matrix products, matmul(): return jnp.dot(left_side, right_side, preferred_element_type=jnp.float32)  63.7 us
  transfers between devices with their start and end apart: 20, of which 8 were waited for; matrix products, arithmetic and copies ran while one was open for 18% of the time, Pallas kernels for 0%

commit v1 on v0

--- a/solution.py
+++ b/solution.py
@@ -1,10 +1,15 @@
+import functools
+
 import jax
 import jax.numpy as jnp
 from jax import lax
+from jax.experimental import pallas as pl
+from jax.experimental.pallas import tpu as pltpu
 from jax.sharding import PartitionSpec as P
 
 HEADS = 10
 HD = 128
+MESH = pl.DeviceIdType.MESH
 
 
 norm_eps = 1e-06
@@ -134,26 +139,362 @@
     return (grad_query.reshape(queries.shape), grad_keys, grad_values)
 
 
-def swiglu_forward(expert_in, weights):
-    gate_val = matmul(expert_in, weights[0])
-    up_val = matmul(expert_in, weights[1])
-    active = (jax.nn.silu(gate_val) * up_val).astype(jnp.bfloat16)
-    return (matmul(active, weights[2]), (gate_val, up_val, active))
-
-
-def swiglu_backward(expert_in, kept, upstream, weights):
-    gate_val, up_val, active = kept
-    grad_active = inner_cols(upstream, weights[2])
-    sigmoid_val = jax.nn.sigmoid(gate_val)
-    grad_gate = (
-        grad_active * up_val * sigmoid_val * (1.0 + gate_val * (1.0 - sigmoid_val))
-    ).astype(jnp.bfloat16)
-    grad_up = (grad_active * gate_val * sigmoid_val).astype(jnp.bfloat16)
-    grad_down = outer_rows(active, upstream)
-    grad_wgate = outer_rows(expert_in, grad_gate)
-    grad_wup = outer_rows(expert_in, grad_up)
-    grad_input = inner_cols(grad_gate, weights[0]) + inner_cols(grad_up, weights[1])
-    return (grad_input, grad_wgate, grad_wup, grad_down)
+class Place:
+    def __init__(self, n):
+        self.nz = 4; self.m = {16: 2, 64: 4}[n]; m = self.m
+        self.e = lax.axis_index("exp"); self.c = lax.axis_index("hid"); c = self.c; e = self.e
+        self.s1 = m * m; self.s2 = 1 + c * (m - 1); self.s3 = m - c * (m - 1)
+        self.c1 = e // self.s1; self.c2 = (e // self.s2) % m; self.c3 = (e // self.s3) % m
+    def blk(self, a, b, d): return a * self.s1 + b * self.s2 + d * self.s3
+    def o2(self): return [(self.c2 + j) % self.m for j in range(1, self.m)]
+    def o3(self): return [(self.c3 + j) % self.m for j in range(1, self.m)]
+    def enter(self):
+        bar = pltpu.get_barrier_semaphore()
+        c1, c2, c3 = self.c1, self.c2, self.c3
+        def sig(p): pl.semaphore_signal(bar, inc=1, device_id=(p, self.c), device_id_type=MESH)
+        for j in self.o2(): sig(self.blk(c1, j, c3))
+        for j in self.o3(): sig(self.blk(c1, c2, j))
+        for j in range(1, self.nz): sig(self.blk((c1 + j) % self.nz, c2, c3))
+        pl.semaphore_wait(bar, 2 * (self.m - 1) + self.nz - 1)
+
+class Gather:
+    def __init__(self, pc, src, dst, ssem, rsem, split, base=0):
+        self.pc, self.src, self.dst, self.ssem, self.rsem = pc, src, dst, ssem, rsem
+        self.split = split; self.sends = []; self.base = base
+    def view(self, ref, part):
+        R = self.src.shape[0]
+        return ref.at[pl.ds(0, self.split)] if part == 0 else ref.at[pl.ds(self.split, R - self.split)]
+    def send(self, part, own, b, to, cond=None):
+        i = self.base + len(self.sends)
+        src = self.view(self.src if own else self.dst.at[b], part)
+        cp = pltpu.make_async_remote_copy(src_ref=src, dst_ref=self.view(self.dst.at[b], part), send_sem=self.ssem.at[i], recv_sem=self.rsem.at[part, b], device_id=(to, self.pc.c), device_id_type=MESH)
+        self.sends.append((cond, cp))
+        if cond is None: cp.start()
+        else: pl.when(cond)(cp.start)
+    def wait(self, part, b):
+        v = self.view(self.dst.at[b], part)
+        pltpu.make_async_copy(v, v, self.rsem.at[part, b]).wait()
+    def updown(self, part, own, b):
+        pc = self.pc
+        self.send(part, own, b, pc.blk(pc.c1 + 1, pc.c2, pc.c3), pc.c1 < pc.nz - 1)
+        self.send(part, own, b, pc.blk(pc.c1 - 1, pc.c2, pc.c3), pc.c1 > 0)
+    def to2(self, part, own, b):
+        pc = self.pc
+        for j in pc.o2(): self.send(part, own, b, pc.blk(pc.c1, j, pc.c3))
+    def to3(self, part, own, b):
+        pc = self.pc
+        for j in pc.o3(): self.send(part, own, b, pc.blk(pc.c1, pc.c2, j))
+    def start(self):
+        e = self.pc.e
+        self.to3(0, True, e); self.to2(0, True, e); self.updown(0, True, e)
+        if self.split < self.src.shape[0]:
+            self.to3(1, True, e); self.to2(1, True, e); self.updown(1, True, e)
+    def zarr(self, part, s, up, k2, k3, more):
+        pc = self.pc
+        a = pc.c1 - s if up else pc.c1 + s
+        cond = (pc.c1 >= s) if up else (pc.c1 < pc.nz - s)
+        b = pc.blk(a, k2, k3)
+        pl.when(cond)(lambda: self.wait(part, b))
+        if s < pc.nz - 1:
+            if up: self.send(part, False, b, pc.blk(pc.c1 + 1, pc.c2, pc.c3), (pc.c1 >= s) & (pc.c1 < pc.nz - 1))
+            else: self.send(part, False, b, pc.blk(pc.c1 - 1, pc.c2, pc.c3), (pc.c1 < pc.nz - s) & (pc.c1 > 0))
+        if more:
+            for j in pc.o2(): self.send(part, False, b, pc.blk(pc.c1, j, pc.c3), cond)
+            for j in pc.o3(): self.send(part, False, b, pc.blk(pc.c1, pc.c2, j), cond)
+    def events(self):
+        pc = self.pc; ev = []
+        def a2(s):
+            def go():
+                for j in pc.o2():
+                    for sg in ((1, -1) if s else (1,)):
+                        a = pc.c1 + sg * s
+                        cond = None if s == 0 else ((a >= 0) & (a < pc.nz))
+                        b = pc.blk(a, j, pc.c3)
+                        if cond is None: self.wait(0, b)
+                        else: pl.when(cond)(lambda b=b: self.wait(0, b))
+                        for k in pc.o3(): self.send(0, False, b, pc.blk(pc.c1, pc.c2, k), cond)
+            return go
+        def az(s):
+            def go():
+                self.zarr(0, s, True, pc.c2, pc.c3, True); self.zarr(0, s, False, pc.c2, pc.c3, True)
+            return go
+        B = self.split < self.src.shape[0]
+        def f1():
+            for j in pc.o2():
+                b = pc.blk(pc.c1, j, pc.c3); self.wait(1, b); self.to3(1, False, b); self.updown(1, False, b)
+        def f2():
+            for k in pc.o3():
+                b = pc.blk(pc.c1, pc.c2, k); self.wait(1, b); self.updown(1, False, b)
+        def f3():
+            for j in pc.o2():
+                for k in pc.o3():
+                    b = pc.blk(pc.c1, j, k); self.wait(1, b); self.updown(1, False, b)
+        def fz(s):
+            def go():
+                for k2 in range(pc.m):
+                    for k3 in range(pc.m):
+                        self.zarr(1, s, True, k2, k3, False); self.zarr(1, s, False, k2, k3, False)
+            return go
+        ev += [az(1), a2(0)]
+        if B: ev += [f1, f2, f3]
+        ev += [az(2), a2(1)]
+        if B: ev += [fz(1)]
+        ev += [az(3), a2(2)]
+        if B: ev += [fz(2)]
+        ev += [a2(3)]
+        if B: ev += [fz(3)]
+        def last():
+            for a in range(pc.nz):
+                for j in range(pc.m):
+                    for k in pc.o3(): self.wait(0, pc.blk(a, j, k))
+        ev += [last]
+        return ev
+    def finish(self):
+        for cond, cp in self.sends:
+            if cond is None: cp.wait_send()
+            else: pl.when(cond)(cp.wait_send)
+
+
+def gather_kernel(n, x_ref, w_ref, ox_ref, ow_ref, ssem, rsem, lsem):
+    pc = Place(n)
+    pc.enter()
+    rows = x_ref.shape[0]
+    first = Gather(pc, x_ref, ox_ref, ssem.at[0], rsem.at[0], rows)
+    second = Gather(pc, w_ref, ow_ref, ssem.at[1], rsem.at[1], rows)
+    first.start()
+    second.start()
+    own_x = pltpu.make_async_copy(x_ref, ox_ref.at[pc.e], lsem.at[0])
+    own_w = pltpu.make_async_copy(w_ref, ow_ref.at[pc.e], lsem.at[1])
+    own_x.start()
+    own_w.start()
+    for event in first.events():
+        event()
+    for event in second.events():
+        event()
+    first.finish()
+    second.finish()
+    own_x.wait()
+    own_w.wait()
+
+
+def gather_both(x, w):
+    n = lax.axis_size("exp")
+    any_spec = pl.BlockSpec(memory_space=pl.ANY)
+    return pl.pallas_call(
+        functools.partial(gather_kernel, n),
+        out_shape=(jax.ShapeDtypeStruct((n,) + x.shape, x.dtype), jax.ShapeDtypeStruct((n,) + w.shape, w.dtype)),
+        in_specs=[any_spec, any_spec],
+        out_specs=(any_spec, any_spec),
+        scratch_shapes=[
+            pltpu.SemaphoreType.DMA((2, 128)),
+            pltpu.SemaphoreType.DMA((2, 2, n)),
+            pltpu.SemaphoreType.DMA((2,)),
+        ],
+        compiler_params=pltpu.CompilerParams(collective_id=0, has_side_effects=True),
+    )(x, w)
+
+
+def experts_kernel(
+    n, slots,
+    h_hbm, dy_hbm, gate_ref, wg, wu, wd,
+    s_ref, sums_hbm, gg_hbm, gu_hbm, gd_hbm, pg_hbm, pu_hbm, pd_hbm, r3_hbm, r2_hbm, r1_hbm,
+    og, ou, od, ysum, hbuf, dbuf, act, dg, dup, stage, rbuf, xg, xu, xd,
+    lsem, ssem, r3sem, r2sem, r1sem, bsem, xssem, xrsem, osem,
+):
+    pc = Place(n)
+    nz, m = pc.nz, pc.m
+    c1, c2, c3, e, c = pc.c1, pc.c2, pc.c3, pc.e, pc.c
+    barrier = pltpu.get_barrier_semaphore()
+
+    def greet(to, core):
+        pl.semaphore_signal(barrier, inc=1, device_id=(to, core), device_id_type=MESH)
+
+    for j in range(1, m):
+        greet(pc.blk(c1, c2, (c3 + j) % m), c)
+        greet(pc.blk(c1, (c2 + j) % m, c3), c)
+    for j in range(1, nz):
+        greet(pc.blk((c1 + j) % nz, c2, c3), c)
+    greet(e, 1 - c)
+    pl.semaphore_wait(barrier, 2 * (m - 1) + nz)
+
+    og[...] = jnp.zeros_like(og)
+    ou[...] = jnp.zeros_like(ou)
+    od[...] = jnp.zeros_like(od)
+    s_ref[...] = jnp.zeros_like(s_ref)
+    n3 = (m - 1) * nz * m
+    n2 = (m - 1) * nz
+
+    def dest(t):
+        return (c1 + t + 1) % nz, (c2 + t // nz + 1) % m, (c3 + t // (nz * m) + 1) % m
+
+    def load(t, i):
+        b = pc.blk(*dest(t))
+        return (
+            pltpu.make_async_copy(h_hbm.at[b], hbuf.at[i], lsem.at[0, i]),
+            pltpu.make_async_copy(dy_hbm.at[b], dbuf.at[i], lsem.at[1, i]),
+        )
+
+    def partial_copy(i, to, dst, sem):
+        return pltpu.make_async_remote_copy(
+            src_ref=stage.at[i], dst_ref=dst, send_sem=ssem.at[i], recv_sem=sem,
+            device_id=(to, c), device_id_type=MESH,
+        )
+
+    def add_received(src, sem):
+        pltpu.make_async_remote_copy(
+            src_ref=src, dst_ref=src, send_sem=ssem.at[0], recv_sem=sem,
+            device_id=(e, 1 - c), device_id_type=MESH,
+        ).wait_recv()
+        copy = pltpu.make_async_copy(src, rbuf, bsem)
+        copy.start()
+        copy.wait()
+        ysum[...] += rbuf[...].astype(jnp.float32)
+
+    def swaps():
+        return [
+            pltpu.make_async_remote_copy(
+                src_ref=src, dst_ref=dst, send_sem=xssem.at[i], recv_sem=xrsem.at[i],
+                device_id=(e, 1 - c), device_id_type=MESH,
+            )
+            for i, (src, dst) in enumerate(((xg, pg_hbm), (xu, pu_hbm), (xd, pd_hbm)))
+        ]
+
+    def own_halves():
+        return [
+            pltpu.make_async_copy(src.at[c], dst, osem.at[i])
+            for i, (src, dst) in enumerate(((og, gg_hbm), (ou, gu_hbm), (od, gd_hbm)))
+        ]
+
+    for copy in load(0, 0):
+        copy.start()
+
+    def body(t, carry):
+        i = t % 2
+        slot = t % slots
+        a, b2, b3 = dest(t)
+        b = pc.blk(a, b2, b3)
+        for copy in load(t, i):
+            copy.wait()
+
+        @pl.when(t < n - 1)
+        def _():
+            for copy in load(t + 1, 1 - i):
+                copy.start()
+
+        lane = lax.broadcasted_iota(jnp.int32, gate_ref.shape, 1)
+        gate = jnp.sum(jnp.where(lane == b, gate_ref[...], 0.0), axis=1, keepdims=True)
+        h = hbuf[i]
+        dy = dbuf[i].astype(jnp.float32)
+        z = (gate * dy).astype(jnp.bfloat16)
+        for half in range(2):
+            g = matmul(h, wg[half])
+            u = matmul(h, wu[half])
+            da = inner_cols(z, wd[half])
+            sg = jax.nn.sigmoid(g)
+            si = g * sg
+            act[half] = (si * u).astype(jnp.bfloat16)
+            dup[half] = (da * si).astype(jnp.bfloat16)
+            dg[half] = (da * u * sg * (1.0 + g * (1.0 - sg))).astype(jnp.bfloat16)
+        y = (matmul(act[0], wd[0]) + matmul(act[1], wd[1])).astype(jnp.bfloat16).astype(jnp.float32)
+        s = jnp.sum(y * dy, axis=1, keepdims=True)
+        s_ref[...] = jnp.where(lane == b, s, s_ref[...])
+        ysum[0] = gate * y
+        ysum[1] = (
+            inner_cols(dg[0], wg[0]) + inner_cols(dg[1], wg[1])
+            + inner_cols(dup[0], wu[0]) + inner_cols(dup[1], wu[1])
+        ).astype(jnp.bfloat16).astype(jnp.float32)
+
+        @pl.when((t >= slots) & (t - slots < n - 1))
+        def _():
+            partial_copy(slot, e, r1_hbm.at[0], r1sem.at[0]).wait_send()
+
+        @pl.when(t >= n3)
+        def _():
+            for j in range(1, m):
+                add_received(r3_hbm.at[j - 1, a, b2], r3sem.at[j - 1, a, b2])
+
+        @pl.when(t >= n3 + n2)
+        def _():
+            for j in range(1, m):
+                add_received(r2_hbm.at[j - 1, a], r2sem.at[j - 1, a])
+
+        @pl.when(t < n - 1)
+        def _():
+            stage[slot] = ysum[...].astype(jnp.bfloat16)
+
+        for j in range(1, m):
+            @pl.when((t < n3) & (b3 == (c3 + j) % m))
+            def _():
+                partial_copy(slot, pc.blk(c1, c2, b3), r3_hbm.at[m - j - 1, a, b2], r3sem.at[m - j - 1, a, b2]).start()
+
+            @pl.when((t >= n3) & (t < n3 + n2) & (b2 == (c2 + j) % m))
+            def _():
+                partial_copy(slot, pc.blk(c1, b2, c3), r2_hbm.at[m - j - 1, a], r2sem.at[m - j - 1, a]).start()
+
+        for j in range(1, nz):
+            @pl.when((t >= n3 + n2) & (t < n - 1) & (a == (c1 + j) % nz))
+            def _():
+                partial_copy(slot, pc.blk(a, c2, c3), r1_hbm.at[nz - j - 1], r1sem.at[nz - j - 1]).start()
+
+        for half in range(2):
+            og[half] += outer_rows(h, dg[half])
+            ou[half] += outer_rows(h, dup[half])
+            od[half] += outer_rows(act[half], z)
+        return carry
+
+    lax.fori_loop(0, n, body, 0)
+    xg[...] = og[1 - c].astype(jnp.bfloat16)
+    xu[...] = ou[1 - c].astype(jnp.bfloat16)
+    xd[...] = od[1 - c].astype(jnp.bfloat16)
+    for copy in swaps():
+        copy.start()
+    for copy in own_halves():
+        copy.start()
+    for j in range(1, nz):
+        add_received(r1_hbm.at[j - 1], r1sem.at[j - 1])
+    final = pltpu.make_async_copy(ysum, sums_hbm, bsem)
+    final.start()
+    final.wait()
+    for t in range(max(0, n - slots), n - 1):
+        partial_copy(t % slots, e, r1_hbm.at[0], r1sem.at[0]).wait_send()
+    for copy in swaps():
+        copy.wait()
+    for copy in own_halves():
+        copy.wait()
+
+
+def experts(h, dy, gates, wg, wu, wd):
+    n, rows, width = h.shape
+    hidden = wg.shape[2]
+    nz = 4
+    m = {16: 2, 64: 4}[n]
+    slots = 8
+    vmem = pl.BlockSpec(memory_space=pltpu.VMEM)
+    hbm = pl.BlockSpec(memory_space=pl.ANY)
+    f32, b16 = jnp.float32, jnp.bfloat16
+    out = jax.ShapeDtypeStruct
+    return pl.pallas_call(
+        functools.partial(experts_kernel, n, slots),
+        out_shape=(
+            out((rows, n), f32), out((2, rows, width), f32),
+            out((width, hidden), f32), out((width, hidden), f32), out((hidden, width), f32),
+            out((width, hidden), b16), out((width, hidden), b16), out((hidden, width), b16),
+            out((m - 1, nz, m, 2, rows, width), b16), out((m - 1, nz, 2, rows, width), b16), out((nz - 1, 2, rows, width), b16),
+        ),
+        in_specs=[hbm, hbm, vmem, vmem, vmem, vmem],
+        out_specs=(vmem,) + (hbm,) * 10,
+        scratch_shapes=[
+            pltpu.VMEM((2, width, hidden), f32), pltpu.VMEM((2, width, hidden), f32), pltpu.VMEM((2, hidden, width), f32),
+            pltpu.VMEM((2, rows, width), f32), pltpu.VMEM((2, rows, width), b16), pltpu.VMEM((2, rows, width), b16),
+            pltpu.VMEM((2, rows, hidden), b16), pltpu.VMEM((2, rows, hidden), b16), pltpu.VMEM((2, rows, hidden), b16),
+            pltpu.VMEM((slots, 2, rows, width), b16), pltpu.VMEM((2, rows, width), b16),
+            pltpu.VMEM((width, hidden), b16), pltpu.VMEM((width, hidden), b16), pltpu.VMEM((hidden, width), b16),
+            pltpu.SemaphoreType.DMA((2, 2)), pltpu.SemaphoreType.DMA((slots,)),
+            pltpu.SemaphoreType.DMA((m - 1, nz, m)), pltpu.SemaphoreType.DMA((m - 1, nz)), pltpu.SemaphoreType.DMA((nz - 1,)),
+            pltpu.SemaphoreType.DMA, pltpu.SemaphoreType.DMA((3,)), pltpu.SemaphoreType.DMA((3,)), pltpu.SemaphoreType.DMA((3,)),
+        ],
+        compiler_params=pltpu.CompilerParams(collective_id=1, has_side_effects=True, vmem_limit_bytes=60 * 2**20),
+    )(h, dy, gates, wg, wu, wd)
 
 
 def on_device(
@@ -177,10 +518,7 @@
 ):
     seq_len = tokens.shape[0]
     width = tokens.shape[1]
-    top_count = routes.shape[1]
     slot_count = lax.axis_size("exp")
-    routed_count = slot_count - 1
-    capacity = min(seq_len, (seq_len * top_count * 9 // (5 * routed_count) + 7) // 8 * 8)
     seq_length = lengths[0]
     inputs_full = tokens.astype(jnp.float32)
     full_query, full_key, full_value, full_out = (
@@ -205,101 +543,30 @@
     mixed = inputs_full + matmul(attended_low, full_out)
     normed_two, scale_two = rms_parts(mixed)
     hidden_in = (normed_two * norm_two).astype(jnp.bfloat16)
-    flat_routes = routes.reshape(-1)
-    onehot = (flat_routes[:, None] == jnp.arange(slot_count)[None, :]).astype(jnp.int32)
-    earlier = jnp.cumsum(onehot, axis=0) - onehot
-    places = jnp.sum(earlier * onehot, axis=1)
-    target = flat_routes * capacity + places
-    assign_count = seq_len * top_count
-    slot_assign = (
-        jnp.full((slot_count * capacity,), assign_count, jnp.int32)
-        .at[target]
-        .set(jnp.arange(assign_count, dtype=jnp.int32))
-    )
-    slot_token = slot_assign // top_count
+    onehot = (routes[:, :, None] == jnp.arange(slot_count)[None, None, :]).astype(jnp.float32)
     token_valid = (jnp.arange(seq_len) < seq_length).astype(jnp.float32)
     soft_gates = jax.nn.softmax(logits, axis=-1)
     gate_share = soft_gates * token_valid[:, None]
-    local_counts = jnp.sum(
-        onehot.reshape(seq_len, top_count, slot_count).astype(jnp.float32)
-        * token_valid[:, None, None],
-        axis=(0, 1),
-    )
-    zero_row = jnp.zeros((1, width), jnp.bfloat16)
-    send_rows = jnp.concatenate([hidden_in, zero_row], axis=0)[slot_token].reshape(
-        slot_count, capacity, width
-    )
-    arrived = lax.all_to_all(send_rows, "exp", split_axis=0, concat_axis=0, tiled=True)
-    gathered_rows, shared_rows = (
-        lax.all_gather(arrived, "hid", axis=0, tiled=True),
-        lax.all_gather(hidden_in, "hid", axis=0, tiled=True),
-    )
-    expert_in = gathered_rows.reshape(-1, width)
-    routed_weights = (r_gate[0], r_up[0], r_down[0])
-    shared_weights = (s_gate, s_up, s_down)
-    routed_part, routed_kept = swiglu_forward(expert_in, routed_weights)
-    shared_part, shared_kept = swiglu_forward(shared_rows, shared_weights)
-    routed_own, shared_own = (
-        lax.psum_scatter(
-            routed_part.astype(jnp.bfloat16), "hid", scatter_dimension=0, tiled=True
-        ).astype(jnp.float32),
-        lax.psum_scatter(
-            shared_part.astype(jnp.bfloat16), "hid", scatter_dimension=0, tiled=True
-        ).astype(jnp.float32),
-    )
-    returned = lax.all_to_all(
-        routed_own.astype(jnp.bfloat16).reshape(slot_count, capacity, width),
-        "exp",
-        split_axis=0,
-        concat_axis=0,
-        tiled=True,
-    )
-    picked = (
-        returned.reshape(-1, width)[target].reshape(seq_len, top_count, width).astype(jnp.float32)
-    )
-    routed_sum = jnp.einsum("tk,tkd->td", gate_share, picked)
-    output = mixed + shared_own + routed_sum
+    local_counts = jnp.sum(onehot * token_valid[:, None, None], axis=(0, 1))
+    is_last = jnp.arange(slot_count) == slot_count - 1
+    own_gates = jnp.where(is_last[None, :], 1.0, jnp.sum(onehot * gate_share[:, :, None], axis=1))
+    gates = lax.all_to_all(own_gates.T, "exp", split_axis=0, concat_axis=0, tiled=True).T
+    holds_shared = lax.axis_index("exp") == slot_count - 1
+    wg, wu, wd = (
+        lax.all_gather(jnp.where(holds_shared, shared, routed[0]), "hid", axis=0)
+        for shared, routed in ((s_gate, r_gate), (s_up, r_up), (s_down, r_down))
+    )
+    all_dy, all_h = gather_both(cotangent, hidden_in)
+    scores_e, sums, gg, gu, gd, pg, pu, pd = experts(all_h, all_dy, gates, wg, wu, wd)[:8]
+    slot_grads = (gg + pg.astype(jnp.float32), gu + pu.astype(jnp.float32), gd + pd.astype(jnp.float32))
+    scores = lax.all_to_all(scores_e.T, "exp", split_axis=0, concat_axis=0, tiled=True).T
+    output = mixed + sums[0]
     upstream = cotangent.astype(jnp.float32)
-    grad_share = jnp.sum(picked * upstream[:, None, :], axis=-1) * token_valid[:, None]
+    grad_share = jnp.sum(onehot * scores[:, None, :], axis=-1) * token_valid[:, None]
     grad_logits = soft_gates * (
         grad_share - jnp.sum(soft_gates * grad_share, axis=-1, keepdims=True)
     )
-    grad_picked = (
-        (gate_share[:, :, None] * upstream[:, None, :])
-        .astype(jnp.bfloat16)
-        .reshape(assign_count, width)
-    )
-    send_grads = jnp.concatenate([grad_picked, zero_row], axis=0)[slot_assign].reshape(
-        slot_count, capacity, width
-    )
-    arrived_grads = lax.all_to_all(send_grads, "exp", split_axis=0, concat_axis=0, tiled=True)
-    upstream_low = upstream.astype(jnp.bfloat16)
-    gathered_grads, shared_upstream = (
-        lax.all_gather(arrived_grads, "hid", axis=0, tiled=True),
-        lax.all_gather(upstream_low, "hid", axis=0, tiled=True),
-    )
-    routed_upstream = gathered_grads.reshape(-1, width)
-    routed_back = swiglu_backward(expert_in, routed_kept, routed_upstream, routed_weights)
-    shared_back = swiglu_backward(shared_rows, shared_kept, shared_upstream, shared_weights)
-    rows_grad, shared_in_grad = (
-        lax.psum_scatter(
-            routed_back[0].astype(jnp.bfloat16), "hid", scatter_dimension=0, tiled=True
-        ).astype(jnp.float32),
-        lax.psum_scatter(
-            shared_back[0].astype(jnp.bfloat16), "hid", scatter_dimension=0, tiled=True
-        ).astype(jnp.float32),
-    )
-    back_rows = lax.all_to_all(
-        rows_grad.astype(jnp.bfloat16).reshape(slot_count, capacity, width),
-        "exp",
-        split_axis=0,
-        concat_axis=0,
-        tiled=True,
-    )
-    per_assign = (
-        back_rows.reshape(-1, width)[target].reshape(seq_len, top_count, width).astype(jnp.float32)
-    )
-    grad_hidden = jnp.sum(per_assign, axis=1) + shared_in_grad
+    grad_hidden = sums[1]
     grad_norm_in, grad_two = rms_back(normed_two, scale_two, norm_two, grad_hidden)
     grad_mixed = upstream + grad_norm_in
     grad_mixed_low = grad_mixed.astype(jnp.bfloat16)
@@ -330,19 +597,19 @@
     attn_half = (
         lax.psum_scatter(
             grad_wquery.astype(jnp.bfloat16), "hid", scatter_dimension=0, tiled=True
-        ).astype(jnp.float32),
+        ),
         lax.psum_scatter(
             grad_wkey.astype(jnp.bfloat16), "hid", scatter_dimension=0, tiled=True
-        ).astype(jnp.float32),
+        ),
         lax.psum_scatter(
             grad_wvalue.astype(jnp.bfloat16), "hid", scatter_dimension=0, tiled=True
-        ).astype(jnp.float32),
+        ),
         lax.psum_scatter(
             grad_wout.astype(jnp.bfloat16), "hid", scatter_dimension=0, tiled=True
-        ).astype(jnp.float32),
-    )
-    shared_grads = (shared_back[1], shared_back[2], shared_back[3])
-    routed_grads = (routed_back[1][None], routed_back[2][None], routed_back[3][None])
+        ),
+    )
+    shared_grads = tuple(jnp.where(holds_shared, grad, 0.0).astype(jnp.bfloat16) for grad in slot_grads)
+    routed_grads = tuple(jnp.where(holds_shared, 0.0, grad)[None] for grad in slot_grads)
     summed = lax.psum(
         (
             attn_half[0],
@@ -361,17 +628,17 @@
         output.astype(jnp.bfloat16),
         grad_tokens,
         small_sums[0],
-        summed[0],
-        summed[1],
-        summed[2],
-        summed[3],
+        summed[0].astype(jnp.float32),
+        summed[1].astype(jnp.float32),
+        summed[2].astype(jnp.float32),
+        summed[3].astype(jnp.float32),
         small_sums[1],
         routed_grads[0],
         routed_grads[1],
         routed_grads[2],
-        summed[4],
-        summed[5],
-        summed[6],
+        summed[4].astype(jnp.float32),
+        summed[5].astype(jnp.float32),
+        summed[6].astype(jnp.float32),
         grad_logits,
         counts,
     )

time: 1850 us -> 886 us (0.48)
  blocking collectives: 888 us -> 45.6 us
  Pallas kernels: 0 us -> 402 us
  matrix products: 239 us -> 44.3 us
  waiting for transfers between devices: 463 us -> 275 us
  local copies, waits for them, and re-layouts: 150 us -> 42.4 us
  starting transfers between devices: 53.1 us -> 16.5 us
    psum x1 -> x0, blocking collectives: 576 us -> none  [on_device(): lax.psum((attn_half[0], attn_half[1], attn_half[2], attn_half[3], shared_...]
    all_to_all x3 -> x2, waiting for transfers between devices: 402 us -> 0.58 us  [the longest x1 0.58 us: on_device(): lax.all_to_all(own_gates.T, 'exp', split_axis=0, concat_axis=0, tiled=True)]
    pallas_call x0 -> x2, Pallas kernels: none -> 402 us  [the longest x1 221 us: experts(): pl.pallas_call(functools.partial(experts_kernel, n, slots), out_shape=(ou...]
    psum x1, waiting for transfers between devices: 0.01 us -> 245 us  [on_device(): lax.psum((attn_half[0], attn_half[1], attn_half[2], attn_half[3], shared_...]
    all_to_all x1 -> x0, blocking collectives: 234 us -> none  [on_device(): lax.all_to_all(send_grads, 'exp', split_axis=0, concat_axis=0, tiled=True)]
    dot_general x10 -> x4, matrix products: 98.1 us -> 10 us  [inner_cols(): lax.dot_general(left_side, right_side, contract_cols, preferred_element_t...]
    gather x4 -> x0, local copies, waits for them, and re-layouts: 64.7 us -> none  [the longest x1 21.9 us: on_device(): jnp.concatenate([grad_picked, zero_row], axis=0)[slot_assign]]
    dot_general x10 -> x4, matrix products: 63.3 us -> 11.4 us  [outer_rows(): lax.dot_general(left_side, right_side, contract_rows, preferred_element_t...]
  transfers between devices with their start and end apart: 20 -> 14, of which waited for: 8 -> 6; matrix products, arithmetic and copies ran while one was open for 18% -> 10% of each run, Pallas kernels for 0% -> 20%
where the time goes in v1:
time: 886 us; the launch traced here: 882 us
  Pallas kernels  402 us (45%)
  waiting for transfers between devices  275 us (31%)
  blocking collectives  45.6 us (5%)
  matrix products  44.3 us (5%)
  local copies, waits for them, and re-layouts  42.4 us (5%)
  other arithmetic  40.2 us (5%)
  starting transfers between devices  16.5 us (2%)
  between operations  15.9 us (2%)
    psum x1, waiting for transfers between devices, on_device(): lax.psum((attn_half[0], attn_half[1], attn_half[2], attn_half[3], shared_...  245 us
    pallas_call x1, Pallas kernels, experts(): pl.pallas_call(functools.partial(experts_kernel, n, slots), out_shape=(ou...  221 us
    pallas_call x1, Pallas kernels, gather_both(): pl.pallas_call(functools.partial(gather_kernel, n), out_shape=(jax.ShapeD...  180 us
    psum x1, blocking collectives, on_device(): small_sums = lax.psum((grad_one, grad_two, local_counts), ('exp', 'hid'))  45.6 us
    unnamed x121, local copies, waits for them, and re-layouts  34.5 us
  transfers between devices with their start and end apart: 14, of which 6 were waited for; matrix products, arithmetic and copies ran while one was open for 10% of the time, Pallas kernels for 20%

profile of v1, /device:TPU:0, one launch (start us, length us, event | category | flops | bytes accessed | tf_op | source)
XLA Modules:
  0.0 882.0 jit_solution(3143416070723327539)
XLA Ops:
  17.7 8.3 all-to-all-start
  34.1 3.8 fusion.33
  40.8 3.4 fusion.35
  45.3 2.5 copy.167
  47.9 2.6 copy.166
  50.5 4.0 subtract_convert_fusion.3
  54.8 3.0 convolution_convert_fusion.5
  58.8 2.7 fusion.40
  64.2 5.5 all-gather.17.cloned.1.call-done
  69.7 3.3 multiply_reduce_fusion.2
  75.1 180.2 %shard_map.288 = (bf16[16,256,1280]{2,1,0:T(8,128)(2,1)}, bf16[16,256,1280]{2,1,0:T(8,128)(2,1)}) custom-call(bf16[256,1280]{1,0:T(8,128)(2,1)} %x_ref.1, bf16[256,1280]{1,0:T(8,128)(2,1)} %multiply_convert_fusion.1.w_ref), custom_call_target="tpu_custom_call" | custom-call | tf_op jit(solution)/shard_map/pallas_call | solution.py:283
  255.3 221.3 %shard_map.289 = (f32[256,16]{1,0:T(8,128)}, f32[2,256,1280]{2,1,0:T(8,128)}, f32[1280,448]{1,0:T(8,128)}, f32[1280,448]{1,0:T(8,128)}, f32[448,1280]{1,0:T(8,12...) custom-call(bf16[16,256,1280]{2,1,0:T(8,128)(2,1)} %get-tuple-elemen, ...), custom_call_target="tpu_custom_call" | custom-call | tf_op jit(solution)/shard_map/pallas_call | solution.py:476
  476.7 2.9 fusion.17
  479.6 3.1 multiply_add_fusion
  483.7 2.7 convolution_convert_fusion
  486.7 4.2 convolution_convert_fusion.4
  491.0 2.2 copy.136
  496.4 2.9 convolution_convert_fusion.1
  499.4 2.1 multiply_reduce_fusion
  507.3 2.9 convolution_convert_fusion.2
  510.5 2.9 convolution_convert_fusion.3
  515.2 3.6 select_bitcast_fusion.2
  519.7 4.7 select_bitcast_fusion
  524.4 6.4 reduce-scatter.7.cloned.1.call-done
  530.8 15.2 %reduce-scatter.5.cloned.1.call-done = bf16[640,1280]{1,0:T(8,128)(2,1)} async-done(((bf16[1280,1280]{1,0:T(8,128)(2,1)}), bf16[640,1280]{1,0:T(8,128)(2,1)}) %reduce-scatter.5.cloned.1.call-update) | async-done | bytes 1638416 | tf_op jit(solution)/shard_map/reduce_scatter | solution.py:598
  547.6 7.0 all-to-all-start.1
  554.6 3.3 fusion.41
  563.2 3.1 copy.150
  566.3 2.0 copy.149
  568.5 45.6 %all-reduce = (f32[1280]{0:T(1024)}, f32[1280]{0:T(1024)}, f32[16]{0:T(128)S(1)}) all-reduce(f32[1280]{0:T(1024)S(1)} %get-tuple-element.153, f32[1280]{0:T(1024)S(1)} %copy-done.41, f32[16]{0:T(128)S(1)} %get-tuple-element.155), channel_id=1, replica_groups=mesh['exp'=16,'hid'=2] {'exp','hid'}, use_global_device_ids=true, to_apply=%region_11.12 | all-reduce | flops 2576 | bytes 20608 | tf_op jit(solution)/shard_map/psum | solution.py:625
  615.3 244.8 %all-reduce.4.cloned.1.call-done = (bf16[1280,448]{1,0:T(8,128)(2,1)}, bf16[1280,448]{1,0:T(8,128)(2,1)}, bf16[640,1280]{1,0:T(8,128)(2,1)}, bf16[640,1280]{1,0:...) async-done(((bf16[1280,448]{1,0:T(8,128)(2,1)}, bf16[1280,448]{1,0:T(8,128)(2,1)}, bf16[640,1280]{1,0:T(8,128)(2,1)}, ...) | async-done | bytes 9994256 | tf_op jit(solution)/shard_map/psum | solution.py:613
  860.1 2.8 copy.151
  (200 shorter events, 61.1 us)
Async XLA Ops:
  7.2 26.9 %all-gather.15.cloned.1.call-start = ((), (), s32[]{:S(2)}) async-start(), calls=%async_computation.8 | async-start | bytes 4915200 | tf_op jit(solution)/shard_map/all_gather | solution.py:526
  7.9 32.9 %all-gather.13.cloned.1.call-start = ((), (), s32[]{:S(2)}) async-start(), calls=%async_computation.7 | async-start | bytes 4915200 | tf_op jit(solution)/shard_map/all_gather | solution.py:525
  8.7 46.1 %all-gather.11.cloned.1.call-start = ((), (), s32[]{:S(2)}) async-start(), calls=%async_computation.6 | async-start | bytes 4915200 | tf_op jit(solution)/shard_map/all_gather | solution.py:527
  9.4 60.3 %all-gather.17.cloned.1.call-start = ((), (), s32[]{:S(2)}) async-start(), calls=%async_computation.9 | async-start | bytes 4915200 | tf_op jit(solution)/shard_map/all_gather | solution.py:528
  10.0 245.3 %all-gather.23.cloned.1.call-start = ((), (), s32[]{:S(2)}) async-start(), calls=%async_computation.16 | async-start | bytes 3440640 | tf_op jit(solution)/shard_map/all_gather | solution.py:556
  11.4 243.9 %all-gather.19.cloned.1.call-start = ((), (), s32[]{:S(2)}) async-start(), calls=%async_computation.14 | async-start | bytes 3932160 | tf_op jit(solution)/shard_map/all_gather | solution.py:556
  16.1 10.0 %copy-start.28 = (bf16[1,1280,448]{1,2,0:T(8,128)(2,1)S(1)}, bf16[1,1280,448]{1,2,0:T(8,128)(2,1)}, u32[]{:S(2)}) copy-start(bf16[1,1280,448]{1,2,0:T(8,128)(2,1)} %param.25) | copy-start | bytes 3440644
  16.9 9.2 %copy-start.47 = (f32[256]{0:T(256)}, f32[256]{0:T(256)S(1)}, u32[]{:S(2)}) copy-start(f32[256]{0:T(256)S(1)} %reduce_max.20) | copy-start | bytes 3076
  16.9 9.1 %copy-start.49 = (f32[256]{0:T(256)}, f32[256]{0:T(256)S(1)}, u32[]{:S(2)}) copy-start(f32[256]{0:T(256)S(1)} %fusion.29) | copy-start | bytes 3076
  16.9 9.1 %copy-start.51 = (f32[256]{0:T(256)}, f32[256]{0:T(256)S(1)}, u32[]{:S(2)}) copy-start(f32[256]{0:T(256)S(1)} %fusion.25) | copy-start | bytes 3076
  17.7 15.7 %all-to-all-start = ((f32[16,1,256]{2,1,0:T(1,128)}), f32[16,1,256]{2,1,0:T(1,128)S(1)}, u32[]{:S(2)}, u32[]{:S(2)}) async-start(f32[16,1,256]{2,1,0:T(1,128)} %copy.130), calls=%async_computation | async-start | bytes 32768 | tf_op jit(solution)/shard_map/all_to_all | solution.py:553
  26.1 229.2 %all-gather.21.cloned.1.call-start = ((), (), s32[]{:S(2)}) async-start(), calls=%async_computation.15 | async-start | bytes 3932160 | tf_op jit(solution)/shard_map/all_gather | solution.py:556
  29.5 4.6 copy-start.35
  29.6 494.8 %reduce-scatter.11.cloned.1.call-start = ((), (), s32[]{:S(2)}) async-start(), calls=%async_computation.13 | async-start | bytes 4915200 | tf_op jit(solution)/shard_map/reduce_scatter | solution.py:607
  32.8 22.0 %copy-start.44 = (f32[256]{0:T(256)}, f32[256]{0:T(256)S(1)}, u32[]{:S(2)}) copy-start(f32[256]{0:T(256)S(1)} %add_rsqrt_fusion.1) | copy-start | bytes 3076
  69.7 4.4 copy-start.39
  479.6 4.2 copy-start.20
  486.5 37.9 %reduce-scatter.9.cloned.1.call-start = ((), (), s32[]{:S(2)}) async-start(), calls=%async_computation.12 | async-start | bytes 4915200 | tf_op jit(solution)/shard_map/reduce_scatter | solution.py:604
  499.3 31.5 %reduce-scatter.7.cloned.1.call-start = ((), (), s32[]{:S(2)}) async-start(), calls=%async_computation.11 | async-start | bytes 4915200 | tf_op jit(solution)/shard_map/reduce_scatter | solution.py:601
  506.9 3.3 copy-start.5
  510.2 35.8 %reduce-scatter.5.cloned.1.call-start = ((), (), s32[]{:S(2)}) async-start(), calls=%async_computation.10 | async-start | bytes 4915200 | tf_op jit(solution)/shard_map/reduce_scatter | solution.py:598
  510.5 2.9 copy-start.14
  513.4 346.7 %all-reduce.4.cloned.1.call-start = ((), (), s32[]{:S(2)}) async-start(), calls=%async_computation.17 | async-start | bytes 20643840 | tf_op jit(solution)/shard_map/psum | solution.py:613
  515.2 3.6 copy-start.15
  515.2 3.6 copy-start.16
  515.2 4.5 copy-start.25
  547.6 20.8 %all-to-all-start.1 = ((f32[16,1,256]{2,1,0:T(1,128)}), f32[16,1,256]{2,1,0:T(1,128)S(1)}, u32[]{:S(2)}, u32[]{:S(2)}) async-start(f32[16,1,256]{2,1,0:T(1,128)} %copy.148), calls=%async_computation.5 | async-start | bytes 32768 | tf_op jit(solution)/shard_map/all_to_all | solution.py:562
  554.6 3.4 copy-start.6
  554.6 3.4 copy-start.11
  566.3 48.3 %copy-start.33 = (f32[256,7]{0,1:T(8,128)S(1)}, f32[256,7]{0,1:T(8,128)}, u32[]{:S(2)}) copy-start(f32[256,7]{0,1:T(8,128)} %param.30) | copy-start | bytes 21508
  566.3 48.3 %copy-start.48 = (f32[256]{0:T(256)S(1)}, f32[256]{0:T(256)}, u32[]{:S(2)}) copy-start(f32[256]{0:T(256)} %copy-done.47) | copy-start | bytes 3076
  566.3 48.3 %copy-start.52 = (f32[256]{0:T(256)S(1)}, f32[256]{0:T(256)}, u32[]{:S(2)}) copy-start(f32[256]{0:T(256)} %copy-done.51) | copy-start | bytes 3076
  (36 other events, 56.1 us)
Sparse Core Ops, SparseCore 0:
  9.6 15.0 all-gather.14
  26.2 13.4 all-gather.12
  41.2 13.4 all-gather.10
  56.2 13.4 all-gather.16
  71.6 12.0 all-gather.22
  85.7 12.5 all-gather.18
  100.4 12.5 all-gather.20
  486.6 14.0 reduce-scatter.10
  503.6 12.2 reduce-scatter.8
  518.5 12.2 reduce-scatter.6
  533.7 12.2 reduce-scatter.4
  552.8 307.2 all-reduce.3

commit v2 on v1

--- a/solution.py
+++ b/solution.py
@@ -79,69 +79,20 @@
 
 
 def attend_forward(queries, keys_all, values_all, seq_length):
-    total_rows = queries.shape[0]
-    step_rows = min(total_rows, block_rows)
     score_scale = queries.shape[-1] ** (-0.5)
-
-    def one_block(block_start):
-        scores = masked_scores(queries, keys_all, block_start, seq_length, score_scale)
-        top_val = jnp.max(scores, axis=-1, keepdims=True)
-        raised = jnp.exp(scores - top_val)
-        totals = jnp.sum(raised, axis=-1, keepdims=True)
-        attn_prob = (raised / totals).astype(jnp.bfloat16)
-        attended = jnp.einsum(
-            "hqk,khd->qhd", attn_prob, values_all, preferred_element_type=jnp.float32
-        )
-        return (attended, (top_val + jnp.log(totals))[..., 0])
-
-    starts = jnp.arange(total_rows // step_rows) * step_rows
-    attended, log_total = lax.map(one_block, starts)
-    return (attended.reshape(queries.shape), log_total)
-
-
-def attend_backward(queries, keys_all, values_all, seq_length, log_total, grad_out):
-    total_rows = queries.shape[0]
-    step_rows = min(total_rows, block_rows)
-    score_scale = queries.shape[-1] ** (-0.5)
-
-    def one_block(running, inputs):
-        grad_keys, grad_values = running
-        block_start, lse_block = inputs
-        scores = masked_scores(queries, keys_all, block_start, seq_length, score_scale)
-        attn_prob = jnp.exp(scores - lse_block[..., None])
-        grad_values = grad_values + jnp.einsum(
-            "hqk,qhd->khd",
-            attn_prob.astype(jnp.bfloat16),
-            grad_out,
-            preferred_element_type=jnp.float32,
-        )
-        grad_prob = jnp.einsum(
-            "qhd,khd->hqk", grad_out, values_all, preferred_element_type=jnp.float32
-        )
-        row_inner = jnp.sum(attn_prob * grad_prob, axis=-1, keepdims=True)
-        grad_scores = (attn_prob * (grad_prob - row_inner)).astype(jnp.bfloat16)
-        grad_query = (
-            jnp.einsum("hqk,khd->qhd", grad_scores, keys_all, preferred_element_type=jnp.float32)
-            * score_scale
-        )
-        grad_keys = (
-            grad_keys
-            + jnp.einsum("hqk,qhd->khd", grad_scores, queries, preferred_element_type=jnp.float32)
-            * score_scale
-        )
-        return ((grad_keys, grad_values), grad_query)
-
-    zero_grads = jnp.zeros(queries.shape, jnp.float32)
-    starts = jnp.arange(total_rows // step_rows) * step_rows
-    (grad_keys, grad_values), grad_query = lax.scan(
-        one_block, (zero_grads, zero_grads), (starts, log_total)
-    )
-    return (grad_query.reshape(queries.shape), grad_keys, grad_values)
+    scores = masked_scores(queries, keys_all, 0, seq_length, score_scale)
+    top_val = jnp.max(scores, axis=-1, keepdims=True)
+    raised = jnp.exp(scores - top_val)
+    attn_prob = raised / jnp.sum(raised, axis=-1, keepdims=True)
+    attended = jnp.einsum(
+        "hqk,khd->qhd", attn_prob.astype(jnp.bfloat16), values_all, preferred_element_type=jnp.float32
+    )
+    return (attended, attn_prob)
 
 
 class Place:
     def __init__(self, n):
-        self.nz = 4; self.m = {16: 2, 64: 4}[n]; m = self.m
+        self.n = n; self.nz = 4; self.m = {16: 2, 64: 4}[n]; m = self.m
         self.e = lax.axis_index("exp"); self.c = lax.axis_index("hid"); c = self.c; e = self.e
         self.s1 = m * m; self.s2 = 1 + c * (m - 1); self.s3 = m - c * (m - 1)
         self.c1 = e // self.s1; self.c2 = (e // self.s2) % m; self.c3 = (e // self.s3) % m
@@ -497,6 +448,359 @@
     )(h, dy, gates, wg, wu, wd)
 
 
+def swap_halves(values):
+    return pltpu.roll(values, HD // 2, axis=1)
+
+
+class Scatter:
+    def __init__(self, pc, stack, r3, r2, r1, sems):
+        self.pc, self.stack, self.r3, self.r2, self.r1 = pc, stack, r3, r2, r1
+        self.ssem, self.s3, self.s2, self.s1 = sems
+
+    def copy(self, b, dst, sem, to):
+        return pltpu.make_async_remote_copy(
+            src_ref=self.stack.at[b], dst_ref=dst, send_sem=self.ssem.at[b], recv_sem=sem,
+            device_id=(to, self.pc.c), device_id_type=MESH,
+        )
+
+    def add(self, total, src, sem):
+        self.copy(self.pc.e, src, sem, self.pc.blk(self.pc.c1, self.pc.c2, self.pc.o3()[0])).wait_recv()
+        return total + src[...].astype(jnp.float32)
+
+    def places(self):
+        pc = self.pc
+        far = [pc.c1 + j for j in range(1, pc.nz)] + [pc.c1]
+        return [a % pc.nz for a in far]
+
+    def start(self):
+        pc = self.pc
+        for k in range(1, pc.m):
+            for b2 in pc.o2() + [pc.c2]:
+                for a in self.places():
+                    b3 = (pc.c3 + k) % pc.m
+                    self.copy(pc.blk(a, b2, b3), self.r3.at[pc.m - k - 1, a, b2], self.s3.at[pc.m - k - 1, a, b2], pc.blk(pc.c1, pc.c2, b3)).start()
+
+    def collect(self, a, b2, level):
+        pc = self.pc
+        total = self.stack[pc.blk(a, b2, pc.c3)].astype(jnp.float32)
+        for k in range(pc.m - 1):
+            total = self.add(total, self.r3.at[k, a, b2], self.s3.at[k, a, b2])
+        if level >= 2:
+            for k in range(pc.m - 1):
+                total = self.add(total, self.r2.at[k, a], self.s2.at[k, a])
+        if level >= 3:
+            for k in range(pc.nz - 1):
+                total = self.add(total, self.r1.at[k], self.s1.at[k])
+        self.stack[pc.blk(a, b2, pc.c3)] = total.astype(jnp.bfloat16)
+
+    def second(self):
+        pc = self.pc
+        for k in range(1, pc.m):
+            for a in self.places():
+                b2 = (pc.c2 + k) % pc.m
+                self.collect(a, b2, 1)
+                self.copy(pc.blk(a, b2, pc.c3), self.r2.at[pc.m - k - 1, a], self.s2.at[pc.m - k - 1, a], pc.blk(pc.c1, b2, pc.c3)).start()
+
+    def third(self):
+        pc = self.pc
+        for k in range(1, pc.nz):
+            a = (pc.c1 + k) % pc.nz
+            self.collect(a, pc.c2, 2)
+            self.copy(pc.blk(a, pc.c2, pc.c3), self.r1.at[pc.nz - k - 1], self.s1.at[pc.nz - k - 1], pc.blk(a, pc.c2, pc.c3)).start()
+
+    def last(self):
+        self.collect(self.pc.c1, self.pc.c2, 3)
+
+    def finish(self):
+        pc = self.pc
+        for j in range(1, pc.n):
+            self.copy((pc.e + j) % pc.n, self.r1.at[0], self.s1.at[0], (pc.e + j) % pc.n).wait_send()
+
+
+def tail_kernel(
+    n,
+    x_ref, x1_ref, cot_ref, sums_ref, q_ref, k_ref, v_ref, o_ref, p_ref, wq, wk, wv, wo,
+    gain1, gain2, cos_ref, sin_ref, cnt_ref, sg_hbm, su_hbm, sd_hbm,
+    out_ref, gtok_ref, small_ref, ag0, ag1, agg, agu, agd,
+    dx_ref, dq_ref, dk_ref, dv_ref, do_ref, a_ref, give, take, stack0, stack1, r3, r2, r1,
+    sm_core, sm_d3, sm_d2, sm_z,
+    wbuf, wsem,
+    gs, gr, ss, s3, s2, s1, xs, xr, cs, cr, scs, scr, locs,
+):
+    pc = Place(n)
+    c1, c2, c3, e, c, nz, m = pc.c1, pc.c2, pc.c3, pc.e, pc.c, pc.nz, pc.m
+    rows, width = x_ref.shape
+    half = width // 2
+    barrier = pltpu.get_barrier_semaphore()
+
+    def greet(j, carry):
+        pl.semaphore_signal(barrier, inc=1, device_id=((e + j) % n, c), device_id_type=MESH)
+        return carry
+
+    lax.fori_loop(1, n, greet, 0)
+    pl.semaphore_signal(barrier, inc=1, device_id=(e, 1 - c), device_id_type=MESH)
+    pl.semaphore_wait(barrier, n)
+
+    shared = ((sg_hbm, agg), (su_hbm, agu), (sd_hbm, agd))
+
+    def deal(i, to):
+        src, dst = shared[i]
+        return pltpu.make_async_remote_copy(
+            src_ref=src.at[to], dst_ref=dst.at[to], send_sem=scs.at[i, to], recv_sem=scr.at[i],
+            device_id=(to, c), device_id_type=MESH,
+        )
+
+    def keep(i):
+        src, dst = shared[i]
+        return pltpu.make_async_copy(src.at[n - 1], dst.at[n - 1], scs.at[i, n - 1])
+
+    @pl.when(e == n - 1)
+    def _():
+        def one(j, carry):
+            for i in range(3):
+                deal(i, n - 2 - j).start()
+            return carry
+
+        lax.fori_loop(0, n - 1, one, 0)
+        for i in range(3):
+            keep(i).start()
+
+    gathers = [Gather(pc, dst.at[e], dst, gs.at[i], gr.at[i], dst.shape[1]) for i, (src, dst) in enumerate(shared)]
+
+    def shared_start():
+        @pl.when(e == n - 1)
+        def _():
+            for i in range(3):
+                keep(i).wait()
+
+        @pl.when(e != n - 1)
+        def _():
+            for i in range(3):
+                src, dst = shared[i]
+                pltpu.make_async_remote_copy(
+                    src_ref=dst.at[e], dst_ref=dst.at[e], send_sem=scs.at[i, 0], recv_sem=scr.at[i],
+                    device_id=(n - 1, c), device_id_type=MESH,
+                ).wait_recv()
+
+        for g in gathers:
+            g.start()
+
+    def fetch(src, i):
+        return pltpu.make_async_copy(src, wbuf.at[i], wsem.at[i])
+
+    fetch(wo, 0).start()
+    fetch(wv, 1).start()
+
+    x1 = x1_ref[...]
+    up = cot_ref[...].astype(jnp.float32)
+    out_ref[...] = (x1 + sums_ref[0]).astype(jnp.bfloat16)
+    dh = sums_ref[1]
+    r_two = lax.rsqrt(jnp.mean(x1 * x1, axis=-1, keepdims=True) + norm_eps)
+    n_two = x1 * r_two
+    scaled = dh * gain2[...]
+    grad_two = jnp.sum(dh * n_two, axis=0, keepdims=True)
+    dx = up + r_two * (scaled - n_two * jnp.mean(scaled * n_two, axis=-1, keepdims=True))
+    dx_ref[...] = dx
+    dx_low = dx.astype(jnp.bfloat16)
+
+    def columns(ref, which):
+        return ref[:, pl.ds(pl.multiple_of(which * half, 128), half)]
+
+    def hand(i):
+        return pltpu.make_async_remote_copy(
+            src_ref=give.at[i], dst_ref=take.at[i], send_sem=xs.at[i], recv_sem=xr.at[i],
+            device_id=(e, 1 - c), device_id_type=MESH,
+        )
+
+    def to_partner(i, left, right):
+        give[i] = outer_rows(columns(left, 1 - c), right).astype(jnp.bfloat16)
+        hand(i).start()
+
+    def own_part(i, left, right, stack, at):
+        block = stack.shape[1]
+        part = outer_rows(columns(left, c), right)
+        hand(i).wait_recv()
+        total = (part + take[i].astype(jnp.float32)).astype(jnp.bfloat16)
+        stack[pl.ds(at * (half // block), half // block)] = total.reshape(half // block, block, width)
+
+    to_partner(0, o_ref, dx_low)
+    fetch(wo, 0).wait()
+    do_ref[...] = inner_cols(dx_low, wbuf[0]).astype(jnp.bfloat16)
+    fetch(wk, 0).start()
+    cosine, sine = cos_ref[...], sin_ref[...]
+    scale = HD ** (-0.5)
+
+    def one_head(hd, carry):
+        at = pl.ds(pl.multiple_of(hd * HD, HD), HD)
+        prob = p_ref[hd]
+        d_o, val, que, key = do_ref[:, at], v_ref[:, at], q_ref[:, at], k_ref[:, at]
+        dv_ref[:, at] = outer_rows(prob.astype(jnp.bfloat16), d_o).astype(jnp.bfloat16)
+        d_prob = inner_cols(d_o, val)
+        inner = jnp.sum(prob * d_prob, axis=-1, keepdims=True)
+        d_score = (prob * (d_prob - inner)).astype(jnp.bfloat16)
+        d_q = matmul(d_score, key) * scale
+        d_k = outer_rows(d_score, que) * scale
+        dq_ref[:, at] = (d_q * cosine - swap_halves(d_q) * sine).astype(jnp.bfloat16)
+        dk_ref[:, at] = (d_k * cosine - swap_halves(d_k) * sine).astype(jnp.bfloat16)
+        return carry
+
+    lax.fori_loop(0, HEADS, one_head, 0)
+    xv = x_ref[...].astype(jnp.float32)
+    r_one = lax.rsqrt(jnp.mean(xv * xv, axis=-1, keepdims=True) + norm_eps)
+    n_one = xv * r_one
+    a_ref[...] = (n_one * gain1[...]).astype(jnp.bfloat16)
+    to_partner(1, a_ref, dv_ref[...])
+    to_partner(2, a_ref, dk_ref[...])
+    to_partner(3, a_ref, dq_ref[...])
+    if n * stack0.shape[1] > 2 * half:
+        stack0[...] = jnp.zeros_like(stack0)
+        stack1[...] = jnp.zeros_like(stack1)
+    own_part(0, o_ref, dx_low, stack0, 0)
+    own_part(1, a_ref, dv_ref[...], stack0, 1)
+    first = Scatter(pc, stack0, r3.at[0], r2.at[0], r1.at[0], (ss.at[0], s3.at[0], s2.at[0], s1.at[0]))
+    second = Scatter(pc, stack1, r3.at[1], r2.at[1], r1.at[1], (ss.at[1], s3.at[1], s2.at[1], s1.at[1]))
+    first.start()
+    shared_start()
+    own_part(2, a_ref, dk_ref[...], stack1, 0)
+    own_part(3, a_ref, dq_ref[...], stack1, 1)
+    second.start()
+    fetch(wv, 1).wait()
+    da = inner_cols(dv_ref[...], wbuf[1])
+    fetch(wq, 1).start()
+    fetch(wk, 0).wait()
+    da = da + inner_cols(dk_ref[...], wbuf[0])
+    fetch(wq, 1).wait()
+    da = da + inner_cols(dq_ref[...], wbuf[1])
+    scaled_one = da * gain1[...]
+    grad_one = jnp.sum(da * n_one, axis=0, keepdims=True)
+    back = r_one * (scaled_one - n_one * jnp.mean(scaled_one * n_one, axis=-1, keepdims=True))
+    gtok_ref[...] = (dx_ref[...] + back).astype(jnp.bfloat16)
+
+    def exchange(ref, own, level, peers, value):
+        ref[own] = value
+        copies = [
+            pltpu.make_async_remote_copy(
+                src_ref=ref.at[own], dst_ref=ref.at[own], send_sem=cs.at[level, i], recv_sem=cr.at[level, own],
+                device_id=to, device_id_type=MESH,
+            )
+            for i, (to, at) in enumerate(peers)
+        ]
+        for copy in copies:
+            copy.start()
+
+        def done():
+            for i, (to, at) in enumerate(peers):
+                pltpu.make_async_remote_copy(
+                    src_ref=ref.at[own], dst_ref=ref.at[at], send_sem=cs.at[level, i], recv_sem=cr.at[level, at],
+                    device_id=to, device_id_type=MESH,
+                ).wait_recv()
+            for copy in copies:
+                copy.wait_send()
+            total = ref[0]
+            for i in range(1, ref.shape[0]):
+                total = total + ref[i]
+            return total
+
+        return done
+
+    small = jnp.concatenate([grad_one, grad_two, cnt_ref[...], jnp.zeros((5, width), jnp.float32)], axis=0)
+    level0 = exchange(sm_core, c, 0, [((e, 1 - c), 1 - c)], small)
+    first.second()
+    level1 = exchange(sm_d3, c3, 1, [((pc.blk(c1, c2, j), c), j) for j in pc.o3()], level0())
+    second.second()
+    level2 = exchange(sm_d2, c2, 2, [((pc.blk(c1, j, c3), c), j) for j in pc.o2()], level1())
+    first.third()
+    level3 = exchange(sm_z, c1, 3, [((pc.blk((c1 + j) % nz, c2, c3), c), (c1 + j) % nz) for j in range(1, nz)], level2())
+    second.third()
+    small_ref[...] = level3()
+
+    events = [g.events() for g in gathers]
+    for i in range(len(events[0])):
+        for ev in events:
+            ev[i]()
+    first.last()
+    g0 = Gather(pc, stack0.at[e], ag0, gs.at[3], gr.at[3], stack0.shape[1])
+    g0.start()
+    loc0 = pltpu.make_async_copy(stack0.at[e], ag0.at[e], locs.at[0])
+    loc0.start()
+    second.last()
+    g1 = Gather(pc, stack1.at[e], ag1, gs.at[4], gr.at[4], stack1.shape[1])
+    g1.start()
+    loc1 = pltpu.make_async_copy(stack1.at[e], ag1.at[e], locs.at[1])
+    loc1.start()
+    ev0, ev1 = g0.events(), g1.events()
+    for i in range(len(ev0)):
+        ev0[i]()
+        ev1[i]()
+    for g in gathers + [g0, g1]:
+        g.finish()
+    first.finish()
+    second.finish()
+    loc0.wait()
+    loc1.wait()
+    for i in range(4):
+        hand(i).wait_send()
+
+    @pl.when(e == n - 1)
+    def _():
+        def one(j, carry):
+            for i in range(3):
+                deal(i, j).wait_send()
+            return carry
+
+        lax.fori_loop(0, n - 1, one, 0)
+
+
+def tail(n, x, x1, cot, sums, q, k, v, o, prob, wq, wk, wv, wo, gain1, gain2, cosine, sine, cnt, sg, su, sd):
+    nz = 4
+    m = {16: 2, 64: 4}[n]
+    rows, width = x.shape
+    half = width // 2
+    block = blocked(2 * half, n)
+    vmem = pl.BlockSpec(memory_space=pltpu.VMEM)
+    hbm = pl.BlockSpec(memory_space=pl.ANY)
+    f32, b16 = jnp.float32, jnp.bfloat16
+    out = jax.ShapeDtypeStruct
+    dma = pltpu.SemaphoreType.DMA
+    wide = pltpu.VMEM((rows, width), b16)
+    return pl.pallas_call(
+        functools.partial(tail_kernel, n),
+        out_shape=(
+            out((rows, width), b16), out((rows, width), b16), out((8, width), f32),
+            out((n, block, width), b16), out((n, block, width), b16),
+            out(sg.shape, b16), out(su.shape, b16), out(sd.shape, b16),
+        ),
+        in_specs=[vmem] * 9 + [hbm] * 4 + [vmem] * 5 + [hbm] * 3,
+        out_specs=(vmem, vmem, vmem) + (hbm,) * 5,
+        scratch_shapes=[
+            pltpu.VMEM((rows, width), f32), wide, wide, wide, wide, wide,
+            pltpu.VMEM((4, half, width), b16), pltpu.VMEM((4, half, width), b16),
+            pltpu.VMEM((n, block, width), b16), pltpu.VMEM((n, block, width), b16),
+            pltpu.VMEM((2, m - 1, nz, m, block, width), b16), pltpu.VMEM((2, m - 1, nz, block, width), b16),
+            pltpu.VMEM((2, nz - 1, block, width), b16),
+            pltpu.VMEM((2, 8, width), f32), pltpu.VMEM((m, 8, width), f32), pltpu.VMEM((m, 8, width), f32), pltpu.VMEM((nz, 8, width), f32),
+            pltpu.VMEM((2, width, width), b16), dma((2,)),
+            dma((5, 160)), dma((5, 1, n)), dma((2, n)), dma((2, m - 1, nz, m)), dma((2, m - 1, nz)), dma((2, nz - 1)),
+            dma((4,)), dma((4,)), dma((4, max(nz, m))), dma((4, max(nz, m, 2))), dma((3, n)), dma((3,)), dma((2,)),
+        ],
+        compiler_params=pltpu.CompilerParams(collective_id=2, has_side_effects=True, vmem_limit_bytes=62 * 2**20),
+    )(x, x1, cot, sums, q, k, v, o, prob, wq, wk, wv, wo, gain1, gain2, cosine, sine, cnt, sg, su, sd)
+
+
+def blocked(count, n):
+    return -(-count // (16 * n)) * 16
+
+
+def to_blocks(values, n):
+    block = blocked(values.shape[0], n)
+    padded = jnp.pad(values.astype(jnp.bfloat16), ((0, n * block - values.shape[0]), (0, 0)))
+    return padded.reshape(n, block, values.shape[1])
+
+
+def from_blocks(blocks, count):
+    return blocks.reshape(-1, blocks.shape[2])[:count].astype(jnp.float32)
+
+
 def on_device(
     tokens,
     norm_one,
@@ -538,7 +842,7 @@
         matmul(attn_in, full_key).reshape(heads_shape), cosine_table, sine_table
     ).astype(jnp.bfloat16)
     values_all = matmul(attn_in, full_value).reshape(heads_shape).astype(jnp.bfloat16)
-    attended, log_total = attend_forward(queries, keys_all, values_all, seq_length)
+    attended, attn_prob = attend_forward(queries, keys_all, values_all, seq_length)
     attended_low = attended.reshape(seq_len, width).astype(jnp.bfloat16)
     mixed = inputs_full + matmul(attended_low, full_out)
     normed_two, scale_two = rms_parts(mixed)
@@ -560,87 +864,42 @@
     scores_e, sums, gg, gu, gd, pg, pu, pd = experts(all_h, all_dy, gates, wg, wu, wd)[:8]
     slot_grads = (gg + pg.astype(jnp.float32), gu + pu.astype(jnp.float32), gd + pd.astype(jnp.float32))
     scores = lax.all_to_all(scores_e.T, "exp", split_axis=0, concat_axis=0, tiled=True).T
-    output = mixed + sums[0]
-    upstream = cotangent.astype(jnp.float32)
     grad_share = jnp.sum(onehot * scores[:, None, :], axis=-1) * token_valid[:, None]
     grad_logits = soft_gates * (
         grad_share - jnp.sum(soft_gates * grad_share, axis=-1, keepdims=True)
     )
-    grad_hidden = sums[1]
-    grad_norm_in, grad_two = rms_back(normed_two, scale_two, norm_two, grad_hidden)
-    grad_mixed = upstream + grad_norm_in
-    grad_mixed_low = grad_mixed.astype(jnp.bfloat16)
-    grad_wout = outer_rows(attended_low, grad_mixed_low)
-    grad_attended = inner_cols(grad_mixed_low, full_out).astype(jnp.bfloat16).reshape(heads_shape)
-    grad_query_rot, grad_key_rot, grad_value_all = attend_backward(
-        queries, keys_all, values_all, seq_length, log_total, grad_attended
-    )
-    grad_query_pre = (
-        rotate(grad_query_rot, cosine_table, -sine_table)
-        .reshape(seq_len, width)
-        .astype(jnp.bfloat16)
-    )
-    grad_key_pre = (
-        rotate(grad_key_rot, cosine_table, -sine_table).reshape(seq_len, width).astype(jnp.bfloat16)
-    )
-    grad_value_pre = grad_value_all.reshape(seq_len, width).astype(jnp.bfloat16)
-    grad_wquery = outer_rows(attn_in, grad_query_pre)
-    grad_wkey = outer_rows(attn_in, grad_key_pre)
-    grad_wvalue = outer_rows(attn_in, grad_value_pre)
-    grad_attn_in = (
-        inner_cols(grad_query_pre, full_query)
-        + inner_cols(grad_key_pre, full_key)
-        + inner_cols(grad_value_pre, full_value)
-    )
-    grad_in_one, grad_one = rms_back(normed_one, scale_one, norm_one, grad_attn_in)
-    grad_tokens = (grad_mixed + grad_in_one).astype(jnp.bfloat16)
-    attn_half = (
-        lax.psum_scatter(
-            grad_wquery.astype(jnp.bfloat16), "hid", scatter_dimension=0, tiled=True
-        ),
-        lax.psum_scatter(
-            grad_wkey.astype(jnp.bfloat16), "hid", scatter_dimension=0, tiled=True
-        ),
-        lax.psum_scatter(
-            grad_wvalue.astype(jnp.bfloat16), "hid", scatter_dimension=0, tiled=True
-        ),
-        lax.psum_scatter(
-            grad_wout.astype(jnp.bfloat16), "hid", scatter_dimension=0, tiled=True
-        ),
-    )
-    shared_grads = tuple(jnp.where(holds_shared, grad, 0.0).astype(jnp.bfloat16) for grad in slot_grads)
+    flat = (seq_len, width)
+    cosine = jnp.tile(cosine_table[:, 0], (1, 2))
+    sine = jnp.concatenate([-sine_table[:, 0], sine_table[:, 0]], axis=1)
+    count_row = jnp.pad(local_counts[None], ((0, 0), (0, width - slot_count)))
+    output, grad_tokens, small_sums, sum0, sum1, sum_g, sum_u, sum_d = tail(
+        slot_count, tokens, mixed, cotangent, sums, queries.reshape(flat), keys_all.reshape(flat),
+        values_all.reshape(flat), attended_low, attn_prob, full_query, full_key, full_value, full_out,
+        norm_one[None], norm_two[None], cosine, sine, count_row,
+        to_blocks(slot_grads[0], slot_count), to_blocks(slot_grads[1], slot_count), to_blocks(slot_grads[2], slot_count),
+    )
+    half = width // 2
+    wout_value = from_blocks(sum0, width)
+    key_query = from_blocks(sum1, width)
+    hidden = s_gate.shape[1]
     routed_grads = tuple(jnp.where(holds_shared, 0.0, grad)[None] for grad in slot_grads)
-    summed = lax.psum(
-        (
-            attn_half[0],
-            attn_half[1],
-            attn_half[2],
-            attn_half[3],
-            shared_grads[0],
-            shared_grads[1],
-            shared_grads[2],
-        ),
-        "exp",
-    )
-    small_sums = lax.psum((grad_one, grad_two, local_counts), ("exp", "hid"))
-    counts = small_sums[2].astype(jnp.int32)
     return (
-        output.astype(jnp.bfloat16),
+        output,
         grad_tokens,
         small_sums[0],
-        summed[0].astype(jnp.float32),
-        summed[1].astype(jnp.float32),
-        summed[2].astype(jnp.float32),
-        summed[3].astype(jnp.float32),
+        key_query[half:],
+        key_query[:half],
+        wout_value[half:],
+        wout_value[:half],
         small_sums[1],
         routed_grads[0],
         routed_grads[1],
         routed_grads[2],
-        summed[4].astype(jnp.float32),
-        summed[5].astype(jnp.float32),
-        summed[6].astype(jnp.float32),
+        from_blocks(sum_g, width),
+        from_blocks(sum_u, width),
+        from_blocks(sum_d, hidden),
         grad_logits,
-        counts,
+        small_sums[2, :slot_count].astype(jnp.int32),
     )
 
 

time: 886 us -> 776 us (0.88)
  waiting for transfers between devices: 275 us -> 11 us
  Pallas kernels: 402 us -> 621 us
  blocking collectives: 45.6 us -> 0 us
  matrix products: 44.3 us -> 16.1 us
  local copies, waits for them, and re-layouts: 42.4 us -> 61.5 us
  other arithmetic: 40.2 us -> 27.5 us
    psum x1 -> x0, waiting for transfers between devices: 245 us -> none  [on_device(): lax.psum((attn_half[0], attn_half[1], attn_half[2], attn_half[3], shared_...]
    pallas_call x0 -> x1, Pallas kernels: none -> 220 us  [tail(): pl.pallas_call(functools.partial(tail_kernel, n), out_shape=(out((rows, w...]
    psum x1 -> x0, blocking collectives: 45.6 us -> none  [on_device(): small_sums = lax.psum((grad_one, grad_two, local_counts), ('exp', 'hid'))]
    dot_general x14 -> x1, matrix products: 30.8 us -> 0.56 us  [attend_forward(): jnp.einsum('hqk,khd->qhd', attn_prob.astype(jnp.bfloat16), values_all, pr...]
    reduce_scatter x4 -> x0, waiting for transfers between devices: 21.6 us -> none  [the longest x1 15.2 us: on_device(): lax.psum_scatter(grad_wquery.astype(jnp.bfloat16), 'hid', scatter_dimensi...]
    slice x0 -> x4, local copies, waits for them, and re-layouts: none -> 9.74 us  [the longest x1 3.46 us: on_device(): wout_value[:half]]
    unnamed x121 -> x79, local copies, waits for them, and re-layouts: 34.5 us -> 30.9 us
  transfers between devices with their start and end apart: 14 -> 9, of which waited for: 6 -> 1; matrix products, arithmetic and copies ran while one was open for 10% -> 9% of each run, Pallas kernels for 20% -> 23%
where the time goes in v2:
time: 776 us; the launch traced here: 770 us
  Pallas kernels  621 us (80%)
  local copies, waits for them, and re-layouts  61.5 us (8%)
  other arithmetic  27.5 us (4%)
  starting transfers between devices  17.2 us (2%)
  matrix products  16.1 us (2%)
  between operations  15.6 us (2%)
  waiting for transfers between devices  11 us (1%)
    pallas_call x1, Pallas kernels, experts(): pl.pallas_call(functools.partial(experts_kernel, n, slots), out_shape=(ou...  222 us
    pallas_call x1, Pallas kernels, tail(): pl.pallas_call(functools.partial(tail_kernel, n), out_shape=(out((rows, w...  220 us
    pallas_call x1, Pallas kernels, gather_both(): pl.pallas_call(functools.partial(gather_kernel, n), out_shape=(jax.ShapeD...  180 us
    unnamed x79, local copies, waits for them, and re-layouts  30.9 us
  transfers between devices with their start and end apart: 9, of which 1 were waited for; matrix products, arithmetic and copies ran while one was open for 9% of the time, Pallas kernels for 23%

profile of v2, /device:TPU:0, one launch (start us, length us, event | category | flops | bytes accessed | tf_op | source)
XLA Modules:
  0.0 770.3 jit_solution(18257109846078930978)
XLA Ops:
  18.8 8.4 %all-to-all-start = ((f32[16,1,256]{2,1,0:T(1,128)}), f32[16,1,256]{2,1,0:T(1,128)}, u32[]{:S(2)}, u32[]{:S(2)}) async-start(f32[16,1,256]{2,1,0:T(1,128)} %copy.113), calls=%async_computation | async-start | bytes 32768 | tf_op jit(solution)/shard_map/all_to_all | solution.py:857
  27.9 1.8 copy.118
  37.7 3.0 convolution_convert_fusion.v_ref
  41.8 3.4 fusion.23
  46.5 8.3 %all-gather.15.cloned.1.call-done.wk = bf16[1280,1280]{1,0:T(8,128)(2,1)} async-done(((bf16[640,1280]{1,0:T(8,128)(2,1)}), bf16[1280,1280]{1,0:T(8,128)(2,1)}) %all-gather.15.cloned.1.call-update) | async-done | bytes 3276816 | tf_op jit(solution)/shard_map/all_gather | solution.py:830
  54.8 3.4 fusion.21
  60.8 2.6 copy.137
  63.4 2.6 copy.135
  66.0 2.8 multiply_subtract_fusion
  68.8 1.8 maximum_convert_fusion
  70.6 2.5 fusion.30
  75.7 3.3 multiply_reduce_fusion
  81.0 180.2 %shard_map.288 = (bf16[16,256,1280]{2,1,0:T(8,128)(2,1)}, bf16[16,256,1280]{2,1,0:T(8,128)(2,1)}) custom-call(bf16[256,1280]{1,0:T(8,128)(2,1)} %cot_ref.1, bf16[256,1280]{1,0:T(8,128)(2,1)} %multiply_convert_fusion.w_ref), custom_call_target="tpu_custom_call" | custom-call | tf_op jit(solution)/shard_map/pallas_call | solution.py:234
  261.3 221.6 %shard_map.289 = (f32[256,16]{1,0:T(8,128)}, f32[2,256,1280]{2,1,0:T(8,128)}, f32[1280,448]{1,0:T(8,128)}, f32[1280,448]{1,0:T(8,128)}, f32[448,1280]{1,0:T(8,12...) custom-call(bf16[16,256,1280]{2,1,0:T(8,128)(2,1)} %get-tuple-elemen, ...), custom_call_target="tpu_custom_call" | custom-call | tf_op jit(solution)/shard_map/pallas_call | solution.py:427
  482.9 1.6 copy.126
  484.5 8.6 %all-to-all-start.1 = ((f32[16,1,256]{2,1,0:T(1,128)}), f32[16,1,256]{2,1,0:T(1,128)S(1)}, u32[]{:S(2)}, u32[]{:S(2)}) async-start(f32[16,1,256]{2,1,0:T(1,128)} %copy.126), calls=%async_computation.1 | async-start | bytes 32768 | tf_op jit(solution)/shard_map/all_to_all | solution.py:866
  493.1 3.9 select_bitcast_fusion.1
  497.0 2.5 select_bitcast_fusion
  500.1 2.0 select_bitcast_fusion.2
  503.4 2.2 copy.120
  505.6 2.2 copy.124.o_ref
  508.8 2.2 copy.123.k_ref
  511.0 3.1 copy.128
  514.1 2.0 copy.127
  516.1 2.4 pad.9
  519.3 219.6 %shard_map.290 = (bf16[256,1280]{1,0:T(8,128)(2,1)}, bf16[256,1280]{1,0:T(8,128)(2,1)}, f32[8,1280]{1,0:T(8,128)}, bf16[16,80,1280]{2,1,0:T(8,128)(2,1)}, bf16[1...) custom-call(bf16[256,1280]{1,0:T(8,128)(2,1)} %x_ref.3, ...), custom_call_target="tpu_custom_call" | custom-call | tf_op jit(solution)/shard_map/pallas_call | solution.py:766
  743.6 1.6 bitcast_convert_fusion.2
  745.7 2.0 copy.129
  747.7 3.2 bitcast_convert_fusion
  750.9 3.3 copy.130
  754.1 3.5 fusion.27
  757.6 3.5 fusion.26
  (136 shorter events, 40.0 us)
Async XLA Ops:
  7.2 30.5 %all-gather.11.cloned.1.call-start = ((), (), s32[]{:S(2)}) async-start(), calls=%async_computation.2 | async-start | bytes 4915200 | tf_op jit(solution)/shard_map/all_gather | solution.py:831
  7.9 33.8 %all-gather.13.cloned.1.call-start = ((), (), s32[]{:S(2)}) async-start(), calls=%async_computation.3 | async-start | bytes 4915200 | tf_op jit(solution)/shard_map/all_gather | solution.py:829
  8.7 1.6 copy-start.16
  8.7 46.1 %all-gather.15.cloned.1.call-start = ((), (), s32[]{:S(2)}) async-start(), calls=%async_computation.4 | async-start | bytes 4915200 | tf_op jit(solution)/shard_map/all_gather | solution.py:830
  9.4 66.2 %all-gather.17.cloned.1.call-start = ((), (), s32[]{:S(2)}) async-start(), calls=%async_computation.5 | async-start | bytes 4915200 | tf_op jit(solution)/shard_map/all_gather | solution.py:832
  10.0 251.2 %all-gather.23.cloned.1.call-start = ((), (), s32[]{:S(2)}) async-start(), calls=%async_computation.8 | async-start | bytes 3440640 | tf_op jit(solution)/shard_map/all_gather | solution.py:860
  11.4 249.8 %all-gather.19.cloned.1.call-start = ((), (), s32[]{:S(2)}) async-start(), calls=%async_computation.6 | async-start | bytes 3932160 | tf_op jit(solution)/shard_map/all_gather | solution.py:860
  16.1 2.0 copy-start.22
  16.1 11.2 %copy-start.14 = (bf16[1,1280,448]{1,2,0:T(8,128)(2,1)S(1)}, bf16[1,1280,448]{1,2,0:T(8,128)(2,1)}, u32[]{:S(2)}) copy-start(bf16[1,1280,448]{1,2,0:T(8,128)(2,1)} %param.25) | copy-start | bytes 3440644
  18.8 17.4 %all-to-all-start = ((f32[16,1,256]{2,1,0:T(1,128)}), f32[16,1,256]{2,1,0:T(1,128)}, u32[]{:S(2)}, u32[]{:S(2)}) async-start(f32[16,1,256]{2,1,0:T(1,128)} %copy.113), calls=%async_computation | async-start | bytes 32768 | tf_op jit(solution)/shard_map/all_to_all | solution.py:857
  27.2 234.1 %all-gather.21.cloned.1.call-start = ((), (), s32[]{:S(2)}) async-start(), calls=%async_computation.7 | async-start | bytes 3932160 | tf_op jit(solution)/shard_map/all_gather | solution.py:860
  30.9 3.3 copy-start.21
  30.9 3.9 copy-start.30
  32.2 9.6 %copy-start.31 = (f32[256]{0:T(256)}, f32[256]{0:T(256)S(1)}, u32[]{:S(2)}) copy-start(f32[256]{0:T(256)S(1)} %add_rsqrt_fusion.1) | copy-start | bytes 3076
  40.7 4.5 copy-start.5
  68.8 1.8 copy-start.20
  73.1 1.9 copy-start.8
  73.6 1.5 copy-start
  75.6 3.3 copy-start.7
  484.5 34.0 %all-to-all-start.1 = ((f32[16,1,256]{2,1,0:T(1,128)}), f32[16,1,256]{2,1,0:T(1,128)S(1)}, u32[]{:S(2)}, u32[]{:S(2)}) async-start(f32[16,1,256]{2,1,0:T(1,128)} %copy.126), calls=%async_computation.1 | async-start | bytes 32768 | tf_op jit(solution)/shard_map/all_to_all | solution.py:866
  493.1 3.9 copy-start.6
  493.1 3.9 copy-start.11
  497.0 2.5 copy-start.9
  497.0 3.1 copy-start.12
  516.1 2.4 copy-start.23
  516.1 2.4 copy-start.27
  519.3 222.3 %copy-start.25 = (f32[256]{0:T(256)S(1)}, f32[256]{0:T(256)}, u32[]{:S(2)}) copy-start(f32[256]{0:T(256)} %copy-done.24) | copy-start | bytes 3076
  519.3 222.3 %copy-start.29 = (f32[256]{0:T(256)S(1)}, f32[256]{0:T(256)}, u32[]{:S(2)}) copy-start(f32[256]{0:T(256)} %copy-done.28) | copy-start | bytes 3076
  743.6 1.7 copy-start.10
  750.9 3.3 copy-start.2
  754.1 3.5 copy-start.1
  757.6 3.5 copy-start.18
  (9 other events, 8.6 us)
Sparse Core Ops, SparseCore 0:
  9.6 15.0 all-gather.10
  26.2 13.5 all-gather.12
  41.3 13.4 all-gather.14
  56.2 13.4 all-gather.16
  71.6 12.0 all-gather.22
  85.7 12.5 all-gather.18
  100.3 12.5 all-gather.20

commit v3 on v2

--- a/solution.py
+++ b/solution.py
@@ -2,6 +2,7 @@
 
 import jax
 import jax.numpy as jnp
+import numpy as np
 from jax import lax
 from jax.experimental import pallas as pl
 from jax.experimental.pallas import tpu as pltpu
@@ -14,7 +15,6 @@
 
 norm_eps = 1e-06
 rotary_base = 10000.0
-block_rows = 512
 contract_rows = (((0,), (0,)), ((), ()))
 contract_cols = (((1,), (1,)), ((), ()))
 
@@ -29,65 +29,6 @@
 
 def inner_cols(left_side, right_side):
     return lax.dot_general(left_side, right_side, contract_cols, preferred_element_type=jnp.float32)
-
-
-def rms_parts(values):
-    inv_rms = lax.rsqrt(jnp.mean(values * values, axis=-1, keepdims=True) + norm_eps)
-    return (values * inv_rms, inv_rms)
-
-
-def rms_back(normed, inv_rms, norm_gain, upstream):
-    gain_grad = jnp.sum(upstream * normed, axis=0)
-    scaled_up = upstream * norm_gain
-    return (
-        inv_rms * (scaled_up - normed * jnp.mean(scaled_up * normed, axis=-1, keepdims=True)),
-        gain_grad,
-    )
-
-
-def rotary_tables(seq_len, head_size):
-    position = jnp.arange(seq_len).astype(jnp.float32)
-    inverse_freq = rotary_base ** (
-        -2.0 * jnp.arange(head_size // 2).astype(jnp.float32) / head_size
-    )
-    angle_grid = position[:, None] * inverse_freq[None, :]
-    return (jnp.cos(angle_grid)[:, None, :], jnp.sin(angle_grid)[:, None, :])
-
-
-def rotate(values, cosine_table, sine_table):
-    half_width = values.shape[-1] // 2
-    first_half = values[..., :half_width]
-    second_half = values[..., half_width:]
-    return jnp.concatenate(
-        [
-            first_half * cosine_table - second_half * sine_table,
-            second_half * cosine_table + first_half * sine_table,
-        ],
-        axis=-1,
-    )
-
-
-def masked_scores(query_blk, keys_all, block_start, seq_length, score_scale):
-    scores = (
-        jnp.einsum("qhd,khd->hqk", query_blk, keys_all, preferred_element_type=jnp.float32)
-        * score_scale
-    )
-    row_pos = block_start + jnp.arange(query_blk.shape[0])[:, None]
-    col_pos = jnp.arange(keys_all.shape[0])[None, :]
-    allowed = (col_pos <= row_pos) & (col_pos < seq_length)
-    return jnp.where(allowed[None], scores, -1e30)
-
-
-def attend_forward(queries, keys_all, values_all, seq_length):
-    score_scale = queries.shape[-1] ** (-0.5)
-    scores = masked_scores(queries, keys_all, 0, seq_length, score_scale)
-    top_val = jnp.max(scores, axis=-1, keepdims=True)
-    raised = jnp.exp(scores - top_val)
-    attn_prob = raised / jnp.sum(raised, axis=-1, keepdims=True)
-    attended = jnp.einsum(
-        "hqk,khd->qhd", attn_prob.astype(jnp.bfloat16), values_all, preferred_element_type=jnp.float32
-    )
-    return (attended, attn_prob)
 
 
 class Place:
@@ -99,14 +40,17 @@
     def blk(self, a, b, d): return a * self.s1 + b * self.s2 + d * self.s3
     def o2(self): return [(self.c2 + j) % self.m for j in range(1, self.m)]
     def o3(self): return [(self.c3 + j) % self.m for j in range(1, self.m)]
-    def enter(self):
-        bar = pltpu.get_barrier_semaphore()
-        c1, c2, c3 = self.c1, self.c2, self.c3
-        def sig(p): pl.semaphore_signal(bar, inc=1, device_id=(p, self.c), device_id_type=MESH)
-        for j in self.o2(): sig(self.blk(c1, j, c3))
-        for j in self.o3(): sig(self.blk(c1, c2, j))
-        for j in range(1, self.nz): sig(self.blk((c1 + j) % self.nz, c2, c3))
-        pl.semaphore_wait(bar, 2 * (self.m - 1) + self.nz - 1)
+    def greet_all(self):
+        barrier = pltpu.get_barrier_semaphore()
+
+        def greet(j, carry):
+            pl.semaphore_signal(barrier, inc=1, device_id=((self.e + j) % self.n, self.c), device_id_type=MESH)
+            return carry
+
+        lax.fori_loop(1, self.n, greet, 0)
+        pl.semaphore_signal(barrier, inc=1, device_id=(self.e, 1 - self.c), device_id_type=MESH)
+        pl.semaphore_wait(barrier, self.n)
+
 
 class Gather:
     def __init__(self, pc, src, dst, ssem, rsem, split, base=0):
@@ -124,7 +68,8 @@
         else: pl.when(cond)(cp.start)
     def wait(self, part, b):
         v = self.view(self.dst.at[b], part)
-        pltpu.make_async_copy(v, v, self.rsem.at[part, b]).wait()
+        to = self.pc.blk(self.pc.c1, self.pc.c2, self.pc.o3()[0])
+        pltpu.make_async_remote_copy(src_ref=v, dst_ref=v, send_sem=self.ssem.at[0], recv_sem=self.rsem.at[part, b], device_id=(to, self.pc.c), device_id_type=MESH).wait_recv()
     def updown(self, part, own, b):
         pc = self.pc
         self.send(part, own, b, pc.blk(pc.c1 + 1, pc.c2, pc.c3), pc.c1 < pc.nz - 1)
@@ -206,68 +151,219 @@
             else: pl.when(cond)(cp.wait_send)
 
 
-def gather_kernel(n, x_ref, w_ref, ox_ref, ow_ref, ssem, rsem, lsem):
+def run_staggered(first, second, lag):
+    for i in range(max(len(first), len(second) + lag)):
+        if i < len(first):
+            first[i]()
+        if lag <= i < len(second) + lag:
+            second[i - lag]()
+
+
+def part_rows(rows):
+    return rows
+
+
+def front_kernel(
+    n,
+    x_ref, cot_hbm, gain1, gain2, cos_ref, sin_ref, len_ref, logit_ref, route_ref,
+    wq, wk, wv, wo, rg, ru, rd, sg, su, sd,
+    all_dy, all_h, fq, fk, fv, fo, fg, fu, fd,
+    x1_ref, q_ref, k_ref, v_ref, o_ref, p_ref, gates_in, cnt_ref,
+    wbuf, h_ref, rows_out,
+    gs, gr, ls, ws, wr, wl, es, er, el, gss, grs,
+):
     pc = Place(n)
-    pc.enter()
-    rows = x_ref.shape[0]
-    first = Gather(pc, x_ref, ox_ref, ssem.at[0], rsem.at[0], rows)
-    second = Gather(pc, w_ref, ow_ref, ssem.at[1], rsem.at[1], rows)
-    first.start()
-    second.start()
-    own_x = pltpu.make_async_copy(x_ref, ox_ref.at[pc.e], lsem.at[0])
-    own_w = pltpu.make_async_copy(w_ref, ow_ref.at[pc.e], lsem.at[1])
-    own_x.start()
-    own_w.start()
-    for event in first.events():
-        event()
-    for event in second.events():
-        event()
-    first.finish()
-    second.finish()
-    own_x.wait()
-    own_w.wait()
-
-
-def gather_both(x, w):
-    n = lax.axis_size("exp")
-    any_spec = pl.BlockSpec(memory_space=pl.ANY)
+    e, c = pc.e, pc.c
+    rows, width = x_ref.shape
+    half = width // 2
+    pc.greet_all()
+    gather_dy = Gather(pc, cot_hbm, all_dy, gs.at[0], gr.at[0], part_rows(rows))
+    gather_h = Gather(pc, h_ref, all_h, gs.at[1], gr.at[1], part_rows(rows))
+    gather_dy.start()
+    own_dy = pltpu.make_async_copy(cot_hbm, all_dy.at[e], ls.at[0])
+    own_dy.start()
+    partner = (e, 1 - c)
+    halves = (wq, wk, wv, wo)
+    fulls = (fq, fk, fv, fo)
+
+    def swap(i):
+        return pltpu.make_async_remote_copy(
+            src_ref=halves[i], dst_ref=wbuf.at[i, c], send_sem=ws.at[i], recv_sem=wr.at[i],
+            device_id=partner, device_id_type=MESH,
+        )
+
+    def own(i):
+        return pltpu.make_async_copy(halves[i], wbuf.at[i, c], wl.at[0, i])
+
+    def keep(i):
+        return pltpu.make_async_copy(wbuf.at[i], fulls[i], wl.at[1, i])
+
+    experts_full = (fg, fu, fd)
+
+    def expert_swap(i, src):
+        return pltpu.make_async_remote_copy(
+            src_ref=src, dst_ref=experts_full[i].at[c], send_sem=es.at[i], recv_sem=er.at[i],
+            device_id=partner, device_id_type=MESH,
+        )
+
+    def expert_own(i, src):
+        return pltpu.make_async_copy(src, experts_full[i].at[c], el.at[i])
+
+    for i in range(4):
+        swap(i).start()
+        own(i).start()
+    for i, (routed, shared) in enumerate(((rg, sg), (ru, su), (rd, sd))):
+        @pl.when(e == n - 1)
+        def _():
+            expert_swap(i, shared).start()
+            expert_own(i, shared).start()
+
+        @pl.when(e != n - 1)
+        def _():
+            expert_swap(i, routed).start()
+            expert_own(i, routed).start()
+
+    lane = lax.broadcasted_iota(jnp.int32, (rows, 128), 1)
+    row = lax.broadcasted_iota(jnp.int32, (rows, 128), 0)
+    valid = (row < len_ref[...]).astype(jnp.float32)
+    logits = logit_ref[...]
+    raised = jnp.exp(logits - jnp.max(logits, axis=-1, keepdims=True))
+    soft = raised / jnp.sum(raised, axis=-1, keepdims=True)
+    routes = route_ref[...]
+    dense = jnp.zeros((rows, 128), jnp.float32)
+    named = jnp.zeros((rows, 128), jnp.float32)
+    for i in range(routes.shape[1]):
+        hit = lane == routes[:, i : i + 1]
+        dense = dense + jnp.where(hit, soft[:, i : i + 1], 0.0)
+        named = named + jnp.where(hit, 1.0, 0.0)
+    dense = jnp.where(lane == n - 1, 1.0, dense * valid)
+    cnt_ref[...] = jnp.zeros_like(cnt_ref)
+    cnt_ref[:, 0:128] = jnp.sum(named * valid, axis=0, keepdims=True)
+    turned = dense.T
+    for i in range(n):
+        rows_out[i] = turned[i : i + 1, :]
+    gates_in[e] = rows_out[e]
+
+    def gate_send(to):
+        return pltpu.make_async_remote_copy(
+            src_ref=rows_out.at[to], dst_ref=gates_in.at[e], send_sem=gss.at[to], recv_sem=grs.at[e],
+            device_id=(to, c), device_id_type=MESH,
+        )
+
+    def gate_start(j, carry):
+        gate_send((e + j) % n).start()
+        return carry
+
+    lax.fori_loop(1, n, gate_start, 0)
+
+    xv = x_ref[...].astype(jnp.float32)
+    a = (xv * lax.rsqrt(jnp.mean(xv * xv, axis=-1, keepdims=True) + norm_eps) * gain1[...]).astype(jnp.bfloat16)
+    cosine, sine = cos_ref[...], sin_ref[...]
+
+    def project(values, i):
+        own(i).wait()
+        swap(i).wait_recv()
+        keep(i).start()
+        return matmul(values[:, :half], wbuf[i, 0]) + matmul(values[:, half:], wbuf[i, 1])
+
+    for i, ref in ((0, q_ref), (1, k_ref)):
+        flat = project(a, i)
+        for hd in range(HEADS):
+            part = flat[:, hd * HD : (hd + 1) * HD]
+            ref[:, hd * HD : (hd + 1) * HD] = (part * cosine + swap_halves(part) * sine).astype(jnp.bfloat16)
+    v_ref[...] = project(a, 2).astype(jnp.bfloat16)
+    events = gather_dy.events()
+    events[0]()
+    scale = HD ** (-0.5)
+    row_pos = lax.broadcasted_iota(jnp.int32, (rows, rows), 0)
+    col_pos = lax.broadcasted_iota(jnp.int32, (rows, rows), 1)
+    length = jnp.concatenate([len_ref[...]] * (rows // 128), axis=1)
+    allowed = (col_pos <= row_pos) & (col_pos < length)
+
+    def one_head(hd, carry):
+        at = pl.ds(pl.multiple_of(hd * HD, HD), HD)
+        scores = jnp.where(allowed, inner_cols(q_ref[:, at], k_ref[:, at]) * scale, -1e30)
+        up = jnp.exp(scores - jnp.max(scores, axis=-1, keepdims=True))
+        prob = up / jnp.sum(up, axis=-1, keepdims=True)
+        p_ref[hd] = prob
+        o_ref[:, at] = matmul(prob.astype(jnp.bfloat16), v_ref[:, at]).astype(jnp.bfloat16)
+        return carry
+
+    lax.fori_loop(0, HEADS, one_head, 0)
+    events[1]()
+    x1 = xv + project(o_ref[...], 3)
+    x1_ref[...] = x1
+    h_ref[...] = (x1 * lax.rsqrt(jnp.mean(x1 * x1, axis=-1, keepdims=True) + norm_eps) * gain2[...]).astype(jnp.bfloat16)
+    gather_h.start()
+    own_h = pltpu.make_async_copy(h_ref, all_h.at[e], ls.at[1])
+    own_h.start()
+    run_staggered(events[2:], gather_h.events(), 2)
+
+    def gate_wait(j, carry):
+        pltpu.make_async_remote_copy(
+            src_ref=rows_out.at[0], dst_ref=gates_in.at[(e + j) % n], send_sem=gss.at[0], recv_sem=grs.at[(e + j) % n],
+            device_id=((e + j) % n, c), device_id_type=MESH,
+        ).wait_recv()
+        gate_send((e + j) % n).wait_send()
+        return carry
+
+    lax.fori_loop(1, n, gate_wait, 0)
+    gather_dy.finish()
+    gather_h.finish()
+    own_dy.wait()
+    own_h.wait()
+    for i in range(4):
+        swap(i).wait_send()
+        keep(i).wait()
+    for i, shared in enumerate((sg, su, sd)):
+        expert_swap(i, shared).wait()
+        expert_own(i, shared).wait()
+
+
+def front(n, x, cot, gain1, gain2, cosine, sine, length, logits, routes, attn_w, routed_w, shared_w):
+    rows, width = x.shape
+    hidden = shared_w[0].shape[1]
+    vmem = pl.BlockSpec(memory_space=pltpu.VMEM)
+    hbm = pl.BlockSpec(memory_space=pl.ANY)
+    f32, b16 = jnp.float32, jnp.bfloat16
+    out = jax.ShapeDtypeStruct
+    dma = pltpu.SemaphoreType.DMA
+    wide = out((rows, width), b16)
+    full = out((2, width // 2, width), b16)
     return pl.pallas_call(
-        functools.partial(gather_kernel, n),
-        out_shape=(jax.ShapeDtypeStruct((n,) + x.shape, x.dtype), jax.ShapeDtypeStruct((n,) + w.shape, w.dtype)),
-        in_specs=[any_spec, any_spec],
-        out_specs=(any_spec, any_spec),
+        functools.partial(front_kernel, n),
+        out_shape=(
+            out((n, rows, width), b16), out((n, rows, width), b16), full, full, full, full,
+            out((2, width, hidden), b16), out((2, width, hidden), b16), out((2, hidden, width), b16),
+            out((rows, width), f32), wide, wide, wide, wide, out((HEADS, rows, rows), f32),
+            out((n, 1, rows), f32), out((1, width), f32),
+        ),
+        in_specs=[vmem, hbm] + [vmem] * 7 + [hbm] * 10,
+        out_specs=(hbm,) * 9 + (vmem,) * 8,
         scratch_shapes=[
-            pltpu.SemaphoreType.DMA((2, 128)),
-            pltpu.SemaphoreType.DMA((2, 2, n)),
-            pltpu.SemaphoreType.DMA((2,)),
+            pltpu.VMEM((4, 2, width // 2, width), b16), pltpu.VMEM((rows, width), b16), pltpu.VMEM((n, 1, rows), f32),
+            dma((2, 160)), dma((2, 2, n)), dma((2,)), dma((4,)), dma((4,)), dma((2, 4)), dma((3,)), dma((3,)), dma((3,)),
+            dma((n,)), dma((n,)),
         ],
-        compiler_params=pltpu.CompilerParams(collective_id=0, has_side_effects=True),
-    )(x, w)
+        compiler_params=pltpu.CompilerParams(collective_id=0, has_side_effects=True, vmem_limit_bytes=56 * 2**20),
+    )(x, cot, gain1, gain2, cosine, sine, length, logits, routes, *attn_w, *routed_w, *shared_w)
 
 
 def experts_kernel(
     n, slots,
-    h_hbm, dy_hbm, gate_ref, wg, wu, wd,
-    s_ref, sums_hbm, gg_hbm, gu_hbm, gd_hbm, pg_hbm, pu_hbm, pd_hbm, r3_hbm, r2_hbm, r1_hbm,
-    og, ou, od, ysum, hbuf, dbuf, act, dg, dup, stage, rbuf, xg, xu, xd,
-    lsem, ssem, r3sem, r2sem, r1sem, bsem, xssem, xrsem, osem,
+    h_hbm, dy_hbm, gates_in, wg, wu, wd,
+    scores_in, sums_hbm, tg_hbm, tu_hbm, td_hbm, bg_hbm, bu_hbm, bd_hbm, r3_hbm, r2_hbm, r1_hbm,
+    og, ou, od, ysum, hbuf, dbuf, act, dg, dup, stage, rbuf, xg, xu, xd, pg, pu, pd, gate_ref, s_ref, turn_ref, rows_out,
+    lsem, ssem, r3sem, r2sem, r1sem, bsem, xssem, xrsem, osem, psem, scs, scr,
 ):
     pc = Place(n)
     nz, m = pc.nz, pc.m
     c1, c2, c3, e, c = pc.c1, pc.c2, pc.c3, pc.e, pc.c
-    barrier = pltpu.get_barrier_semaphore()
-
-    def greet(to, core):
-        pl.semaphore_signal(barrier, inc=1, device_id=(to, core), device_id_type=MESH)
-
-    for j in range(1, m):
-        greet(pc.blk(c1, c2, (c3 + j) % m), c)
-        greet(pc.blk(c1, (c2 + j) % m, c3), c)
-    for j in range(1, nz):
-        greet(pc.blk((c1 + j) % nz, c2, c3), c)
-    greet(e, 1 - c)
-    pl.semaphore_wait(barrier, 2 * (m - 1) + nz)
-
+    pc.greet_all()
+    turn_ref[...] = jnp.zeros_like(turn_ref)
+    for i in range(n):
+        turn_ref[i : i + 1, :] = gates_in[i]
+    gate_ref[...] = turn_ref[...].T
     og[...] = jnp.zeros_like(og)
     ou[...] = jnp.zeros_like(ou)
     od[...] = jnp.zeros_like(od)
@@ -307,14 +403,26 @@
                 src_ref=src, dst_ref=dst, send_sem=xssem.at[i], recv_sem=xrsem.at[i],
                 device_id=(e, 1 - c), device_id_type=MESH,
             )
-            for i, (src, dst) in enumerate(((xg, pg_hbm), (xu, pu_hbm), (xd, pd_hbm)))
+            for i, (src, dst) in enumerate(((xg, pg), (xu, pu), (xd, pd)))
         ]
 
-    def own_halves():
+    def totals():
         return [
             pltpu.make_async_copy(src.at[c], dst, osem.at[i])
-            for i, (src, dst) in enumerate(((og, gg_hbm), (ou, gu_hbm), (od, gd_hbm)))
+            for i, (src, dst) in enumerate(((og, tg_hbm), (ou, tu_hbm), (od, td_hbm)))
         ]
+
+    def payload():
+        return [
+            pltpu.make_async_copy(src, dst.at[pl.ds(0, src.shape[0])], psem.at[i])
+            for i, (src, dst) in enumerate(((xg, bg_hbm), (xu, bu_hbm), (xd, bd_hbm)))
+        ]
+
+    def score_send(to):
+        return pltpu.make_async_remote_copy(
+            src_ref=rows_out.at[to], dst_ref=scores_in.at[e], send_sem=scs.at[to], recv_sem=scr.at[e],
+            device_id=(to, c), device_id_type=MESH,
+        )
 
     for copy in load(0, 0):
         copy.start()
@@ -394,12 +502,26 @@
         return carry
 
     lax.fori_loop(0, n, body, 0)
-    xg[...] = og[1 - c].astype(jnp.bfloat16)
-    xu[...] = ou[1 - c].astype(jnp.bfloat16)
-    xd[...] = od[1 - c].astype(jnp.bfloat16)
+    for buf, total in ((xg, og), (xu, ou), (xd, od)):
+        buf[...] = total[1 - c].astype(jnp.bfloat16)
     for copy in swaps():
         copy.start()
-    for copy in own_halves():
+    turned = s_ref[...].T
+    for i in range(n):
+        rows_out[i] = turned[i : i + 1, :]
+    scores_in[e] = rows_out[e]
+
+    def score_start(j, carry):
+        score_send((e + j) % n).start()
+        return carry
+
+    lax.fori_loop(1, n, score_start, 0)
+    for copy in swaps():
+        copy.wait()
+    for buf, got, total in ((xg, pg, og), (xu, pu, ou), (xd, pd, od)):
+        total[c] += got[...].astype(jnp.float32)
+        buf[...] = total[c].astype(jnp.bfloat16)
+    for copy in totals() + payload():
         copy.start()
     for j in range(1, nz):
         add_received(r1_hbm.at[j - 1], r1sem.at[j - 1])
@@ -408,9 +530,17 @@
     final.wait()
     for t in range(max(0, n - slots), n - 1):
         partial_copy(t % slots, e, r1_hbm.at[0], r1sem.at[0]).wait_send()
-    for copy in swaps():
-        copy.wait()
-    for copy in own_halves():
+
+    def score_wait(j, carry):
+        pltpu.make_async_remote_copy(
+            src_ref=rows_out.at[0], dst_ref=scores_in.at[(e + j) % n], send_sem=scs.at[0], recv_sem=scr.at[(e + j) % n],
+            device_id=((e + j) % n, c), device_id_type=MESH,
+        ).wait_recv()
+        score_send((e + j) % n).wait_send()
+        return carry
+
+    lax.fori_loop(1, n, score_wait, 0)
+    for copy in totals() + payload():
         copy.wait()
 
 
@@ -424,12 +554,14 @@
     hbm = pl.BlockSpec(memory_space=pl.ANY)
     f32, b16 = jnp.float32, jnp.bfloat16
     out = jax.ShapeDtypeStruct
+    dma = pltpu.SemaphoreType.DMA
+    up_rows, down_rows = n * blocked(width, n), n * blocked(hidden, n)
     return pl.pallas_call(
         functools.partial(experts_kernel, n, slots),
         out_shape=(
-            out((rows, n), f32), out((2, rows, width), f32),
+            out((n, 1, rows), f32), out((2, rows, width), f32),
             out((width, hidden), f32), out((width, hidden), f32), out((hidden, width), f32),
-            out((width, hidden), b16), out((width, hidden), b16), out((hidden, width), b16),
+            out((up_rows, hidden), b16), out((up_rows, hidden), b16), out((down_rows, width), b16),
             out((m - 1, nz, m, 2, rows, width), b16), out((m - 1, nz, 2, rows, width), b16), out((nz - 1, 2, rows, width), b16),
         ),
         in_specs=[hbm, hbm, vmem, vmem, vmem, vmem],
@@ -440,11 +572,12 @@
             pltpu.VMEM((2, rows, hidden), b16), pltpu.VMEM((2, rows, hidden), b16), pltpu.VMEM((2, rows, hidden), b16),
             pltpu.VMEM((slots, 2, rows, width), b16), pltpu.VMEM((2, rows, width), b16),
             pltpu.VMEM((width, hidden), b16), pltpu.VMEM((width, hidden), b16), pltpu.VMEM((hidden, width), b16),
-            pltpu.SemaphoreType.DMA((2, 2)), pltpu.SemaphoreType.DMA((slots,)),
-            pltpu.SemaphoreType.DMA((m - 1, nz, m)), pltpu.SemaphoreType.DMA((m - 1, nz)), pltpu.SemaphoreType.DMA((nz - 1,)),
-            pltpu.SemaphoreType.DMA, pltpu.SemaphoreType.DMA((3,)), pltpu.SemaphoreType.DMA((3,)), pltpu.SemaphoreType.DMA((3,)),
+            pltpu.VMEM((width, hidden), b16), pltpu.VMEM((width, hidden), b16), pltpu.VMEM((hidden, width), b16),
+            pltpu.VMEM((rows, 128), f32), pltpu.VMEM((rows, 128), f32), pltpu.VMEM((128, rows), f32), pltpu.VMEM((n, 1, rows), f32),
+            dma((2, 2)), dma((slots,)), dma((m - 1, nz, m)), dma((m - 1, nz)), dma((nz - 1,)), dma,
+            dma((3,)), dma((3,)), dma((3,)), dma((3,)), dma((n,)), dma((n,)),
         ],
-        compiler_params=pltpu.CompilerParams(collective_id=1, has_side_effects=True, vmem_limit_bytes=60 * 2**20),
+        compiler_params=pltpu.CompilerParams(collective_id=1, has_side_effects=True, vmem_limit_bytes=62 * 2**20),
     )(h, dy, gates, wg, wu, wd)
 
 
@@ -520,26 +653,18 @@
 def tail_kernel(
     n,
     x_ref, x1_ref, cot_ref, sums_ref, q_ref, k_ref, v_ref, o_ref, p_ref, wq, wk, wv, wo,
-    gain1, gain2, cos_ref, sin_ref, cnt_ref, sg_hbm, su_hbm, sd_hbm,
-    out_ref, gtok_ref, small_ref, ag0, ag1, agg, agu, agd,
+    gain1, gain2, cos_ref, sin_ref, cnt_ref, len_ref, logit_ref, route_ref, scores_in, sg_hbm, su_hbm, sd_hbm,
+    out_ref, gtok_ref, glog_ref, small_ref, ag0, ag1, agg, agu, agd,
     dx_ref, dq_ref, dk_ref, dv_ref, do_ref, a_ref, give, take, stack0, stack1, r3, r2, r1,
     sm_core, sm_d3, sm_d2, sm_z,
-    wbuf, wsem,
+    wbuf, wsem, turn_ref,
     gs, gr, ss, s3, s2, s1, xs, xr, cs, cr, scs, scr, locs,
 ):
     pc = Place(n)
     c1, c2, c3, e, c, nz, m = pc.c1, pc.c2, pc.c3, pc.e, pc.c, pc.nz, pc.m
     rows, width = x_ref.shape
     half = width // 2
-    barrier = pltpu.get_barrier_semaphore()
-
-    def greet(j, carry):
-        pl.semaphore_signal(barrier, inc=1, device_id=((e + j) % n, c), device_id_type=MESH)
-        return carry
-
-    lax.fori_loop(1, n, greet, 0)
-    pl.semaphore_signal(barrier, inc=1, device_id=(e, 1 - c), device_id_type=MESH)
-    pl.semaphore_wait(barrier, n)
+    pc.greet_all()
 
     shared = ((sg_hbm, agg), (su_hbm, agu), (sd_hbm, agd))
 
@@ -703,6 +828,23 @@
 
         return done
 
+    turn_ref[...] = jnp.zeros_like(turn_ref)
+    for i in range(n):
+        turn_ref[i : i + 1, :] = scores_in[i]
+    scores = turn_ref[...].T
+    lane = lax.broadcasted_iota(jnp.int32, (rows, 128), 1)
+    row = lax.broadcasted_iota(jnp.int32, (rows, 128), 0)
+    scores = jnp.where(row < len_ref[...], scores, 0.0)
+    logits, routes = logit_ref[...], route_ref[...]
+    raised = jnp.exp(logits - jnp.max(logits, axis=-1, keepdims=True))
+    soft = raised / jnp.sum(raised, axis=-1, keepdims=True)
+    picked = [
+        jnp.sum(jnp.where(lane == routes[:, i : i + 1], scores, 0.0), axis=-1, keepdims=True)
+        for i in range(routes.shape[1])
+    ]
+    share = jnp.concatenate(picked, axis=1)
+    glog_ref[...] = soft * (share - jnp.sum(soft * share, axis=-1, keepdims=True))
+
     small = jnp.concatenate([grad_one, grad_two, cnt_ref[...], jnp.zeros((5, width), jnp.float32)], axis=0)
     level0 = exchange(sm_core, c, 0, [((e, 1 - c), 1 - c)], small)
     first.second()
@@ -751,7 +893,7 @@
         lax.fori_loop(0, n - 1, one, 0)
 
 
-def tail(n, x, x1, cot, sums, q, k, v, o, prob, wq, wk, wv, wo, gain1, gain2, cosine, sine, cnt, sg, su, sd):
+def tail(n, x, x1, cot, sums, q, k, v, o, prob, wq, wk, wv, wo, gain1, gain2, cosine, sine, cnt, length, logits, routes, scores, sg, su, sd):
     nz = 4
     m = {16: 2, 64: 4}[n]
     rows, width = x.shape
@@ -766,12 +908,12 @@
     return pl.pallas_call(
         functools.partial(tail_kernel, n),
         out_shape=(
-            out((rows, width), b16), out((rows, width), b16), out((8, width), f32),
+            out((rows, width), b16), out((rows, width), b16), out(logits.shape, f32), out((8, width), f32),
             out((n, block, width), b16), out((n, block, width), b16),
             out(sg.shape, b16), out(su.shape, b16), out(sd.shape, b16),
         ),
-        in_specs=[vmem] * 9 + [hbm] * 4 + [vmem] * 5 + [hbm] * 3,
-        out_specs=(vmem, vmem, vmem) + (hbm,) * 5,
+        in_specs=[vmem] * 9 + [hbm] * 4 + [vmem] * 9 + [hbm] * 3,
+        out_specs=(vmem,) * 4 + (hbm,) * 5,
         scratch_shapes=[
             pltpu.VMEM((rows, width), f32), wide, wide, wide, wide, wide,
             pltpu.VMEM((4, half, width), b16), pltpu.VMEM((4, half, width), b16),
@@ -779,127 +921,65 @@
             pltpu.VMEM((2, m - 1, nz, m, block, width), b16), pltpu.VMEM((2, m - 1, nz, block, width), b16),
             pltpu.VMEM((2, nz - 1, block, width), b16),
             pltpu.VMEM((2, 8, width), f32), pltpu.VMEM((m, 8, width), f32), pltpu.VMEM((m, 8, width), f32), pltpu.VMEM((nz, 8, width), f32),
-            pltpu.VMEM((2, width, width), b16), dma((2,)),
+            pltpu.VMEM((2, width, width), b16), dma((2,)), pltpu.VMEM((128, rows), f32),
             dma((5, 160)), dma((5, 1, n)), dma((2, n)), dma((2, m - 1, nz, m)), dma((2, m - 1, nz)), dma((2, nz - 1)),
             dma((4,)), dma((4,)), dma((4, max(nz, m))), dma((4, max(nz, m, 2))), dma((3, n)), dma((3,)), dma((2,)),
         ],
         compiler_params=pltpu.CompilerParams(collective_id=2, has_side_effects=True, vmem_limit_bytes=62 * 2**20),
-    )(x, x1, cot, sums, q, k, v, o, prob, wq, wk, wv, wo, gain1, gain2, cosine, sine, cnt, sg, su, sd)
+    )(x, x1, cot, sums, q, k, v, o, prob, wq, wk, wv, wo, gain1, gain2, cosine, sine, cnt, length, logits, routes, scores, sg, su, sd)
 
 
 def blocked(count, n):
     return -(-count // (16 * n)) * 16
 
 
-def to_blocks(values, n):
-    block = blocked(values.shape[0], n)
-    padded = jnp.pad(values.astype(jnp.bfloat16), ((0, n * block - values.shape[0]), (0, 0)))
-    return padded.reshape(n, block, values.shape[1])
-
-
 def from_blocks(blocks, count):
     return blocks.reshape(-1, blocks.shape[2])[:count].astype(jnp.float32)
 
 
+def rotary_rows(seq_len):
+    position = np.arange(seq_len).astype(np.float32)
+    inverse_freq = (rotary_base ** (-2.0 * np.arange(HD // 2).astype(np.float32) / HD)).astype(np.float32)
+    angle = position[:, None] * inverse_freq[None, :]
+    cosine, sine = np.cos(angle), np.sin(angle)
+    return np.concatenate([cosine, cosine], axis=1), np.concatenate([-sine, sine], axis=1)
+
+
 def on_device(
-    tokens,
-    norm_one,
-    w_query,
-    w_key,
-    w_value,
-    w_out,
-    norm_two,
-    r_gate,
-    r_up,
-    r_down,
-    s_gate,
-    s_up,
-    s_down,
-    logits,
-    routes,
-    lengths,
-    cotangent,
+    tokens, norm_one, w_query, w_key, w_value, w_out, norm_two, r_gate, r_up, r_down, s_gate, s_up, s_down,
+    logits, routes, lengths, cotangent,
 ):
-    seq_len = tokens.shape[0]
-    width = tokens.shape[1]
-    slot_count = lax.axis_size("exp")
-    seq_length = lengths[0]
-    inputs_full = tokens.astype(jnp.float32)
-    full_query, full_key, full_value, full_out = (
-        lax.all_gather(w_query, "hid", axis=0, tiled=True),
-        lax.all_gather(w_key, "hid", axis=0, tiled=True),
-        lax.all_gather(w_value, "hid", axis=0, tiled=True),
-        lax.all_gather(w_out, "hid", axis=0, tiled=True),
+    rows, width = tokens.shape
+    n = lax.axis_size("exp")
+    hidden = s_gate.shape[1]
+    cosine, sine = (jnp.asarray(table) for table in rotary_rows(rows))
+    length = jnp.broadcast_to(lengths[:, None], (1, 128))
+    gain1, gain2 = norm_one[None], norm_two[None]
+    (
+        all_dy, all_h, fq, fk, fv, fo, fg, fu, fd, mixed, queries, keys_all, values_all, attended, prob, gates, counts,
+    ) = front(
+        n, tokens, cotangent, gain1, gain2, cosine, sine, length, logits, routes,
+        (w_query, w_key, w_value, w_out), (r_gate[0], r_up[0], r_down[0]), (s_gate, s_up, s_down),
     )
-    normed_one, scale_one = rms_parts(inputs_full)
-    attn_in = (normed_one * norm_one).astype(jnp.bfloat16)
-    cosine_table, sine_table = rotary_tables(seq_len, HD)
-    heads_shape = (seq_len, HEADS, HD)
-    queries = rotate(
-        matmul(attn_in, full_query).reshape(heads_shape), cosine_table, sine_table
-    ).astype(jnp.bfloat16)
-    keys_all = rotate(
-        matmul(attn_in, full_key).reshape(heads_shape), cosine_table, sine_table
-    ).astype(jnp.bfloat16)
-    values_all = matmul(attn_in, full_value).reshape(heads_shape).astype(jnp.bfloat16)
-    attended, attn_prob = attend_forward(queries, keys_all, values_all, seq_length)
-    attended_low = attended.reshape(seq_len, width).astype(jnp.bfloat16)
-    mixed = inputs_full + matmul(attended_low, full_out)
-    normed_two, scale_two = rms_parts(mixed)
-    hidden_in = (normed_two * norm_two).astype(jnp.bfloat16)
-    onehot = (routes[:, :, None] == jnp.arange(slot_count)[None, None, :]).astype(jnp.float32)
-    token_valid = (jnp.arange(seq_len) < seq_length).astype(jnp.float32)
-    soft_gates = jax.nn.softmax(logits, axis=-1)
-    gate_share = soft_gates * token_valid[:, None]
-    local_counts = jnp.sum(onehot * token_valid[:, None, None], axis=(0, 1))
-    is_last = jnp.arange(slot_count) == slot_count - 1
-    own_gates = jnp.where(is_last[None, :], 1.0, jnp.sum(onehot * gate_share[:, :, None], axis=1))
-    gates = lax.all_to_all(own_gates.T, "exp", split_axis=0, concat_axis=0, tiled=True).T
-    holds_shared = lax.axis_index("exp") == slot_count - 1
-    wg, wu, wd = (
-        lax.all_gather(jnp.where(holds_shared, shared, routed[0]), "hid", axis=0)
-        for shared, routed in ((s_gate, r_gate), (s_up, r_up), (s_down, r_down))
-    )
-    all_dy, all_h = gather_both(cotangent, hidden_in)
-    scores_e, sums, gg, gu, gd, pg, pu, pd = experts(all_h, all_dy, gates, wg, wu, wd)[:8]
-    slot_grads = (gg + pg.astype(jnp.float32), gu + pu.astype(jnp.float32), gd + pd.astype(jnp.float32))
-    scores = lax.all_to_all(scores_e.T, "exp", split_axis=0, concat_axis=0, tiled=True).T
-    grad_share = jnp.sum(onehot * scores[:, None, :], axis=-1) * token_valid[:, None]
-    grad_logits = soft_gates * (
-        grad_share - jnp.sum(soft_gates * grad_share, axis=-1, keepdims=True)
-    )
-    flat = (seq_len, width)
-    cosine = jnp.tile(cosine_table[:, 0], (1, 2))
-    sine = jnp.concatenate([-sine_table[:, 0], sine_table[:, 0]], axis=1)
-    count_row = jnp.pad(local_counts[None], ((0, 0), (0, width - slot_count)))
-    output, grad_tokens, small_sums, sum0, sum1, sum_g, sum_u, sum_d = tail(
-        slot_count, tokens, mixed, cotangent, sums, queries.reshape(flat), keys_all.reshape(flat),
-        values_all.reshape(flat), attended_low, attn_prob, full_query, full_key, full_value, full_out,
-        norm_one[None], norm_two[None], cosine, sine, count_row,
-        to_blocks(slot_grads[0], slot_count), to_blocks(slot_grads[1], slot_count), to_blocks(slot_grads[2], slot_count),
+    scores, sums, tg, tu, td, bg, bu, bd = experts(all_h, all_dy, gates, fg, fu, fd)[:8]
+    full = (width, width)
+    output, grad_tokens, grad_logits, small_sums, sum0, sum1, sum_g, sum_u, sum_d = tail(
+        n, tokens, mixed, cotangent, sums, queries, keys_all, values_all, attended, prob,
+        fq.reshape(full), fk.reshape(full), fv.reshape(full), fo.reshape(full),
+        gain1, gain2, cosine, sine, counts, length, logits, routes, scores,
+        bg.reshape(n, -1, hidden), bu.reshape(n, -1, hidden), bd.reshape(n, -1, width),
     )
     half = width // 2
     wout_value = from_blocks(sum0, width)
     key_query = from_blocks(sum1, width)
-    hidden = s_gate.shape[1]
-    routed_grads = tuple(jnp.where(holds_shared, 0.0, grad)[None] for grad in slot_grads)
+    holds_shared = lax.axis_index("exp") == n - 1
+    routed_grads = tuple(jnp.where(holds_shared, 0.0, grad)[None] for grad in (tg, tu, td))
     return (
-        output,
-        grad_tokens,
-        small_sums[0],
-        key_query[half:],
-        key_query[:half],
-        wout_value[half:],
-        wout_value[:half],
-        small_sums[1],
-        routed_grads[0],
-        routed_grads[1],
-        routed_grads[2],
-        from_blocks(sum_g, width),
-        from_blocks(sum_u, width),
-        from_blocks(sum_d, hidden),
-        grad_logits,
-        small_sums[2, :slot_count].astype(jnp.int32),
+        output, grad_tokens, small_sums[0],
+        key_query[half:], key_query[:half], wout_value[half:], wout_value[:half],
+        small_sums[1], routed_grads[0], routed_grads[1], routed_grads[2],
+        from_blocks(sum_g, width), from_blocks(sum_u, width), from_blocks(sum_d, hidden),
+        grad_logits, small_sums[2, :n].astype(jnp.int32),
     )
 
 

time: 776 us -> 691 us (0.89)
  local copies, waits for them, and re-layouts: 61.5 us -> 34.5 us
  starting transfers between devices: 17.2 us -> 0 us
  matrix products: 16.1 us -> 0 us
  other arithmetic: 27.5 us -> 13 us
  between operations: 15.6 us -> 1.81 us
  Pallas kernels: 621 us -> 633 us
  waiting for transfers between devices: 11 us -> 0 us
    all_to_all x2 -> x0, starting transfers between devices: 17 us -> none  [the longest x1 8.6 us: on_device(): lax.all_to_all(scores_e.T, 'exp', split_axis=0, concat_axis=0, tiled=True)]
    dot_general x5 -> x0, matrix products: 13.6 us -> none  [the longest x4 13 us: matmul(): return jnp.dot(left_side, right_side, preferred_element_type=jnp.float32)]
    convert_element_type x6 -> x0, local copies, waits for them, and re-layouts: 9.99 us -> none  [the longest x2 4.33 us: on_device(): keys_all = rotate(matmul(attn_in, full_key).reshape(heads_shape), cosine_...]
    all_gather x7 -> x0, waiting for transfers between devices: 8.36 us -> none  [the longest x1 8.28 us: on_device(): lax.all_gather(w_key, 'hid', axis=0, tiled=True)]
    unnamed x79 -> x31, local copies, waits for them, and re-layouts: 30.9 us -> 22.6 us
  transfers between devices with their start and end apart: 9 -> 0, of which waited for: 1 -> 0; matrix products, arithmetic and copies ran while one was open for 9% -> 0% of each run, Pallas kernels for 23% -> 0%
where the time goes in v3:
time: 691 us; the launch traced here: 682 us
  Pallas kernels  633 us (92%)
  local copies, waits for them, and re-layouts  34.5 us (5%)
  other arithmetic  13 us (2%)
    pallas_call x1, Pallas kernels, experts(): pl.pallas_call(functools.partial(experts_kernel, n, slots), out_shape=(ou...  224 us
    pallas_call x1, Pallas kernels, tail(): pl.pallas_call(functools.partial(tail_kernel, n), out_shape=(out((rows, w...  223 us
    pallas_call x1, Pallas kernels, front(): pl.pallas_call(functools.partial(front_kernel, n), out_shape=(out((n, row...  187 us
    unnamed x31, local copies, waits for them, and re-layouts  22.6 us

profile of v3, /device:TPU:0, one launch (start us, length us, event | category | flops | bytes accessed | tf_op | source)
XLA Modules:
  0.0 682.2 jit_solution(9674121862792031899)
XLA Ops:
  0.6 0.0 copy-start.2
  0.7 0.0 copy-start.3
  0.7 1.6 copy.37.logit_ref
  2.3 1.5 copy.38.route_ref
  3.8 1.3 broadcast_in_dim.32.gain1
  5.1 1.3 broadcast_in_dim.33.gain2
  7.0 0.5 broadcast_in_dim.35.len_ref
  7.5 2.4 copy.35
  9.9 1.4 copy.36
  11.4 1.4 copy.39.sg
  12.9 1.4 copy.40.su
  14.3 186.6 %shard_map.306 = (bf16[16,256,1280]{2,1,0:T(8,128)(2,1)}, bf16[16,256,1280]{2,1,0:T(8,128)(2,1)}, bf16[2,640,1280]{2,1,0:T(8,128)(2,1)}, bf16[2,640,1280]{2,1,0:...) custom-call(bf16[256,1280]{1,0:T(8,128)(2,1)} %x_ref.3, ...), custom_call_target="tpu_custom_call" | custom-call | tf_op jit(solution)/shard_map/pallas_call | solution.py:333
  201.0 223.6 %shard_map.307 = (f32[16,1,256]{2,1,0:T(1,128)}, f32[2,256,1280]{2,1,0:T(8,128)}, f32[1280,448]{1,0:T(8,128)}, f32[1280,448]{1,0:T(8,128)}, f32[448,1280]{1,0:T(...) custom-call(bf16[16,256,1280]{2,1,0:T(8,128)(2,1)} %get-tuple-elemen, ...), custom_call_target="tpu_custom_call" | custom-call | tf_op jit(solution)/shard_map/pallas_call | solution.py:559
  424.6 222.6 %shard_map.308 = (bf16[256,1280]{1,0:T(8,128)(2,1)}, bf16[256,1280]{1,0:T(8,128)(2,1)}, f32[256,7]{1,0:T(8,128)}, f32[8,1280]{1,0:T(8,128)}, bf16[16,80,1280]{2,...) custom-call(bf16[256,1280]{1,0:T(8,128)(2,1)} %x_ref.3, ...), custom_call_target="tpu_custom_call" | custom-call | tf_op jit(solution)/shard_map/pallas_call | solution.py:908
  647.3 4.0 bitcast_convert_fusion
  651.2 3.1 copy.45
  654.3 2.0 copy.46
  656.3 4.7 select_bitcast_fusion
  661.0 2.0 copy.43
  663.0 3.3 copy.44
  666.2 7.2 %fusion = (f32[8,80,1280]{2,1,0:T(8,128)}, f32[8,80,1280]{2,1,0:T(8,128)}, f32[8,80,1280]{2,1,0:T(8,128)}, f32[8,80,1280]{2,1,0:T(8,128)}) fusion(bf16[16,80,1280]{2,1,0:T(8,128)(2,1)S(1)} %copy-done, bf16[16,80,1280]{2,1,0:T(8,128)(2,1)} %get-tuple-element.75), kind=kLoop, calls=%fused_computation.9 | loop fusion | bytes 26214400 | tf_op jit(solution)/shard_map/slice | solution.py:979
  673.5 0.1 slice.47
  673.6 1.6 bitcast_convert_fusion.2
  675.2 1.5 slice_reduce_fusion
  676.7 0.0 copy-done.8
  676.7 0.7 copy.47
  677.4 1.2 convert_bitcast_fusion
  678.6 0.0 copy-done.1
  678.6 1.5 select_bitcast_fusion.2
  680.1 0.0 copy-done.7
  680.1 0.8 copy.51
  680.9 0.8 copy.52
  (13 shorter events, 0.0 us)
Async XLA Ops:
  0.6 9.3 %copy-start.2 = (bf16[1,1280,448]{1,2,0:T(8,128)(2,1)S(1)}, bf16[1,1280,448]{1,2,0:T(8,128)(2,1)}, u32[]{:S(2)}) copy-start(bf16[1,1280,448]{1,2,0:T(8,128)(2,1)} %param.27) | copy-start | bytes 3440644
  0.7 10.7 %copy-start.3 = (bf16[1280,448]{0,1:T(8,128)(2,1)S(1)}, bf16[1280,448]{0,1:T(8,128)(2,1)}, u32[]{:S(2)}) copy-start(bf16[1280,448]{0,1:T(8,128)(2,1)} %param.29) | copy-start | bytes 3440644
  9.9 2.9 copy-start.4
  663.0 3.3 copy-start
  666.2 7.2 %copy-start.5 = (bf16[16,32,1280]{2,1,0:T(8,128)(2,1)S(1)}, bf16[16,32,1280]{2,1,0:T(8,128)(2,1)}, u32[]{:S(2)}) copy-start(bf16[16,32,1280]{2,1,0:T(8,128)(2,1)} %get-tuple-element.82) | copy-start | bytes 3932164
  673.5 3.2 copy-start.8
  673.5 5.1 copy-start.1
  675.2 4.9 copy-start.7
  678.6 2.4 copy-start.6

commit v4 on v3

--- a/solution.py
+++ b/solution.py
@@ -160,27 +160,27 @@
 
 
 def part_rows(rows):
-    return rows
+    return rows - rows // 80 * 16
 
 
 def front_kernel(
     n,
-    x_ref, cot_hbm, gain1, gain2, cos_ref, sin_ref, len_ref, logit_ref, route_ref,
+    x_ref, cot_ref, gain1, gain2, cos_ref, sin_ref, len_ref, logit_ref, route_ref,
     wq, wk, wv, wo, rg, ru, rd, sg, su, sd,
     all_dy, all_h, fq, fk, fv, fo, fg, fu, fd,
     x1_ref, q_ref, k_ref, v_ref, o_ref, p_ref, gates_in, cnt_ref,
-    wbuf, h_ref, rows_out,
-    gs, gr, ls, ws, wr, wl, es, er, el, gss, grs,
+    wbuf, h_ref, rows_out, turn_ref,
+    gs, gr, ls, ws, wr, wl, es, er, gss, grs,
 ):
     pc = Place(n)
     e, c = pc.e, pc.c
     rows, width = x_ref.shape
     half = width // 2
     pc.greet_all()
-    gather_dy = Gather(pc, cot_hbm, all_dy, gs.at[0], gr.at[0], part_rows(rows))
+    gather_dy = Gather(pc, cot_ref, all_dy, gs.at[0], gr.at[0], part_rows(rows))
     gather_h = Gather(pc, h_ref, all_h, gs.at[1], gr.at[1], part_rows(rows))
     gather_dy.start()
-    own_dy = pltpu.make_async_copy(cot_hbm, all_dy.at[e], ls.at[0])
+    own_dy = pltpu.make_async_copy(cot_ref, all_dy.at[e], ls.at[0])
     own_dy.start()
     partner = (e, 1 - c)
     halves = (wq, wk, wv, wo)
@@ -198,16 +198,13 @@
     def keep(i):
         return pltpu.make_async_copy(wbuf.at[i], fulls[i], wl.at[1, i])
 
-    experts_full = (fg, fu, fd)
+    experts_other = (fg, fu, fd)
 
     def expert_swap(i, src):
         return pltpu.make_async_remote_copy(
-            src_ref=src, dst_ref=experts_full[i].at[c], send_sem=es.at[i], recv_sem=er.at[i],
+            src_ref=src, dst_ref=experts_other[i], send_sem=es.at[i], recv_sem=er.at[i],
             device_id=partner, device_id_type=MESH,
         )
-
-    def expert_own(i, src):
-        return pltpu.make_async_copy(src, experts_full[i].at[c], el.at[i])
 
     for i in range(4):
         swap(i).start()
@@ -216,23 +213,18 @@
         @pl.when(e == n - 1)
         def _():
             expert_swap(i, shared).start()
-            expert_own(i, shared).start()
 
         @pl.when(e != n - 1)
         def _():
             expert_swap(i, routed).start()
-            expert_own(i, routed).start()
 
     lane = lax.broadcasted_iota(jnp.int32, (rows, 128), 1)
     row = lax.broadcasted_iota(jnp.int32, (rows, 128), 0)
-    valid = (row < len_ref[...]).astype(jnp.float32)
-    logits = logit_ref[...]
-    raised = jnp.exp(logits - jnp.max(logits, axis=-1, keepdims=True))
-    soft = raised / jnp.sum(raised, axis=-1, keepdims=True)
-    routes = route_ref[...]
+    valid = (row < len_ref[0]).astype(jnp.float32)
+    soft, routes = route_columns(logit_ref, route_ref, turn_ref)
     dense = jnp.zeros((rows, 128), jnp.float32)
     named = jnp.zeros((rows, 128), jnp.float32)
-    for i in range(routes.shape[1]):
+    for i in range(route_ref.shape[0]):
         hit = lane == routes[:, i : i + 1]
         dense = dense + jnp.where(hit, soft[:, i : i + 1], 0.0)
         named = named + jnp.where(hit, 1.0, 0.0)
@@ -277,8 +269,7 @@
     scale = HD ** (-0.5)
     row_pos = lax.broadcasted_iota(jnp.int32, (rows, rows), 0)
     col_pos = lax.broadcasted_iota(jnp.int32, (rows, rows), 1)
-    length = jnp.concatenate([len_ref[...]] * (rows // 128), axis=1)
-    allowed = (col_pos <= row_pos) & (col_pos < length)
+    allowed = (col_pos <= row_pos) & (col_pos < len_ref[0])
 
     def one_head(hd, carry):
         at = pl.ds(pl.multiple_of(hd * HD, HD), HD)
@@ -317,12 +308,11 @@
         keep(i).wait()
     for i, shared in enumerate((sg, su, sd)):
         expert_swap(i, shared).wait()
-        expert_own(i, shared).wait()
 
 
 def front(n, x, cot, gain1, gain2, cosine, sine, length, logits, routes, attn_w, routed_w, shared_w):
     rows, width = x.shape
-    hidden = shared_w[0].shape[1]
+    hidden = shared_w[0].shape[0]
     vmem = pl.BlockSpec(memory_space=pltpu.VMEM)
     hbm = pl.BlockSpec(memory_space=pl.ANY)
     f32, b16 = jnp.float32, jnp.bfloat16
@@ -334,15 +324,15 @@
         functools.partial(front_kernel, n),
         out_shape=(
             out((n, rows, width), b16), out((n, rows, width), b16), full, full, full, full,
-            out((2, width, hidden), b16), out((2, width, hidden), b16), out((2, hidden, width), b16),
+            out((hidden, width), b16), out((hidden, width), b16), out((hidden, width), b16),
             out((rows, width), f32), wide, wide, wide, wide, out((HEADS, rows, rows), f32),
             out((n, 1, rows), f32), out((1, width), f32),
         ),
-        in_specs=[vmem, hbm] + [vmem] * 7 + [hbm] * 10,
+        in_specs=[vmem] * 6 + [pl.BlockSpec(memory_space=pltpu.SMEM)] + [vmem] * 2 + [hbm] * 10,
         out_specs=(hbm,) * 9 + (vmem,) * 8,
         scratch_shapes=[
-            pltpu.VMEM((4, 2, width // 2, width), b16), pltpu.VMEM((rows, width), b16), pltpu.VMEM((n, 1, rows), f32),
-            dma((2, 160)), dma((2, 2, n)), dma((2,)), dma((4,)), dma((4,)), dma((2, 4)), dma((3,)), dma((3,)), dma((3,)),
+            pltpu.VMEM((4, 2, width // 2, width), b16), pltpu.VMEM((rows, width), b16), pltpu.VMEM((n, 1, rows), f32), pltpu.VMEM((128, rows), f32),
+            dma((2, 160)), dma((2, 2, n)), dma((2,)), dma((4,)), dma((4,)), dma((2, 4)), dma((3,)), dma((3,)),
             dma((n,)), dma((n,)),
         ],
         compiler_params=pltpu.CompilerParams(collective_id=0, has_side_effects=True, vmem_limit_bytes=56 * 2**20),
@@ -351,28 +341,37 @@
 
 def experts_kernel(
     n, slots,
-    h_hbm, dy_hbm, gates_in, wg, wu, wd,
-    scores_in, sums_hbm, tg_hbm, tu_hbm, td_hbm, bg_hbm, bu_hbm, bd_hbm, r3_hbm, r2_hbm, r1_hbm,
-    og, ou, od, ysum, hbuf, dbuf, act, dg, dup, stage, rbuf, xg, xu, xd, pg, pu, pd, gate_ref, s_ref, turn_ref, rows_out,
-    lsem, ssem, r3sem, r2sem, r1sem, bsem, xssem, xrsem, osem, psem, scs, scr,
+    h_hbm, dy_hbm, gates_in, rg, ru, rd, shg, shu, shd, xg, xu, xd,
+    scores_in, sums_hbm, tg_hbm, tu_hbm, td_hbm, pay_hbm, r3_hbm, r2_hbm, r1_hbm,
+    wg, wu, wd, og, ou, od, ysum, hbuf, dbuf, act, dg, dup, stage, rbuf, give, take, gate_ref, s_ref, turn_ref, rows_out,
+    lsem, ssem, r3sem, r2sem, r1sem, bsem, xssem, xrsem, osem, psem, scs, scr, wsem,
 ):
     pc = Place(n)
     nz, m = pc.nz, pc.m
+    plane = m * m
     c1, c2, c3, e, c = pc.c1, pc.c2, pc.c3, pc.e, pc.c
+    weights = (wg, wu, wd)
+
+    def weight(i, src, which):
+        return pltpu.make_async_copy(src, weights[i].at[which], wsem.at[i, which])
+
+    for i, (routed, shared, other) in enumerate(((rg, shg, xg), (ru, shu, xu), (rd, shd, xd))):
+        pl.when(e == n - 1)(weight(i, shared, c).start)
+        pl.when(e != n - 1)(weight(i, routed, c).start)
+        weight(i, other, 1 - c).start()
     pc.greet_all()
     turn_ref[...] = jnp.zeros_like(turn_ref)
     for i in range(n):
         turn_ref[i : i + 1, :] = gates_in[i]
     gate_ref[...] = turn_ref[...].T
-    og[...] = jnp.zeros_like(og)
-    ou[...] = jnp.zeros_like(ou)
-    od[...] = jnp.zeros_like(od)
+    grads = (og, ou, od)
+    for total in grads:
+        total[...] = jnp.zeros_like(total)
     s_ref[...] = jnp.zeros_like(s_ref)
-    n3 = (m - 1) * nz * m
-    n2 = (m - 1) * nz
 
     def dest(t):
-        return (c1 + t + 1) % nz, (c2 + t // nz + 1) % m, (c3 + t // (nz * m) + 1) % m
+        r = t % plane
+        return (c1 + t // plane + 1) % nz, (c2 + r % m + 1) % m, (c3 + r // m + 1) % m
 
     def load(t, i):
         b = pc.blk(*dest(t))
@@ -387,23 +386,39 @@
             device_id=(to, c), device_id_type=MESH,
         )
 
-    def add_received(src, sem):
-        pltpu.make_async_remote_copy(
-            src_ref=src, dst_ref=src, send_sem=ssem.at[0], recv_sem=sem,
-            device_id=(e, 1 - c), device_id_type=MESH,
-        ).wait_recv()
-        copy = pltpu.make_async_copy(src, rbuf, bsem)
-        copy.start()
-        copy.wait()
-        ysum[...] += rbuf[...].astype(jnp.float32)
+    def collect(slot, received):
+        def fetch(i):
+            return pltpu.make_async_copy(received[i][0], rbuf.at[i % 2], bsem.at[i % 2])
+
+        def begin(i):
+            src, sem = received[i]
+            partial_copy(slot, e, src, sem).wait_recv()
+            fetch(i).start()
+
+        begin(0)
+        ysum[...] = stage[slot].astype(jnp.float32)
+        for i in range(len(received)):
+            if i + 1 < len(received):
+                begin(i + 1)
+            fetch(i).wait()
+            ysum[...] += rbuf[i % 2].astype(jnp.float32)
+
+    def from3(a, b2):
+        return [(r3_hbm.at[j, a, b2], r3sem.at[j, a, b2]) for j in range(m - 1)]
+
+    def from2(a):
+        return [(r2_hbm.at[j, a], r2sem.at[j, a]) for j in range(m - 1)]
+
+    def from1():
+        return [(r1_hbm.at[j], r1sem.at[j]) for j in range(nz - 1)]
 
     def swaps():
         return [
             pltpu.make_async_remote_copy(
-                src_ref=src, dst_ref=dst, send_sem=xssem.at[i], recv_sem=xrsem.at[i],
+                src_ref=give.at[i], dst_ref=take.at[i], send_sem=xssem.at[i], recv_sem=xrsem.at[i],
                 device_id=(e, 1 - c), device_id_type=MESH,
             )
-            for i, (src, dst) in enumerate(((xg, pg), (xu, pu), (xd, pd)))
+            for i in range(3)
         ]
 
     def totals():
@@ -413,10 +428,7 @@
         ]
 
     def payload():
-        return [
-            pltpu.make_async_copy(src, dst.at[pl.ds(0, src.shape[0])], psem.at[i])
-            for i, (src, dst) in enumerate(((xg, bg_hbm), (xu, bu_hbm), (xd, bd_hbm)))
-        ]
+        return [pltpu.make_async_copy(give.at[i], pay_hbm.at[i, pl.ds(0, give.shape[1])], psem.at[i]) for i in range(3)]
 
     def score_send(to):
         return pltpu.make_async_remote_copy(
@@ -426,6 +438,9 @@
 
     for copy in load(0, 0):
         copy.start()
+    for i, other in enumerate((xg, xu, xd)):
+        for which in range(2):
+            weight(i, other, which).wait()
 
     def body(t, carry):
         i = t % 2
@@ -446,64 +461,62 @@
         dy = dbuf[i].astype(jnp.float32)
         z = (gate * dy).astype(jnp.bfloat16)
         for half in range(2):
-            g = matmul(h, wg[half])
-            u = matmul(h, wu[half])
+            g = inner_cols(h, wg[half])
+            u = inner_cols(h, wu[half])
             da = inner_cols(z, wd[half])
             sg = jax.nn.sigmoid(g)
             si = g * sg
             act[half] = (si * u).astype(jnp.bfloat16)
             dup[half] = (da * si).astype(jnp.bfloat16)
             dg[half] = (da * u * sg * (1.0 + g * (1.0 - sg))).astype(jnp.bfloat16)
+
+        @pl.when(t >= slots)
+        def _():
+            partial_copy(slot, e, r1_hbm.at[0], r1sem.at[0]).wait_send()
+
         y = (matmul(act[0], wd[0]) + matmul(act[1], wd[1])).astype(jnp.bfloat16).astype(jnp.float32)
         s = jnp.sum(y * dy, axis=1, keepdims=True)
         s_ref[...] = jnp.where(lane == b, s, s_ref[...])
-        ysum[0] = gate * y
-        ysum[1] = (
-            inner_cols(dg[0], wg[0]) + inner_cols(dg[1], wg[1])
-            + inner_cols(dup[0], wu[0]) + inner_cols(dup[1], wu[1])
-        ).astype(jnp.bfloat16).astype(jnp.float32)
-
-        @pl.when((t >= slots) & (t - slots < n - 1))
-        def _():
-            partial_copy(slot, e, r1_hbm.at[0], r1sem.at[0]).wait_send()
-
-        @pl.when(t >= n3)
+        stage[slot, 0] = (gate * y).astype(jnp.bfloat16)
+        stage[slot, 1] = (
+            matmul(dg[0], wg[0]) + matmul(dg[1], wg[1]) + matmul(dup[0], wu[0]) + matmul(dup[1], wu[1])
+        ).astype(jnp.bfloat16)
+
+        for j in range(1, m):
+            @pl.when(b3 == (c3 + j) % m)
+            def _():
+                partial_copy(slot, pc.blk(c1, c2, b3), r3_hbm.at[m - j - 1, a, b2], r3sem.at[m - j - 1, a, b2]).start()
+
+        for half in range(2):
+            og[half] += outer_rows(dg[half], h)
+            ou[half] += outer_rows(dup[half], h)
+            od[half] += outer_rows(act[half], z)
+
+        @pl.when(t % plane == plane - 1)
         def _():
             for j in range(1, m):
-                add_received(r3_hbm.at[j - 1, a, b2], r3sem.at[j - 1, a, b2])
-
-        @pl.when(t >= n3 + n2)
+                to2 = (c2 + j) % m
+                at = (t - m + j) % slots
+                collect(at, from3(a, to2))
+                stage[at] = ysum[...].astype(jnp.bfloat16)
+                partial_copy(at, pc.blk(c1, to2, c3), r2_hbm.at[m - j - 1, a], r2sem.at[m - j - 1, a]).start()
+
+        @pl.when((t % plane == 1) & (t >= plane))
         def _():
-            for j in range(1, m):
-                add_received(r2_hbm.at[j - 1, a], r2sem.at[j - 1, a])
-
-        @pl.when(t < n - 1)
-        def _():
-            stage[slot] = ysum[...].astype(jnp.bfloat16)
-
-        for j in range(1, m):
-            @pl.when((t < n3) & (b3 == (c3 + j) % m))
-            def _():
-                partial_copy(slot, pc.blk(c1, c2, b3), r3_hbm.at[m - j - 1, a, b2], r3sem.at[m - j - 1, a, b2]).start()
-
-            @pl.when((t >= n3) & (t < n3 + n2) & (b2 == (c2 + j) % m))
-            def _():
-                partial_copy(slot, pc.blk(c1, b2, c3), r2_hbm.at[m - j - 1, a], r2sem.at[m - j - 1, a]).start()
-
-        for j in range(1, nz):
-            @pl.when((t >= n3 + n2) & (t < n - 1) & (a == (c1 + j) % nz))
-            def _():
-                partial_copy(slot, pc.blk(a, c2, c3), r1_hbm.at[nz - j - 1], r1sem.at[nz - j - 1]).start()
-
-        for half in range(2):
-            og[half] += outer_rows(h, dg[half])
-            ou[half] += outer_rows(h, dup[half])
-            od[half] += outer_rows(act[half], z)
+            at = (t - 2) % slots
+            for j in range(1, nz):
+                @pl.when(t // plane == j)
+                def _():
+                    a1 = (c1 + j) % nz
+                    collect(at, from3(a1, c2) + from2(a1))
+                    stage[at] = ysum[...].astype(jnp.bfloat16)
+                    partial_copy(at, pc.blk(a1, c2, c3), r1_hbm.at[nz - j - 1], r1sem.at[nz - j - 1]).start()
+
         return carry
 
     lax.fori_loop(0, n, body, 0)
-    for buf, total in ((xg, og), (xu, ou), (xd, od)):
-        buf[...] = total[1 - c].astype(jnp.bfloat16)
+    for i, total in enumerate(grads):
+        give[i] = total[1 - c].astype(jnp.bfloat16)
     for copy in swaps():
         copy.start()
     turned = s_ref[...].T
@@ -518,14 +531,13 @@
     lax.fori_loop(1, n, score_start, 0)
     for copy in swaps():
         copy.wait()
-    for buf, got, total in ((xg, pg, og), (xu, pu, ou), (xd, pd, od)):
-        total[c] += got[...].astype(jnp.float32)
-        buf[...] = total[c].astype(jnp.bfloat16)
+    for i, total in enumerate(grads):
+        total[c] += take[i].astype(jnp.float32)
+        give[i] = total[c].astype(jnp.bfloat16)
     for copy in totals() + payload():
         copy.start()
-    for j in range(1, nz):
-        add_received(r1_hbm.at[j - 1], r1sem.at[j - 1])
-    final = pltpu.make_async_copy(ysum, sums_hbm, bsem)
+    collect((n - 1) % slots, from3(c1, c2) + from2(c1) + from1())
+    final = pltpu.make_async_copy(ysum, sums_hbm, bsem.at[0])
     final.start()
     final.wait()
     for t in range(max(0, n - slots), n - 1):
@@ -544,9 +556,9 @@
         copy.wait()
 
 
-def experts(h, dy, gates, wg, wu, wd):
+def experts(h, dy, gates, routed_w, shared_w, other_w):
     n, rows, width = h.shape
-    hidden = wg.shape[2]
+    hidden = shared_w[0].shape[0]
     nz = 4
     m = {16: 2, 64: 4}[n]
     slots = 8
@@ -555,34 +567,44 @@
     f32, b16 = jnp.float32, jnp.bfloat16
     out = jax.ShapeDtypeStruct
     dma = pltpu.SemaphoreType.DMA
-    up_rows, down_rows = n * blocked(width, n), n * blocked(hidden, n)
+    grad, both = pltpu.VMEM((2, hidden, width), f32), pltpu.VMEM((2, hidden, width), b16)
     return pl.pallas_call(
         functools.partial(experts_kernel, n, slots),
         out_shape=(
             out((n, 1, rows), f32), out((2, rows, width), f32),
-            out((width, hidden), f32), out((width, hidden), f32), out((hidden, width), f32),
-            out((up_rows, hidden), b16), out((up_rows, hidden), b16), out((down_rows, width), b16),
+            out((hidden, width), f32), out((hidden, width), f32), out((hidden, width), f32),
+            out((3, n * blocked(hidden, n), width), b16),
             out((m - 1, nz, m, 2, rows, width), b16), out((m - 1, nz, 2, rows, width), b16), out((nz - 1, 2, rows, width), b16),
         ),
-        in_specs=[hbm, hbm, vmem, vmem, vmem, vmem],
-        out_specs=(vmem,) + (hbm,) * 10,
+        in_specs=[hbm, hbm, vmem] + [hbm] * 9,
+        out_specs=(vmem,) + (hbm,) * 8,
         scratch_shapes=[
-            pltpu.VMEM((2, width, hidden), f32), pltpu.VMEM((2, width, hidden), f32), pltpu.VMEM((2, hidden, width), f32),
+            both, both, both, grad, grad, grad,
             pltpu.VMEM((2, rows, width), f32), pltpu.VMEM((2, rows, width), b16), pltpu.VMEM((2, rows, width), b16),
             pltpu.VMEM((2, rows, hidden), b16), pltpu.VMEM((2, rows, hidden), b16), pltpu.VMEM((2, rows, hidden), b16),
-            pltpu.VMEM((slots, 2, rows, width), b16), pltpu.VMEM((2, rows, width), b16),
-            pltpu.VMEM((width, hidden), b16), pltpu.VMEM((width, hidden), b16), pltpu.VMEM((hidden, width), b16),
-            pltpu.VMEM((width, hidden), b16), pltpu.VMEM((width, hidden), b16), pltpu.VMEM((hidden, width), b16),
+            pltpu.VMEM((slots, 2, rows, width), b16), pltpu.VMEM((2, 2, rows, width), b16),
+            pltpu.VMEM((3, hidden, width), b16), pltpu.VMEM((3, hidden, width), b16),
             pltpu.VMEM((rows, 128), f32), pltpu.VMEM((rows, 128), f32), pltpu.VMEM((128, rows), f32), pltpu.VMEM((n, 1, rows), f32),
-            dma((2, 2)), dma((slots,)), dma((m - 1, nz, m)), dma((m - 1, nz)), dma((nz - 1,)), dma,
-            dma((3,)), dma((3,)), dma((3,)), dma((3,)), dma((n,)), dma((n,)),
+            dma((2, 2)), dma((slots,)), dma((m - 1, nz, m)), dma((m - 1, nz)), dma((nz - 1,)), dma((2,)),
+            dma((3,)), dma((3,)), dma((3,)), dma((3,)), dma((n,)), dma((n,)), dma((3, 2)),
         ],
         compiler_params=pltpu.CompilerParams(collective_id=1, has_side_effects=True, vmem_limit_bytes=62 * 2**20),
-    )(h, dy, gates, wg, wu, wd)
+    )(h, dy, gates, *routed_w, *shared_w, *other_w)
 
 
 def swap_halves(values):
     return pltpu.roll(values, HD // 2, axis=1)
+
+
+def route_columns(logit_ref, route_ref, turn_ref):
+    count = logit_ref.shape[0]
+    logits = logit_ref[...]
+    raised = jnp.exp(logits - jnp.max(logits, axis=0, keepdims=True))
+    turn_ref[...] = jnp.zeros_like(turn_ref)
+    turn_ref[0:count, :] = raised / jnp.sum(raised, axis=0, keepdims=True)
+    soft = turn_ref[...].T
+    turn_ref[0:count, :] = route_ref[...].astype(jnp.float32)
+    return soft, turn_ref[...].T.astype(jnp.int32)
 
 
 class Scatter:
@@ -653,11 +675,11 @@
 def tail_kernel(
     n,
     x_ref, x1_ref, cot_ref, sums_ref, q_ref, k_ref, v_ref, o_ref, p_ref, wq, wk, wv, wo,
-    gain1, gain2, cos_ref, sin_ref, cnt_ref, len_ref, logit_ref, route_ref, scores_in, sg_hbm, su_hbm, sd_hbm,
-    out_ref, gtok_ref, glog_ref, small_ref, ag0, ag1, agg, agu, agd,
+    gain1, gain2, cos_ref, sin_ref, cnt_ref, len_ref, logit_ref, route_ref, scores_in, pay_hbm,
+    out_ref, gtok_ref, glog_ref, small_ref, ag0, ag1, ags,
     dx_ref, dq_ref, dk_ref, dv_ref, do_ref, a_ref, give, take, stack0, stack1, r3, r2, r1,
     sm_core, sm_d3, sm_d2, sm_z,
-    wbuf, wsem, turn_ref,
+    wbuf, wsem, turn_ref, own_pay,
     gs, gr, ss, s3, s2, s1, xs, xr, cs, cr, scs, scr, locs,
 ):
     pc = Place(n)
@@ -666,18 +688,15 @@
     half = width // 2
     pc.greet_all()
 
-    shared = ((sg_hbm, agg), (su_hbm, agu), (sd_hbm, agd))
 
     def deal(i, to):
-        src, dst = shared[i]
         return pltpu.make_async_remote_copy(
-            src_ref=src.at[to], dst_ref=dst.at[to], send_sem=scs.at[i, to], recv_sem=scr.at[i],
+            src_ref=pay_hbm.at[i, to], dst_ref=own_pay.at[i], send_sem=scs.at[i, to], recv_sem=scr.at[i],
             device_id=(to, c), device_id_type=MESH,
         )
 
     def keep(i):
-        src, dst = shared[i]
-        return pltpu.make_async_copy(src.at[n - 1], dst.at[n - 1], scs.at[i, n - 1])
+        return pltpu.make_async_copy(pay_hbm.at[i, n - 1], own_pay.at[i], scs.at[i, n - 1])
 
     @pl.when(e == n - 1)
     def _():
@@ -690,7 +709,8 @@
         for i in range(3):
             keep(i).start()
 
-    gathers = [Gather(pc, dst.at[e], dst, gs.at[i], gr.at[i], dst.shape[1]) for i, (src, dst) in enumerate(shared)]
+    gather_s = Gather(pc, own_pay, ags, gs.at[2], gr.at[2], 3)
+    loc_s = pltpu.make_async_copy(own_pay, ags.at[e], locs.at[2])
 
     def shared_start():
         @pl.when(e == n - 1)
@@ -701,14 +721,13 @@
         @pl.when(e != n - 1)
         def _():
             for i in range(3):
-                src, dst = shared[i]
                 pltpu.make_async_remote_copy(
-                    src_ref=dst.at[e], dst_ref=dst.at[e], send_sem=scs.at[i, 0], recv_sem=scr.at[i],
+                    src_ref=own_pay.at[i], dst_ref=own_pay.at[i], send_sem=scs.at[i, 0], recv_sem=scr.at[i],
                     device_id=(n - 1, c), device_id_type=MESH,
                 ).wait_recv()
 
-        for g in gathers:
-            g.start()
+        gather_s.start()
+        loc_s.start()
 
     def fetch(src, i):
         return pltpu.make_async_copy(src, wbuf.at[i], wsem.at[i])
@@ -785,10 +804,11 @@
     first = Scatter(pc, stack0, r3.at[0], r2.at[0], r1.at[0], (ss.at[0], s3.at[0], s2.at[0], s1.at[0]))
     second = Scatter(pc, stack1, r3.at[1], r2.at[1], r1.at[1], (ss.at[1], s3.at[1], s2.at[1], s1.at[1]))
     first.start()
-    shared_start()
     own_part(2, a_ref, dk_ref[...], stack1, 0)
     own_part(3, a_ref, dq_ref[...], stack1, 1)
     second.start()
+    shared_start()
+    shared_events = gather_s.events()
     fetch(wv, 1).wait()
     da = inner_cols(dv_ref[...], wbuf[1])
     fetch(wq, 1).start()
@@ -834,50 +854,49 @@
     scores = turn_ref[...].T
     lane = lax.broadcasted_iota(jnp.int32, (rows, 128), 1)
     row = lax.broadcasted_iota(jnp.int32, (rows, 128), 0)
-    scores = jnp.where(row < len_ref[...], scores, 0.0)
-    logits, routes = logit_ref[...], route_ref[...]
-    raised = jnp.exp(logits - jnp.max(logits, axis=-1, keepdims=True))
-    soft = raised / jnp.sum(raised, axis=-1, keepdims=True)
-    picked = [
-        jnp.sum(jnp.where(lane == routes[:, i : i + 1], scores, 0.0), axis=-1, keepdims=True)
-        for i in range(routes.shape[1])
-    ]
-    share = jnp.concatenate(picked, axis=1)
-    glog_ref[...] = soft * (share - jnp.sum(soft * share, axis=-1, keepdims=True))
+    scores = jnp.where(row < len_ref[0], scores, 0.0)
+    soft, routes = route_columns(logit_ref, route_ref, turn_ref)
+    share = jnp.zeros((rows, 128), jnp.float32)
+    for i in range(route_ref.shape[0]):
+        picked = jnp.sum(jnp.where(lane == routes[:, i : i + 1], scores, 0.0), axis=-1, keepdims=True)
+        share = jnp.where(lane == i, picked, share)
+    grad_logits = soft * (share - jnp.sum(soft * share, axis=-1, keepdims=True))
+    glog_ref[...] = grad_logits.T[0 : route_ref.shape[0], :]
 
     small = jnp.concatenate([grad_one, grad_two, cnt_ref[...], jnp.zeros((5, width), jnp.float32)], axis=0)
     level0 = exchange(sm_core, c, 0, [((e, 1 - c), 1 - c)], small)
     first.second()
+    shared_events[0]()
     level1 = exchange(sm_d3, c3, 1, [((pc.blk(c1, c2, j), c), j) for j in pc.o3()], level0())
     second.second()
+    shared_events[1]()
     level2 = exchange(sm_d2, c2, 2, [((pc.blk(c1, j, c3), c), j) for j in pc.o2()], level1())
     first.third()
     level3 = exchange(sm_z, c1, 3, [((pc.blk((c1 + j) % nz, c2, c3), c), (c1 + j) % nz) for j in range(1, nz)], level2())
+    shared_events[2]()
     second.third()
+    shared_events[3]()
     small_ref[...] = level3()
-
-    events = [g.events() for g in gathers]
-    for i in range(len(events[0])):
-        for ev in events:
-            ev[i]()
     first.last()
-    g0 = Gather(pc, stack0.at[e], ag0, gs.at[3], gr.at[3], stack0.shape[1])
+    g0 = Gather(pc, stack0.at[e], ag0, gs.at[0], gr.at[0], stack0.shape[1])
     g0.start()
     loc0 = pltpu.make_async_copy(stack0.at[e], ag0.at[e], locs.at[0])
     loc0.start()
+    shared_events[4]()
     second.last()
-    g1 = Gather(pc, stack1.at[e], ag1, gs.at[4], gr.at[4], stack1.shape[1])
+    g1 = Gather(pc, stack1.at[e], ag1, gs.at[1], gr.at[1], stack1.shape[1])
     g1.start()
     loc1 = pltpu.make_async_copy(stack1.at[e], ag1.at[e], locs.at[1])
     loc1.start()
-    ev0, ev1 = g0.events(), g1.events()
-    for i in range(len(ev0)):
-        ev0[i]()
-        ev1[i]()
-    for g in gathers + [g0, g1]:
+    for event in shared_events[5:-1]:
+        event()
+    run_staggered(g0.events(), g1.events(), 1)
+    shared_events[-1]()
+    for g in (gather_s, g0, g1):
         g.finish()
     first.finish()
     second.finish()
+    loc_s.wait()
     loc0.wait()
     loc1.wait()
     for i in range(4):
@@ -893,7 +912,7 @@
         lax.fori_loop(0, n - 1, one, 0)
 
 
-def tail(n, x, x1, cot, sums, q, k, v, o, prob, wq, wk, wv, wo, gain1, gain2, cosine, sine, cnt, length, logits, routes, scores, sg, su, sd):
+def tail(n, x, x1, cot, sums, q, k, v, o, prob, wq, wk, wv, wo, gain1, gain2, cosine, sine, cnt, length, logits, routes, scores, pay):
     nz = 4
     m = {16: 2, 64: 4}[n]
     rows, width = x.shape
@@ -910,10 +929,10 @@
         out_shape=(
             out((rows, width), b16), out((rows, width), b16), out(logits.shape, f32), out((8, width), f32),
             out((n, block, width), b16), out((n, block, width), b16),
-            out(sg.shape, b16), out(su.shape, b16), out(sd.shape, b16),
+            out((n, 3, pay.shape[2], width), b16),
         ),
-        in_specs=[vmem] * 9 + [hbm] * 4 + [vmem] * 9 + [hbm] * 3,
-        out_specs=(vmem,) * 4 + (hbm,) * 5,
+        in_specs=[vmem] * 9 + [hbm] * 4 + [vmem] * 5 + [pl.BlockSpec(memory_space=pltpu.SMEM)] + [vmem] * 3 + [hbm],
+        out_specs=(vmem,) * 4 + (hbm,) * 3,
         scratch_shapes=[
             pltpu.VMEM((rows, width), f32), wide, wide, wide, wide, wide,
             pltpu.VMEM((4, half, width), b16), pltpu.VMEM((4, half, width), b16),
@@ -921,12 +940,12 @@
             pltpu.VMEM((2, m - 1, nz, m, block, width), b16), pltpu.VMEM((2, m - 1, nz, block, width), b16),
             pltpu.VMEM((2, nz - 1, block, width), b16),
             pltpu.VMEM((2, 8, width), f32), pltpu.VMEM((m, 8, width), f32), pltpu.VMEM((m, 8, width), f32), pltpu.VMEM((nz, 8, width), f32),
-            pltpu.VMEM((2, width, width), b16), dma((2,)), pltpu.VMEM((128, rows), f32),
-            dma((5, 160)), dma((5, 1, n)), dma((2, n)), dma((2, m - 1, nz, m)), dma((2, m - 1, nz)), dma((2, nz - 1)),
-            dma((4,)), dma((4,)), dma((4, max(nz, m))), dma((4, max(nz, m, 2))), dma((3, n)), dma((3,)), dma((2,)),
+            pltpu.VMEM((2, width, width), b16), dma((2,)), pltpu.VMEM((128, rows), f32), pltpu.VMEM((3, pay.shape[2], width), b16),
+            dma((3, 160)), dma((3, 2, n)), dma((2, n)), dma((2, m - 1, nz, m)), dma((2, m - 1, nz)), dma((2, nz - 1)),
+            dma((4,)), dma((4,)), dma((4, max(nz, m))), dma((4, max(nz, m, 2))), dma((3, n)), dma((3,)), dma((3,)),
         ],
         compiler_params=pltpu.CompilerParams(collective_id=2, has_side_effects=True, vmem_limit_bytes=62 * 2**20),
-    )(x, x1, cot, sums, q, k, v, o, prob, wq, wk, wv, wo, gain1, gain2, cosine, sine, cnt, length, logits, routes, scores, sg, su, sd)
+    )(x, x1, cot, sums, q, k, v, o, prob, wq, wk, wv, wo, gain1, gain2, cosine, sine, cnt, length, logits, routes, scores, pay)
 
 
 def blocked(count, n):
@@ -953,33 +972,38 @@
     n = lax.axis_size("exp")
     hidden = s_gate.shape[1]
     cosine, sine = (jnp.asarray(table) for table in rotary_rows(rows))
-    length = jnp.broadcast_to(lengths[:, None], (1, 128))
     gain1, gain2 = norm_one[None], norm_two[None]
+    logits, routes = logits.T, routes.T
+    attn_w = (w_query, w_key, w_value, w_out)
+    routed_w = (r_gate[0].T, r_up[0].T, r_down[0])
+    shared_w = (s_gate.T, s_up.T, s_down)
     (
         all_dy, all_h, fq, fk, fv, fo, fg, fu, fd, mixed, queries, keys_all, values_all, attended, prob, gates, counts,
     ) = front(
-        n, tokens, cotangent, gain1, gain2, cosine, sine, length, logits, routes,
-        (w_query, w_key, w_value, w_out), (r_gate[0], r_up[0], r_down[0]), (s_gate, s_up, s_down),
+        n, tokens, cotangent, gain1, gain2, cosine, sine, lengths, logits, routes,
+        attn_w, routed_w, shared_w,
     )
-    scores, sums, tg, tu, td, bg, bu, bd = experts(all_h, all_dy, gates, fg, fu, fd)[:8]
+    scores, sums, tg, tu, td, payload = experts(
+        all_h, all_dy, gates, routed_w, shared_w, (fg, fu, fd)
+    )[:6]
     full = (width, width)
-    output, grad_tokens, grad_logits, small_sums, sum0, sum1, sum_g, sum_u, sum_d = tail(
+    output, grad_tokens, grad_logits, small_sums, sum0, sum1, sum_s = tail(
         n, tokens, mixed, cotangent, sums, queries, keys_all, values_all, attended, prob,
         fq.reshape(full), fk.reshape(full), fv.reshape(full), fo.reshape(full),
-        gain1, gain2, cosine, sine, counts, length, logits, routes, scores,
-        bg.reshape(n, -1, hidden), bu.reshape(n, -1, hidden), bd.reshape(n, -1, width),
+        gain1, gain2, cosine, sine, counts, lengths, logits, routes, scores,
+        payload.reshape(3, n, -1, width),
     )
     half = width // 2
     wout_value = from_blocks(sum0, width)
     key_query = from_blocks(sum1, width)
     holds_shared = lax.axis_index("exp") == n - 1
-    routed_grads = tuple(jnp.where(holds_shared, 0.0, grad)[None] for grad in (tg, tu, td))
+    tg, tu, td = (jnp.where(holds_shared, 0.0, grad) for grad in (tg, tu, td))
+    sg, su, sd = (from_blocks(sum_s[:, i], hidden) for i in range(3))
     return (
         output, grad_tokens, small_sums[0],
         key_query[half:], key_query[:half], wout_value[half:], wout_value[:half],
-        small_sums[1], routed_grads[0], routed_grads[1], routed_grads[2],
-        from_blocks(sum_g, width), from_blocks(sum_u, width), from_blocks(sum_d, hidden),
-        grad_logits, small_sums[2, :n].astype(jnp.int32),
+        small_sums[1], tg.T[None], tu.T[None], td[None], sg.T, su.T, sd,
+        grad_logits.T, small_sums[2, :n].astype(jnp.int32),
     )
 
 

time: 691 us -> 635 us (0.919); the launches traced: 682 us -> 633 us
  Pallas kernels: 633 us -> 606 us
  local copies, waits for them, and re-layouts: 34.5 us -> 14.4 us
    unnamed x31 -> x17, local copies, waits for them, and re-layouts: 22.6 us -> 2.9 us
    pallas_call x1, Pallas kernels: 223 us -> 210 us  [tail(): pl.pallas_call(functools.partial(tail_kernel, n), out_shape=(out((rows, w...]
    pallas_call x1, Pallas kernels: 224 us -> 214 us  [experts(): pl.pallas_call(functools.partial(experts_kernel, n, slots), out_shape=(ou...]
where the time goes in v4:
time: 635 us; the launch traced here: 633 us
  Pallas kernels  606 us (95%)
  local copies, waits for them, and re-layouts  14.4 us (2%)
  other arithmetic  11.2 us (2%)
    pallas_call x1, Pallas kernels, experts(): pl.pallas_call(functools.partial(experts_kernel, n, slots), out_shape=(ou...  214 us
    pallas_call x1, Pallas kernels, tail(): pl.pallas_call(functools.partial(tail_kernel, n), out_shape=(out((rows, w...  210 us
    pallas_call x1, Pallas kernels, front(): pl.pallas_call(functools.partial(front_kernel, n), out_shape=(out((n, row...  182 us

profile of v4, /device:TPU:0, one launch (start us, length us, event | category | flops | bytes accessed | tf_op | source)
XLA Modules:
  0.0 633.2 jit_solution(9907960506303638979)
XLA Ops:
  0.6 1.3 broadcast_in_dim.21.gain1
  1.9 1.3 broadcast_in_dim.22.gain2
  3.9 181.8 %shard_map.306 = (bf16[16,256,1280]{2,1,0:T(8,128)(2,1)}, bf16[16,256,1280]{2,1,0:T(8,128)(2,1)}, bf16[2,640,1280]{2,1,0:T(8,128)(2,1)}, bf16[2,640,1280]{2,1,0:...) custom-call(bf16[256,1280]{1,0:T(8,128)(2,1)} %x_ref.3, ...), custom_call_target="tpu_custom_call" | custom-call | tf_op jit(solution)/shard_map/pallas_call | solution.py:323
  185.7 214.0 %shard_map.307 = (f32[16,1,256]{2,1,0:T(1,128)}, f32[2,256,1280]{2,1,0:T(8,128)}, f32[448,1280]{1,0:T(8,128)}, f32[448,1280]{1,0:T(8,128)}, f32[448,1280]{1,0:T(...) custom-call(bf16[16,256,1280]{2,1,0:T(8,128)(2,1)} %get-tuple-elemen, ...), custom_call_target="tpu_custom_call" | custom-call | tf_op jit(solution)/shard_map/pallas_call | solution.py:571
  399.7 210.0 %shard_map.308 = (bf16[256,1280]{1,0:T(8,128)(2,1)}, bf16[256,1280]{1,0:T(8,128)(2,1)}, f32[7,256]{1,0:T(8,128)}, f32[8,1280]{1,0:T(8,128)}, bf16[16,80,1280]{2,...) custom-call(bf16[256,1280]{1,0:T(8,128)(2,1)} %x_ref.3, ...), custom_call_target="tpu_custom_call" | custom-call | tf_op jit(solution)/shard_map/pallas_call | solution.py:927
  609.8 2.2 fusion
  612.0 0.0 copy-start.2
  612.0 2.6 convert_bitcast_fusion
  614.6 0.0 copy-done.2
  614.6 0.0 copy-start
  614.6 0.0 copy-start.1
  614.6 4.2 select_bitcast_fusion
  618.8 0.0 copy-done
  618.8 0.6 copy-done.1
  619.4 5.2 fusion.1
  624.7 0.0 copy-start.3
  624.7 1.6 bitcast_convert_fusion
  626.3 1.5 slice_reduce_fusion
  627.8 1.2 convert_bitcast_fusion.2
  629.0 0.0 copy-done.3
  629.0 0.0 copy-start.5
  629.0 0.0 copy-start.4
  629.0 1.5 select_bitcast_fusion.2
  630.5 0.0 copy-done.5
  630.5 0.0 copy-start.6
  630.5 0.8 copy.39
  631.4 0.0 copy-done.4
  631.4 0.8 copy.40
  632.2 0.0 copy-done.6
  632.2 0.6 copy.41
Async XLA Ops:
  612.0 2.6 copy-start.2
  614.6 4.2 copy-start
  614.6 4.8 copy-start.1
  624.7 4.3 copy-start.3
  629.0 1.5 copy-start.5
  629.0 2.4 copy-start.4
  630.5 1.7 copy-start.6
